TPU v7x, 32 devices: a whole 2x2x4 slice. The times are simulated.
32 devices in a mesh: dp: 8 (over y, x, core), tensor: 4 (over z).
Axes of the slice: x: 2, y: 2, z: 4, core: 2. Of those that a mesh axis runs over, the one named last changes fastest.
Arguments:
- queries: bfloat16 [384, 5, 8192], P('dp', None, 'tensor'), may hold values from -6 to 6
- new_keys: bfloat16 [384, 5, 1024], P('dp', None, 'tensor'), may hold values from -6 to 6
- new_values: bfloat16 [384, 5, 1024], P('dp', None, 'tensor'), may hold values from -6 to 6
- key_cache: bfloat16 [384, 256, 1024], P('dp', None, 'tensor'), may hold values from -6 to 6
- value_cache: bfloat16 [384, 256, 1024], P('dp', None, 'tensor'), may hold values from -6 to 6
- cache_lengths: int32 [384], P('dp'), may hold values from 2 to 256, as said below
- accepted: int32 [384], P('dp'), may hold values from 0 to 4
- head_weight: bfloat16 [8192, 32768], P('tensor', 'dp'), may hold values from -1.3203125 to 1.3203125
Outputs:
- drafter_logits: float32 [384, 32768], P('tensor', 'dp')
Inputs may be any that keep to these rules, and one draw needn't show every extreme that they name: `cache_lengths`: row 0 holds 256 valid slots.
All inputs are finite; a program needn't handle non-finite values.
Results may differ from a plain program's by a relative error of at most 0.015.
Values may be sent and summed in bfloat16 or wider, within the bound.
No kernel may reach another device: no remote copies, remote signals or barrier semaphores. Data moves between devices by JAX's collectives and lax.ppermute only.
A program may use at most 128 MiB of HBM per device.

v0:
```python
import jax
import jax.numpy as jnp
from jax import lax
from jax.sharding import PartitionSpec as P

HEAD_DIM = 128


def verify(queries, new_keys, new_values, key_cache, value_cache, cache_lengths):
    row_count, draft_len, query_cols = queries.shape
    cache_len = key_cache.shape[1]
    groups = key_cache.shape[2] // HEAD_DIM
    sharing = query_cols // (groups * HEAD_DIM)
    query_heads = queries.reshape(row_count, draft_len, groups, sharing, HEAD_DIM)
    past_keys = key_cache.reshape(row_count, cache_len, groups, HEAD_DIM)
    past_values = value_cache.reshape(row_count, cache_len, groups, HEAD_DIM)
    fresh_keys = new_keys.reshape(row_count, draft_len, groups, HEAD_DIM)
    fresh_values = new_values.reshape(row_count, draft_len, groups, HEAD_DIM)
    scaling = HEAD_DIM ** (-0.5)
    past_scores = (
        jnp.einsum("bpgjd,blgd->bpgjl", query_heads, past_keys, preferred_element_type=jnp.float32)
        * scaling
    )
    fresh_scores = (
        jnp.einsum("bpgjd,bqgd->bpgjq", query_heads, fresh_keys, preferred_element_type=jnp.float32)
        * scaling
    )
    past_mask = (jnp.arange(cache_len, dtype=jnp.int32)[None, :] < cache_lengths[:, None])[
        :, None, None, None, :
    ]
    fresh_mask = (jnp.arange(draft_len)[None, :] <= jnp.arange(draft_len)[:, None])[
        None, :, None, None, :
    ]
    lowest = -1e30
    past_masked = jnp.where(past_mask, past_scores, lowest)
    fresh_masked = jnp.where(fresh_mask, fresh_scores, lowest)
    peaks = jnp.maximum(
        jnp.max(past_masked, axis=-1, keepdims=True), jnp.max(fresh_masked, axis=-1, keepdims=True)
    )
    past_exp = jnp.exp(past_masked - peaks)
    fresh_exp = jnp.exp(fresh_masked - peaks)
    totals = jnp.sum(past_exp, axis=-1, keepdims=True) + jnp.sum(fresh_exp, axis=-1, keepdims=True)
    past_weights = (past_exp / totals).astype(jnp.bfloat16)
    fresh_weights = (fresh_exp / totals).astype(jnp.bfloat16)
    mixed = jnp.einsum(
        "bpgjl,blgd->bpgjd", past_weights, past_values, preferred_element_type=jnp.float32
    )
    mixed = mixed + jnp.einsum(
        "bpgjq,bqgd->bpgjd", fresh_weights, fresh_values, preferred_element_type=jnp.float32
    )
    return mixed.astype(jnp.bfloat16).reshape(row_count, draft_len, query_cols)


def shards(
    queries, new_keys, new_values, key_cache, value_cache, cache_lengths, accepted, head_weight
):
    attended = verify(queries, new_keys, new_values, key_cache, value_cache, cache_lengths)
    everything = lax.all_gather(attended, "dp", axis=0, tiled=True)
    all_counts = lax.all_gather(accepted, "dp", axis=0, tiled=True)
    gathered = jnp.take_along_axis(everything, all_counts[:, None, None], axis=1)[:, 0, :]
    return lax.psum_scatter(
        jnp.dot(gathered, head_weight, preferred_element_type=jnp.float32).astype(jnp.bfloat16),
        "tensor",
        scatter_dimension=0,
        tiled=True,
    ).astype(jnp.float32)


def solution(mesh):
    in_specs = (
        P("dp", None, "tensor"),
        P("dp", None, "tensor"),
        P("dp", None, "tensor"),
        P("dp", None, "tensor"),
        P("dp", None, "tensor"),
        P("dp"),
        P("dp"),
        P("tensor", "dp"),
    )
    out_specs = P("tensor", "dp")
    return jax.shard_map(shards, mesh=mesh, in_specs=in_specs, out_specs=out_specs, check_vma=False)
```

profile of v0, /device:TPU:0, one launch (start us, length us, event | category | flops | bytes accessed | tf_op | source)
XLA Modules:
  0.0 200.6 jit_solution(10398015629314192565)
XLA Ops:
  6.5 0.0 all-gather.2.cloned.1.call-start
  6.5 0.0 copy-start.1
  6.5 1.4 copy.71
  8.0 0.9 reshape.80
  8.9 3.7 %fusion.14 = f32[48,2,5,5,8]{4,2,3,1,0:T(8,128)S(1)} fusion(bf16[48,5,2,8,128]{4,3,2,0,1:T(8,128)(2,1)S(1)} %bitcast.45, bf16[48,5,2,128,1]{3,2,0,1,4:T(2,128)(2,1)S(1)} %bitcast.49), kind=kOutput, calls=%fused_computation.21 | convolution fusion | flops 4915200 | bytes 1182720 | tf_op jit(solution)/shard_map/bpgjd,bqgd->bpgjq/dot_general | solution.py:25
  12.6 0.5 copy.50
  13.1 0.1 fusion.21
  13.2 0.2 copy.51
  13.4 0.0 copy-done.1
  13.4 0.1 iota_compare_fusion
  13.5 9.7 %reshape.78 = bf16[48,256,2,128]{3,2,1,0:T(2,128)(2,1)} reshape(bf16[48,256,256]{2,1,0:T(8,128)(2,1)} %param.11) | data formatting | bytes 12582912 | tf_op jit(solution)/shard_map/reshape | solution.py:15
  23.2 6.9 %bitcast_reduce_fusion = (f32[48,5,2,8]{3,1,2,0:T(8,128)S(1)}, f32[48,2,256,5,8]{2,4,3,1,0:T(8,128)}) fusion(pred[48,256]{1,0:T(8,128)(4,1)S(1)} %iota_compare_fusion, bf16[48,5,2,8,128]{4,3,2,0,1:T(8,128)(2,1)S(1)} %bitcast.46, bf16[48,256,2,128,1]{3,2,1,0,4:T(2,128)(2,1)} %bitcast.44), kind=kOutput, calls=%fused_computation.7 | convolution fusion | flops 254603520 | bytes 11234304 | tf_op jit(solution)/shard_map/bpgjd,blgd->bpgjl/dot_general | solution.py:21
  30.2 0.1 max.8
  30.2 0.2 copy.52
  30.4 3.0 %fusion.5 = f32[48,5,2,8]{3,1,2,0:T(8,128)S(1)} fusion(f32[48,2,256,5,8]{2,4,3,1,0:T(8,128)} %get-tuple-element.6, f32[48,5,2,8]{3,1,2,0:T(8,128)S(1)} %max.8, pred[48,256]{1,0:T(8,128)(4,1)S(1)} %iota_compare_fusion), kind=kLoop, calls=%fused_computation.11 | loop fusion | flops 3928320 | bytes 3975168 | tf_op jit(solution)/shard_map/reduce_sum | solution.py:42
  33.4 0.1 fusion.20
  33.5 0.2 copy.53
  33.8 9.7 %reshape.81 = bf16[48,256,2,128]{3,2,1,0:T(2,128)(2,1)} reshape(bf16[48,256,256]{2,1,0:T(8,128)(2,1)} %param.12) | data formatting | bytes 12582912 | tf_op jit(solution)/shard_map/reshape | solution.py:16
  43.5 0.1 add.25
  43.6 0.2 copy.55
  43.7 0.0 copy-start
  43.7 5.2 %fusion = f32[48,2,5,8,128]{4,3,2,1,0:T(8,128)S(1)} fusion(bf16[48,256,2,128,1]{3,2,1,0,4:T(2,128)(2,1)} %bitcast.43, f32[48,2,256,5,8]{2,4,3,1,0:T(8,128)} %get-tuple-element.6, f32[48,5,2,8]{3,1,2,0:T(8,128)S(1)} %add.25, f32[48,5,2,8]{3,1,2,0:T(8,128)S(1)} %max.8, pred[48,256]{1,0:T(8,128)(4,1)S(1)} %iota_compare_fusion), kind=kOutput, calls=%fused_computation.1 | convolution fusion | flops 256573440 | bytes 12232704 | tf_op jit(solution)/shard_map/bpgjl,blgd->bpgjd/dot_general | solution.py:45
  48.9 0.1 divide_convert_fusion.2
  49.0 0.9 copy.56
  49.9 0.0 copy-done
  49.9 0.0 copy-start.3
  49.9 0.0 copy-start.2
  50.0 0.6 fusion.13
  50.6 0.2 copy.58
  50.8 1.4 reshape.83
  52.1 0.0 all-gather.2.cloned.1.call-update
  52.2 0.0 reduce-scatter.2.cloned.1.call-start
  52.2 0.0 copy-done.3
  52.2 0.6 dynamic-slice
  53.5 0.0 copy-done.2
  53.5 0.2 dynamic-update-slice
  53.8 9.5 %all-reduce = s32[384]{0:T(512)S(1)} all-reduce(s32[384]{0:T(512)S(1)} %dynamic-update-slice), channel_id=1, replica_groups=mesh['dp'=8,'tensor'=4] {'dp'}, use_global_device_ids=true, to_apply=%add | all-reduce | flops 384 | bytes 3072
  63.3 43.9 %all-gather.2.cloned.1.call-done = bf16[384,5,2048]{2,0,1:T(8,128)(2,1)} async-done(((bf16[48,5,2048]{2,0,1:T(8,128)(2,1)}), bf16[384,5,2048]{2,0,1:T(8,128)(2,1)}) %all-gather.2.cloned.1.call-update) | async-done | bytes 7864336 | tf_op jit(solution)/shard_map/all_gather | solution.py:58
  107.2 12.0 %gather_fusion = bf16[384,2048]{1,0:T(8,128)(2,1)S(1)} fusion(bf16[384,5,2048]{2,0,1:T(8,128)(2,1)} %all-gather.2.cloned.1.call-done, s32[384]{0:T(512)S(1)} %fusion.25), kind=kCustom, calls=%fused_computation | custom fusion | bytes 3148800 | tf_op jit(solution)/shard_map/jit(take_along_axis)/gather | solution.py:60
  119.3 11.6 %convolution_convert_fusion = bf16[384,4096]{1,0:T(8,128)(2,1)} fusion(bf16[2048,4096]{1,0:T(8,128)(2,1)} %param.15, bf16[384,2048]{1,0:T(8,128)(2,1)S(1)} %gather_fusion, pred[384]{0:T(512)(128)(4,1)S(1)} %compare_and_fusion), kind=kOutput, calls=%fused_computation.5 | convolution fusion | flops 6444810240 | bytes 21496192 | tf_op jit(solution)/shard_map/dot_general | solution.py:62
  130.9 0.0 reduce-scatter.2.cloned.1.call-update
  130.9 60.4 %reduce-scatter.2.cloned.1.call-done = bf16[96,4096]{1,0:T(8,128)(2,1)} async-done(((bf16[384,4096]{1,0:T(8,128)(2,1)}), bf16[96,4096]{1,0:T(8,128)(2,1)}) %reduce-scatter.2.cloned.1.call-update) | async-done | bytes 786448 | tf_op jit(solution)/shard_map/reduce_scatter | solution.py:61
  191.3 2.4 %convert_element_type.23 = f32[96,4096]{1,0:T(8,128)} convert(bf16[96,4096]{1,0:T(8,128)(2,1)} %reduce-scatter.2.cloned.1.call-done) | non-fusion elementwise | flops 393216 | bytes 2359296 | tf_op jit(solution)/shard_map/convert_element_type | solution.py:66
  (9 shorter events, 0.1 us)
Async XLA Ops:
  6.5 100.7 %all-gather.2.cloned.1.call-start = ((), (), s32[]{:S(2)}) async-start(), calls=%async_computation.1 | async-start | bytes 8847360 | tf_op jit(solution)/shard_map/all_gather | solution.py:58
  6.5 6.9 %copy-start.1 = (s32[48]{0:T(128)S(1)}, s32[48]{0:T(128)}, u32[]{:S(2)}) copy-start(s32[48]{0:T(128)} %param.13) | copy-start | bytes 580
  43.7 6.2 %copy-start = (bf16[48,5,256]{2,0,1:T(8,128)(2,1)S(1)}, bf16[48,5,256]{2,0,1:T(8,128)(2,1)}, u32[]{:S(2)}) copy-start(bf16[48,5,256]{2,0,1:T(8,128)(2,1)} %param.10) | copy-start | bytes 368644
  49.9 2.3 %copy-start.3 = (u32[32]{0:T(128)S(1)}, u32[32]{0:T(128)}, u32[]{:S(2)}) copy-start(u32[32]{0:T(128)} %constant.38) | copy-start | bytes 388
  49.9 3.6 %copy-start.2 = (s32[48]{0:T(128)S(1)}, s32[48]{0:T(128)}, u32[]{:S(2)}) copy-start(s32[48]{0:T(128)} %param.14) | copy-start | bytes 580
  52.2 139.1 %reduce-scatter.2.cloned.1.call-start = ((), (), s32[]{:S(2)}) async-start(), calls=%async_computation.2 | async-start | bytes 3932160 | tf_op jit(solution)/shard_map/reduce_scatter | solution.py:61
Sparse Core Ops, SparseCore 0:
  52.3 54.8 all-gather.1
  131.0 60.2 reduce-scatter.1
where the time goes:
time: 201 us
  waiting for transfers between devices  104 us (52%)
  local copies, waits for them, and re-layouts  38.5 us (19%)
  matrix products  28 us (14%)
  between operations  14.2 us (7%)
  blocking collectives  9.46 us (5%)
  other arithmetic  6 us (3%)
    reduce_scatter x1, waiting for transfers between devices, shards(): lax.psum_scatter(jnp.dot(gathered, head_weight, preferred_element_type=jn...  60.4 us
    all_gather x1, waiting for transfers between devices, shards(): everything = lax.all_gather(attended, 'dp', axis=0, tiled=True)  43.9 us
    gather x1, local copies, waits for them, and re-layouts, shards(): jnp.take_along_axis(everything, all_counts[:, None, None], axis=1)[:, 0, :]  12 us
    dot_general x1, matrix products, shards(): jnp.dot(gathered, head_weight, preferred_element_type=jnp.float32)  11.6 us
    reshape x1, local copies, waits for them, and re-layouts, verify(): past_values = value_cache.reshape(row_count, cache_len, groups, HEAD_DIM)  9.73 us
    reshape x1, local copies, waits for them, and re-layouts, verify(): past_keys = key_cache.reshape(row_count, cache_len, groups, HEAD_DIM)  9.73 us
    unnamed x1, blocking collectives  9.46 us
    dot_general x1, matrix products, verify(): jnp.einsum('bpgjd,blgd->bpgjl', query_heads, past_keys, preferred_element...  6.94 us
  transfers between devices with their start and end apart: 2, of which 2 were waited for; matrix products, arithmetic and copies ran while one was open for 0% of the time, Pallas kernels for 0%

commit v1 on v0

v1 whole, which is shorter than its diff:
```python
import functools

import jax
import jax.numpy as jnp
from jax import lax
from jax.experimental import pallas as pl
from jax.experimental.pallas import tpu as pltpu
from jax.sharding import PartitionSpec as P

HEAD_DIM = 128
BLOCK = 16
CHUNK = 4
LOWEST = -1e30


def attend_kernel(
    first, rows, lengths, accepted, queries, new_keys, new_values, key_cache, value_cache,
    picked, q_buf, nk_buf, nv_buf, k_buf, v_buf, spread, mixed, small_sems, k_sems, v_sems,
):
    draft, _, query_cols = q_buf.shape
    cache_len, key_cols = k_buf.shape[1:]
    groups, heads = key_cols // HEAD_DIM, query_cols // HEAD_DIM
    sharing = heads // groups
    scaling = HEAD_DIM ** (-0.5)
    own = pl.ds(first, rows)
    small = [
        pltpu.make_async_copy(src.at[:, own], dst, small_sems.at[n])
        for n, (src, dst) in enumerate(((queries, q_buf), (new_keys, nk_buf), (new_values, nv_buf)))
    ]
    keys, values = [
        [
            pltpu.make_async_copy(src.at[pl.ds(first + at, CHUNK)], dst.at[pl.ds(at, CHUNK)], sems.at[at // CHUNK])
            for at in range(0, rows, CHUNK)
        ]
        for src, dst, sems in ((key_cache, k_buf, k_sems), (value_cache, v_buf, v_sems))
    ]
    for copy in small:
        copy.start()
    for start in range(0, rows // CHUNK, BLOCK // CHUNK):
        for copy in keys[start : start + BLOCK // CHUNK] + values[start : start + BLOCK // CHUNK]:
            copy.start()
    for copy in small:
        copy.wait()
    nt = (((1,), (1,)), ((), ()))
    for block in range(0, rows, BLOCK):
        here = pl.ds(block, BLOCK)
        row = lax.broadcasted_iota(jnp.int32, (BLOCK, HEAD_DIM), 0)
        chosen = jnp.zeros((BLOCK, HEAD_DIM), jnp.int32)
        for r in range(BLOCK):
            chosen = jnp.where(row == r, accepted[first + block + r], chosen)
        for h in range(heads):
            cols = pl.ds(h * HEAD_DIM, HEAD_DIM)
            query = q_buf[0, here, cols].astype(jnp.float32)
            for p in range(1, draft):
                query = jnp.where(chosen == p, q_buf[p, here, cols].astype(jnp.float32), query)
            spread[:, h, :] = query
        query = spread[...].reshape(BLOCK * heads, HEAD_DIM)
        group = lax.rem(lax.broadcasted_iota(jnp.int32, query.shape, 0), heads) // sharing
        query = jnp.concatenate([jnp.where(group == g, query, 0.0) for g in range(groups)], axis=1)
        query = query.astype(jnp.bfloat16)
        fresh_keys = nk_buf[:, here, :].reshape(draft * BLOCK, key_cols)
        fresh_values = nv_buf[:, here, :].reshape(draft * BLOCK, key_cols)
        fresh = lax.dot_general(query, fresh_keys, nt, preferred_element_type=jnp.float32) * scaling
        slot = lax.broadcasted_iota(jnp.int32, (heads, draft * BLOCK), 1)
        lane = lax.broadcasted_iota(jnp.int32, (heads, cache_len), 1)
        weights, fresh_weights = [], []
        for r in range(BLOCK):
            if r % CHUNK == 0:
                keys[(block + r) // CHUNK].wait()
            mine = slice(r * heads, (r + 1) * heads)
            past = lax.dot_general(query[mine], k_buf[block + r], nt, preferred_element_type=jnp.float32) * scaling
            past = jnp.where(lane < lengths[first + block + r], past, LOWEST)
            open_slot = (lax.rem(slot, BLOCK) == r) & (slot // BLOCK <= accepted[first + block + r])
            fresh_r = jnp.where(open_slot, fresh[mine], LOWEST)
            peak = jnp.maximum(jnp.max(past, axis=1, keepdims=True), jnp.max(fresh_r, axis=1, keepdims=True))
            past, fresh_r = jnp.exp(past - peak), jnp.exp(fresh_r - peak)
            total = jnp.sum(past, axis=1, keepdims=True) + jnp.sum(fresh_r, axis=1, keepdims=True)
            weights.append((past / total).astype(jnp.bfloat16))
            fresh_weights.append((fresh_r / total).astype(jnp.bfloat16))
        fresh = jnp.dot(jnp.concatenate(fresh_weights, axis=0), fresh_values, preferred_element_type=jnp.float32)
        own_group = lax.broadcasted_iota(jnp.int32, (heads, HEAD_DIM), 0) // sharing
        for r in range(BLOCK):
            if r % CHUNK == 0:
                values[(block + r) // CHUNK].wait()
            result = jnp.dot(weights[r], v_buf[block + r], preferred_element_type=jnp.float32)
            result = result + fresh[r * heads : (r + 1) * heads]
            kept = result[:, :HEAD_DIM]
            for g in range(1, groups):
                kept = jnp.where(own_group == g, result[:, g * HEAD_DIM : (g + 1) * HEAD_DIM], kept)
            mixed[r] = kept
        for h in range(heads):
            picked[here, pl.ds(h * HEAD_DIM, HEAD_DIM)] = mixed[:, h, :].astype(jnp.bfloat16)


def attend(first, rows, lengths, accepted, queries, new_keys, new_values, key_cache, value_cache):
    draft, _, query_cols = queries.shape
    _, cache_len, key_cols = key_cache.shape
    heads = query_cols // HEAD_DIM
    smem, anywhere = pl.BlockSpec(memory_space=pltpu.SMEM), pl.BlockSpec(memory_space=pl.ANY)
    cached = 2 * rows * cache_len * key_cols
    return pl.pallas_call(
        functools.partial(attend_kernel, first, rows),
        out_shape=jax.ShapeDtypeStruct((rows, query_cols), jnp.bfloat16),
        in_specs=[smem, smem] + [anywhere] * 5,
        out_specs=pl.BlockSpec(memory_space=pltpu.VMEM),
        scratch_shapes=[
            pltpu.VMEM((draft, rows, query_cols), jnp.bfloat16),
            pltpu.VMEM((draft, rows, key_cols), jnp.bfloat16),
            pltpu.VMEM((draft, rows, key_cols), jnp.bfloat16),
            pltpu.VMEM((rows, cache_len, key_cols), jnp.bfloat16),
            pltpu.VMEM((rows, cache_len, key_cols), jnp.bfloat16),
            pltpu.VMEM((BLOCK, heads, HEAD_DIM), jnp.float32),
            pltpu.VMEM((BLOCK, heads, HEAD_DIM), jnp.float32),
            pltpu.SemaphoreType.DMA((3,)),
            pltpu.SemaphoreType.DMA((rows // CHUNK,)),
            pltpu.SemaphoreType.DMA((rows // CHUNK,)),
        ],
        compiler_params=pltpu.CompilerParams(vmem_limit_bytes=40 << 20),
        cost_estimate=pl.CostEstimate(flops=2 * heads * cached, bytes_accessed=2 * cached, transcendentals=rows * heads * cache_len),
    )(lengths, accepted, queries, new_keys, new_values, key_cache, value_cache)


def head_kernel(count, *refs):
    pieces, weight, part, features = refs[:count], refs[count], refs[count + 1], refs[count + 2]

    @pl.when(pl.program_id(0) == 0)
    def _():
        at = 0
        for piece in pieces:
            features[pl.ds(at, piece.shape[0]), :] = piece[...]
            at += piece.shape[0]

    part[...] = jnp.dot(features[...], weight[...], preferred_element_type=jnp.float32).astype(jnp.bfloat16)


def head(pieces, weight, tile=512):
    depth, cols = weight.shape
    rows = sum(piece.shape[0] for piece in pieces)
    return pl.pallas_call(
        functools.partial(head_kernel, len(pieces)),
        grid=(cols // tile,),
        out_shape=jax.ShapeDtypeStruct((rows, cols), jnp.bfloat16),
        in_specs=[pl.BlockSpec(piece.shape, lambda n: (0, 0)) for piece in pieces]
        + [pl.BlockSpec((depth, tile), lambda n: (0, n))],
        out_specs=pl.BlockSpec((rows, tile), lambda n: (0, n)),
        scratch_shapes=[pltpu.VMEM((rows, depth), jnp.bfloat16)],
        compiler_params=pltpu.CompilerParams(vmem_limit_bytes=40 << 20),
        cost_estimate=pl.CostEstimate(
            flops=2 * rows * depth * cols, bytes_accessed=2 * (depth * cols + rows * depth + rows * cols), transcendentals=0
        ),
    )(*pieces, weight)


def gather(block, dp):
    if dp != 8:
        return [lax.all_gather(block, "dp", axis=0, tiled=True)]

    def swap(array, bits):
        return lax.ppermute(array, "dp", [(i, i ^ bits) for i in range(dp)])

    beside, below, across = swap(block, 2), swap(block, 4), swap(block, 6)
    return [block, swap(block, 1), beside, swap(beside, 1), below, swap(below, 1), across, swap(across, 1)]


def shards(
    tensor, dp, queries, new_keys, new_values, key_cache, value_cache, cache_lengths, accepted, head_weight
):
    rows_dev = queries.shape[0]
    queries, new_keys, new_values = [jnp.transpose(a, (1, 0, 2)) for a in (queries, new_keys, new_values)]
    me, place = lax.axis_index("tensor"), lax.axis_index("dp")
    sources = dp // tensor
    paired = dp == 8 and tensor == 4

    bounds = [(0, BLOCK), (BLOCK, rows_dev - BLOCK)]
    parts = []
    for first, rows in bounds:
        picked = attend(first, rows, cache_lengths, accepted, queries, new_keys, new_values, key_cache, value_cache)
        pieces = gather(picked, dp)
        parts.append(head(pieces, head_weight))

    def term(part, shard):
        size = part.shape[0] // tensor
        if paired:
            shard = shard ^ (place // sources)
        return lax.dynamic_slice_in_dim(part, shard * size, size, axis=0)

    def add(part, shard, arrived):
        mine = term(part, jnp.clip(shard, 0, tensor - 1))
        if arrived is None:
            return mine
        return (mine.astype(jnp.float32) + arrived.astype(jnp.float32)).astype(jnp.bfloat16)

    ups, downs = [None] * len(parts), [None] * len(parts)
    for step in range(1, tensor):
        up = [(z, z + 1) for z in range(step)]
        down = [(tensor - 1 - z, tensor - 2 - z) for z in range(step)]
        for n, part in enumerate(parts):
            ups[n] = lax.ppermute(add(part, tensor - step + me, ups[n]), "tensor", up)
            downs[n] = lax.ppermute(add(part, step - tensor + me, downs[n]), "tensor", down)

    results = []
    for part, up, down in zip(parts, ups, downs):
        total = term(part, me).astype(jnp.float32) + up.astype(jnp.float32) + down.astype(jnp.float32)
        total = total.reshape(sources, -1, total.shape[-1])
        if paired:
            total = jnp.where(place % 2 == 1, total[::-1], total)
        results.append(total)
    total = jnp.concatenate(results, axis=1)
    return total.reshape(-1, total.shape[-1])


def solution(mesh):
    in_specs = (
        P("dp", None, "tensor"),
        P("dp", None, "tensor"),
        P("dp", None, "tensor"),
        P("dp", None, "tensor"),
        P("dp", None, "tensor"),
        P("dp"),
        P("dp"),
        P("tensor", "dp"),
    )
    out_specs = P("tensor", "dp")
    body = functools.partial(shards, mesh.shape["tensor"], mesh.shape["dp"])
    return jax.shard_map(body, mesh=mesh, in_specs=in_specs, out_specs=out_specs, check_vma=False)
```

time: 201 us -> 131 us (0.65)
  waiting for transfers between devices: 104 us -> 47.5 us
  starting transfers between devices: 0.04 us -> 38 us
  Pallas kernels: 0 us -> 32 us
  local copies, waits for them, and re-layouts: 38.5 us -> 10 us
  matrix products: 28 us -> 0 us
  between operations: 14.2 us -> 0.31 us
  blocking collectives: 9.46 us -> 0 us
  other arithmetic: 6 us -> 2.42 us
    reduce_scatter x1 -> x0, waiting for transfers between devices: 60.4 us -> none  [shards(): lax.psum_scatter(jnp.dot(gathered, head_weight, preferred_element_type=jn...]
    ppermute x0 -> x26, waiting for transfers between devices: none -> 47.5 us  [the longest x6 27.3 us: shards(): ups[n] = lax.ppermute(add(part, tensor - step + me, ups[n]), 'tensor', up)]
    all_gather x1 -> x0, waiting for transfers between devices: 43.9 us -> none  [shards(): everything = lax.all_gather(attended, 'dp', axis=0, tiled=True)]
    ppermute x0 -> x26, starting transfers between devices: none -> 38 us  [the longest x6 22.9 us: shards(): ups[n] = lax.ppermute(add(part, tensor - step + me, ups[n]), 'tensor', up)]
    pallas_call x0 -> x4, Pallas kernels: none -> 32 us  [the longest x2 19.9 us: head(): pl.pallas_call(functools.partial(head_kernel, len(pieces)), grid=(cols //...]
    dot_general x5 -> x0, matrix products: 28 us -> none  [the longest x1 11.6 us: shards(): jnp.dot(gathered, head_weight, preferred_element_type=jnp.float32)]
    reshape x5 -> x0, local copies, waits for them, and re-layouts: 21.8 us -> none  [the longest x1 9.73 us: verify(): past_values = value_cache.reshape(row_count, cache_len, groups, HEAD_DIM)]
    gather x1 -> x0, local copies, waits for them, and re-layouts: 12 us -> none  [shards(): jnp.take_along_axis(everything, all_counts[:, None, None], axis=1)[:, 0, :]]
  transfers between devices with their start and end apart: 2 -> 26, of which waited for: 2 -> 7; matrix products, arithmetic and copies ran while one was open for 0% -> 1% of each run, Pallas kernels for 0% -> 21%
where the time goes in v1:
time: 131 us; the launch traced here: 130 us
  waiting for transfers between devices  47.5 us (36%)
  starting transfers between devices  38 us (29%)
  Pallas kernels  32 us (24%)
  local copies, waits for them, and re-layouts  10 us (8%)
  other arithmetic  2.42 us (2%)
    ppermute x6, waiting for transfers between devices, shards(): ups[n] = lax.ppermute(add(part, tensor - step + me, ups[n]), 'tensor', up)  27.3 us
    ppermute x6, starting transfers between devices, shards(): ups[n] = lax.ppermute(add(part, tensor - step + me, ups[n]), 'tensor', up)  22.9 us
    pallas_call x2, Pallas kernels, head(): pl.pallas_call(functools.partial(head_kernel, len(pieces)), grid=(cols //...  19.9 us
    ppermute x6, waiting for transfers between devices, shards(): lax.ppermute(add(part, step - tensor + me, downs[n]), 'tensor', down)  13.8 us
    pallas_call x2, Pallas kernels, attend(): pl.pallas_call(functools.partial(attend_kernel, first, rows), out_shape=j...  12.1 us
    unnamed x14, local copies, waits for them, and re-layouts  9.88 us
    ppermute x14, starting transfers between devices, swap(): return lax.ppermute(array, 'dp', [(i, i ^ bits) for i in range(dp)])  9.8 us
    ppermute x14, waiting for transfers between devices, swap(): return lax.ppermute(array, 'dp', [(i, i ^ bits) for i in range(dp)])  6.44 us
  transfers between devices with their start and end apart: 26, of which 7 were waited for; matrix products, arithmetic and copies ran while one was open for 1% of the time, Pallas kernels for 21%

profile of v1, /device:TPU:0, one launch (start us, length us, event | category | flops | bytes accessed | tf_op | source)
XLA Modules:
  0.0 130.2 jit_solution(16105482702666253997)
XLA Ops:
  0.0 2.8 %copy-done = bf16[48,256,256]{2,1,0:T(8,128)(2,1)S(1)} copy-done((bf16[48,256,256]{2,1,0:T(8,128)(2,1)S(1)}, bf16[48,256,256]{2,1,0:T(8,128)(2,1)}, u32[]{:S(2)}) %copy-start) | copy-done | bytes 6291480
  2.8 2.8 %copy-done.1 = bf16[48,256,256]{2,1,0:T(8,128)(2,1)S(1)} copy-done((bf16[48,256,256]{2,1,0:T(8,128)(2,1)S(1)}, bf16[48,256,256]{2,1,0:T(8,128)(2,1)}, u32[]{:S(2)}) %copy-start.1) | copy-done | bytes 6291480
  5.6 1.2 copy-done.2
  6.8 0.9 copy-done.3
  7.7 0.9 copy-done.4
  8.6 0.7 copy-done.5
  9.2 0.7 copy-done.6
  9.9 4.3 %shard_map.82.refs_0_ = bf16[16,2048]{1,0:T(8,128)(2,1)S(1)} custom-call(s32[48]{0:T(128)S(1)} %copy-done.5, s32[48]{0:T(128)S(1)} %copy-done.6, bf16[5,48,2048]{2,1,0:T(8,128)(2,1)S(1)} %bitcast.6, bf16[5,48,256]{2,1,0:T(8,128)(2,1)S(1)} %bitcast.8, bf16[5,48,256]{2,1,0:T(8,128)(2,1)S(1)} %bitcast.10, bf16[48,256,256]{2,1,0:T(8,128)(2,1)S(1)} %copy-done, ...), custom_call_target="tpu_custom_call" | custom-call | flops 67108864 | bytes 4194304 | tf_op jit(solution)/shard_map/pallas_call | solution.py:101
  14.2 0.5 collective-permute-start
  14.7 2.6 %collective-permute-start.1 = (bf16[16,2048]{1,0:T(8,128)(2,1)S(1)}, bf16[16,2048]{1,0:T(8,128)(2,1)S(1)}, u32[]{:S(2)}, u32[]{:S(2)}) collective-permute-start(bf16[16,2048]{1,0:T(8,128)(2,1)S(1)} %shard_map.82.refs_0_), channel_id=1, source_target_pairs={{0,8},{4,12},{8,0},{12,4},{16,24},{20,28},{24,16},{28,20},{1,9},{5... | collective-permute-start | bytes 196616 | tf_op jit(solution)/shard_map/ppermute | solution.py:159
  17.3 7.8 %shard_map.84.refs_0_ = bf16[32,2048]{1,0:T(8,128)(2,1)S(1)} custom-call(s32[48]{0:T(128)S(1)} %copy-done.5, s32[48]{0:T(128)S(1)} %copy-done.6, bf16[5,48,2048]{2,1,0:T(8,128)(2,1)S(1)} %bitcast.7, bf16[5,48,256]{2,1,0:T(8,128)(2,1)S(1)} %bitcast.9, bf16[5,48,256]{2,1,0:T(8,128)(2,1)S(1)} %bitcast.11, bf16[48,256,256]{2,1,0:T(8,128)(2,1)S(1)} %copy-done, ...), custom_call_target="tpu_custom_call" | custom-call | flops 134217728 | bytes 8388608 | tf_op jit(solution)/shard_map/pallas_call | solution.py:101
  25.1 0.1 collective-permute-start.14
  25.2 2.0 %collective-permute-start.16 = (bf16[32,2048]{1,0:T(8,128)(2,1)S(1)}, bf16[32,2048]{1,0:T(8,128)(2,1)S(1)}, u32[]{:S(2)}, u32[]{:S(2)}) collective-permute-start(bf16[32,2048]{1,0:T(8,128)(2,1)S(1)} %shard_map.84.refs_0_), channel_id=1, source_target_pairs={{0,16},{4,20},{8,24},{12,28},{16,0},{20,4},{24,8},{28,12},{1,17},{... | collective-permute-start | bytes 393224 | tf_op jit(solution)/shard_map/ppermute | solution.py:159
  27.2 1.4 %collective-permute-start.18 = (bf16[32,2048]{1,0:T(8,128)(2,1)S(1)}, bf16[32,2048]{1,0:T(8,128)(2,1)S(1)}, u32[]{:S(2)}, u32[]{:S(2)}) collective-permute-start(bf16[32,2048]{1,0:T(8,128)(2,1)S(1)} %shard_map.84.refs_0_), channel_id=1, source_target_pairs={{0,24},{4,28},{8,16},{12,20},{16,8},{20,12},{24,0},{28,4},{1,25},{... | collective-permute-start | bytes 393224 | tf_op jit(solution)/shard_map/ppermute | solution.py:159
  28.6 1.5 %collective-permute-start.3 = (bf16[16,2048]{1,0:T(8,128)(2,1)S(1)}, bf16[16,2048]{1,0:T(8,128)(2,1)S(1)}, u32[]{:S(2)}, u32[]{:S(2)}) collective-permute-start(bf16[16,2048]{1,0:T(8,128)(2,1)S(1)} %shard_map.82.refs_0_), channel_id=1, source_target_pairs={{0,16},{4,20},{8,24},{12,28},{16,0},{20,4},{24,8},{28,12},{1,17},{... | collective-permute-start | bytes 196616 | tf_op jit(solution)/shard_map/ppermute | solution.py:159
  30.2 0.0 collective-permute-start.5
  30.2 6.3 %collective-permute-done.3.refs_4_ = bf16[16,2048]{1,0:T(8,128)(2,1)S(1)} collective-permute-done((bf16[16,2048]{1,0:T(8,128)(2,1)S(1)}, bf16[16,2048]{1,0:T(8,128)(2,1)S(1)}, u32[]{:S(2)}, u32[]{:S(2)}) %collective-permute-start.3) | collective-permute-done | bytes 65568 | tf_op jit(solution)/shard_map/ppermute | solution.py:159
  36.5 0.0 collective-permute-done.5.refs_6_
  36.5 0.5 collective-permute-start.4
  37.0 0.0 collective-permute-done.14.refs_2_
  37.0 0.1 collective-permute-start.6
  37.1 0.4 collective-permute-start.13
  37.5 0.0 collective-permute-done.18.refs_6_
  37.5 0.1 collective-permute-start.15
  37.6 0.1 collective-permute-done.2.refs_3_
  37.7 0.3 collective-permute-start.17
  38.0 0.2 collective-permute-start.19
  38.2 0.0 collective-permute-done.6.refs_7_
  38.2 9.4 %shard_map.83 = bf16[128,4096]{1,0:T(8,128)(2,1)S(1)} custom-call(bf16[16,2048]{1,0:T(8,128)(2,1)S(1)} %shard_map.82.refs_0_, bf16[16,2048]{1,0:T(8,128)(2,1)S(1)} %collective-permute-done.refs_1_, bf16[16,2048]{1,0:T(8,128)(2,1)S(1)} %collective-permute-done.1.refs_2_, bf16[16,2048]{1,0:T(8,128)(2,1)S(1)} %collective-permute-done.2.refs_3_, ...), custom_call_target="tpu_custom_call" | custom-call | flops 2147483648 | bytes 18350080 | tf_op jit(solution)/shard_map/pallas_call | solution.py:139
  47.7 3.6 %collective-permute-start.7 = (bf16[32,4096]{1,0:T(8,128)(2,1)S(1)}, bf16[32,4096]{1,0:T(8,128)(2,1)S(1)}, u32[]{:S(2)}, u32[]{:S(2)}) collective-permute-start(bf16[32,4096]{1,0:T(8,128)(2,1)S(1)} %get-tuple-element.11), channel_id=1, source_target_pairs={{0,1},{4,5},{8,9},{12,13},{16,17},{20,21},{24,25},{28,29}} | collective-permute-start | bytes 786440 | tf_op jit(solution)/shard_map/ppermute | solution.py:198
  51.3 0.7 collective-permute-start.10
  52.0 0.0 collective-permute-done.15.refs_3_
  52.0 0.0 collective-permute-done.17.refs_5_
  52.0 10.5 %shard_map.85 = bf16[256,4096]{1,0:T(8,128)(2,1)S(1)} custom-call(bf16[32,2048]{1,0:T(8,128)(2,1)S(1)} %shard_map.84.refs_0_, bf16[32,2048]{1,0:T(8,128)(2,1)S(1)} %collective-permute-done.13.refs_1_, bf16[32,2048]{1,0:T(8,128)(2,1)S(1)} %collective-permute-done.14.refs_2_, bf16[32,2048]{1,0:T(8,128)(2,1)S(1)} %collective-permute-done.15.refs_3_, ...), custom_call_target="tpu_custom_call" | custom-call | flops 4294967296 | bytes 19922944 | tf_op jit(solution)/shard_map/pallas_call | solution.py:139
  62.6 0.0 collective-permute-done.7
  62.6 0.1 add_convert_fusion.7
  62.6 1.3 %collective-permute-start.8 = (bf16[32,4096]{1,0:T(8,128)(2,1)S(1)}, bf16[32,4096]{1,0:T(8,128)(2,1)S(1)}, u32[]{:S(2)}, u32[]{:S(2)}) collective-permute-start(bf16[32,4096]{1,0:T(8,128)(2,1)S(1)} %add_convert_fusion.7), channel_id=1, source_target_pairs={{0,1},{1,2},{4,5},{5,6},{8,9},{9,10},{12,13},{13,14},{16,17},{17,1... | collective-permute-start | bytes 786440 | tf_op jit(solution)/shard_map/ppermute | solution.py:198
  64.0 0.1 constant_dynamic-slice_fusion.1
  64.0 3.5 %collective-permute-start.20 = (bf16[64,4096]{1,0:T(8,128)(2,1)S(1)}, bf16[64,4096]{1,0:T(8,128)(2,1)S(1)}, u32[]{:S(2)}, u32[]{:S(2)}) collective-permute-start(bf16[64,4096]{1,0:T(8,128)(2,1)S(1)} %get-tuple-element.7), channel_id=1, source_target_pairs={{0,1},{4,5},{8,9},{12,13},{16,17},{20,21},{24,25},{28,29}} | collective-permute-start | bytes 1572872 | tf_op jit(solution)/shard_map/ppermute | solution.py:198
  67.5 0.7 collective-permute-start.23
  68.2 0.0 collective-permute-done.10
  68.3 2.3 %collective-permute-done.8 = bf16[32,4096]{1,0:T(8,128)(2,1)S(1)} collective-permute-done((bf16[32,4096]{1,0:T(8,128)(2,1)S(1)}, bf16[32,4096]{1,0:T(8,128)(2,1)S(1)}, u32[]{:S(2)}, u32[]{:S(2)}) %collective-permute-start.8) | collective-permute-done | bytes 262176 | tf_op jit(solution)/shard_map/ppermute | solution.py:198
  70.6 0.1 add_convert_fusion.6
  70.7 0.7 collective-permute-start.11
  71.4 5.0 %collective-permute-start.9 = (bf16[32,4096]{1,0:T(8,128)(2,1)S(1)}, bf16[32,4096]{1,0:T(8,128)(2,1)S(1)}, u32[]{:S(2)}, u32[]{:S(2)}) collective-permute-start(bf16[32,4096]{1,0:T(8,128)(2,1)S(1)} %get-tuple-element.9), channel_id=1, source_target_pairs={{0,1},{1,2},{2,3},{4,5},{5,6},{6,7},{8,9},{9,10},{10,11},{12,13},{... | collective-permute-start | bytes 786440 | tf_op jit(solution)/shard_map/ppermute | solution.py:198
  76.4 5.4 %collective-permute-done.20 = bf16[64,4096]{1,0:T(8,128)(2,1)S(1)} collective-permute-done((bf16[64,4096]{1,0:T(8,128)(2,1)S(1)}, bf16[64,4096]{1,0:T(8,128)(2,1)S(1)}, u32[]{:S(2)}, u32[]{:S(2)}) %collective-permute-start.20) | collective-permute-done | bytes 524320 | tf_op jit(solution)/shard_map/ppermute | solution.py:198
  81.8 0.1 add_convert_fusion.3
  81.9 4.4 %collective-permute-start.21 = (bf16[64,4096]{1,0:T(8,128)(2,1)S(1)}, bf16[64,4096]{1,0:T(8,128)(2,1)S(1)}, u32[]{:S(2)}, u32[]{:S(2)}) collective-permute-start(bf16[64,4096]{1,0:T(8,128)(2,1)S(1)} %add_convert_fusion.3), channel_id=1, source_target_pairs={{0,1},{1,2},{4,5},{5,6},{8,9},{9,10},{12,13},{13,14},{16,17},{17,1... | collective-permute-start | bytes 1572872 | tf_op jit(solution)/shard_map/ppermute | solution.py:198
  86.4 0.0 collective-permute-done.11
  86.4 0.1 add_convert_fusion.4
  86.4 1.3 collective-permute-start.12
  87.8 10.3 %collective-permute-done.21 = bf16[64,4096]{1,0:T(8,128)(2,1)S(1)} collective-permute-done((bf16[64,4096]{1,0:T(8,128)(2,1)S(1)}, bf16[64,4096]{1,0:T(8,128)(2,1)S(1)}, u32[]{:S(2)}, u32[]{:S(2)}) %collective-permute-start.21) | collective-permute-done | bytes 524320 | tf_op jit(solution)/shard_map/ppermute | solution.py:198
  98.0 0.3 add_convert_fusion.2
  98.3 0.7 collective-permute-start.24
  99.0 0.0 collective-permute-done.9
  99.0 0.1 convert_add_fusion.1
  99.1 5.0 %collective-permute-start.22 = (bf16[64,4096]{1,0:T(8,128)(2,1)S(1)}, bf16[64,4096]{1,0:T(8,128)(2,1)S(1)}, u32[]{:S(2)}, u32[]{:S(2)}) collective-permute-start(bf16[64,4096]{1,0:T(8,128)(2,1)S(1)} %get-tuple-element.5), channel_id=1, source_target_pairs={{0,1},{1,2},{2,3},{4,5},{5,6},{6,7},{8,9},{9,10},{10,11},{12,13},{... | collective-permute-start | bytes 1572872 | tf_op jit(solution)/shard_map/ppermute | solution.py:198
  104.2 0.1 add_convert_fusion
  104.3 1.3 collective-permute-start.25
  105.7 9.3 %collective-permute-done.22 = bf16[64,4096]{1,0:T(8,128)(2,1)S(1)} collective-permute-done((bf16[64,4096]{1,0:T(8,128)(2,1)S(1)}, bf16[64,4096]{1,0:T(8,128)(2,1)S(1)}, u32[]{:S(2)}, u32[]{:S(2)}) %collective-permute-start.22) | collective-permute-done | bytes 524320 | tf_op jit(solution)/shard_map/ppermute | solution.py:198
  115.0 13.7 %collective-permute-done.25 = bf16[64,4096]{1,0:T(8,128)(2,1)S(1)} collective-permute-done((bf16[64,4096]{1,0:T(8,128)(2,1)S(1)}, bf16[64,4096]{1,0:T(8,128)(2,1)S(1)}, u32[]{:S(2)}, u32[]{:S(2)}) %collective-permute-start.25) | collective-permute-done | bytes 524320 | tf_op jit(solution)/shard_map/ppermute | solution.py:199
  128.7 0.2 convert_add_fusion
  128.9 0.1 reverse_select_fusion
  129.0 1.3 pad_maximum_fusion
  (19 shorter events, 0.1 us)
Async XLA Ops:
  0.0 2.8 %copy-start = (bf16[48,256,256]{2,1,0:T(8,128)(2,1)S(1)}, bf16[48,256,256]{2,1,0:T(8,128)(2,1)}, u32[]{:S(2)}) copy-start(bf16[48,256,256]{2,1,0:T(8,128)(2,1)} %key_cache.3) | copy-start | bytes 18874372
  2.8 2.8 %copy-start.1 = (bf16[48,256,256]{2,1,0:T(8,128)(2,1)S(1)}, bf16[48,256,256]{2,1,0:T(8,128)(2,1)}, u32[]{:S(2)}) copy-start(bf16[48,256,256]{2,1,0:T(8,128)(2,1)} %value_cache.3) | copy-start | bytes 18874372
  5.6 1.2 copy-start.2
  6.8 0.9 copy-start.3
  7.7 0.9 copy-start.4
  8.6 0.7 copy-start.5
  9.2 0.7 copy-start.6
  14.2 14.4 %collective-permute-start = (bf16[16,2048]{1,0:T(8,128)(2,1)S(1)}, bf16[16,2048]{1,0:T(8,128)(2,1)S(1)}, u32[]{:S(2)}, u32[]{:S(2)}) collective-permute-start(bf16[16,2048]{1,0:T(8,128)(2,1)S(1)} %shard_map.82.refs_0_), channel_id=1, source_target_pairs={{0,4},{4,0},{8,12},{12,8},{16,20},{20,16},{24,28},{28,24},{1,5},{5... | collective-permute-start | bytes 196616 | tf_op jit(solution)/shard_map/ppermute | solution.py:159
  14.7 15.4 %collective-permute-start.1 = (bf16[16,2048]{1,0:T(8,128)(2,1)S(1)}, bf16[16,2048]{1,0:T(8,128)(2,1)S(1)}, u32[]{:S(2)}, u32[]{:S(2)}) collective-permute-start(bf16[16,2048]{1,0:T(8,128)(2,1)S(1)} %shard_map.82.refs_0_), channel_id=1, source_target_pairs={{0,8},{4,12},{8,0},{12,4},{16,24},{20,28},{24,16},{28,20},{1,9},{5... | collective-permute-start | bytes 196616 | tf_op jit(solution)/shard_map/ppermute | solution.py:159
  25.1 11.9 %collective-permute-start.14 = (bf16[32,2048]{1,0:T(8,128)(2,1)S(1)}, bf16[32,2048]{1,0:T(8,128)(2,1)S(1)}, u32[]{:S(2)}, u32[]{:S(2)}) collective-permute-start(bf16[32,2048]{1,0:T(8,128)(2,1)S(1)} %shard_map.84.refs_0_), channel_id=1, source_target_pairs={{0,8},{4,12},{8,0},{12,4},{16,24},{20,28},{24,16},{28,20},{1,9},{5... | collective-permute-start | bytes 393224 | tf_op jit(solution)/shard_map/ppermute | solution.py:159
  25.2 11.9 %collective-permute-start.16 = (bf16[32,2048]{1,0:T(8,128)(2,1)S(1)}, bf16[32,2048]{1,0:T(8,128)(2,1)S(1)}, u32[]{:S(2)}, u32[]{:S(2)}) collective-permute-start(bf16[32,2048]{1,0:T(8,128)(2,1)S(1)} %shard_map.84.refs_0_), channel_id=1, source_target_pairs={{0,16},{4,20},{8,24},{12,28},{16,0},{20,4},{24,8},{28,12},{1,17},{... | collective-permute-start | bytes 393224 | tf_op jit(solution)/shard_map/ppermute | solution.py:159
  27.2 10.3 %collective-permute-start.18 = (bf16[32,2048]{1,0:T(8,128)(2,1)S(1)}, bf16[32,2048]{1,0:T(8,128)(2,1)S(1)}, u32[]{:S(2)}, u32[]{:S(2)}) collective-permute-start(bf16[32,2048]{1,0:T(8,128)(2,1)S(1)} %shard_map.84.refs_0_), channel_id=1, source_target_pairs={{0,24},{4,28},{8,16},{12,20},{16,8},{20,12},{24,0},{28,4},{1,25},{... | collective-permute-start | bytes 393224 | tf_op jit(solution)/shard_map/ppermute | solution.py:159
  28.6 7.8 %collective-permute-start.3 = (bf16[16,2048]{1,0:T(8,128)(2,1)S(1)}, bf16[16,2048]{1,0:T(8,128)(2,1)S(1)}, u32[]{:S(2)}, u32[]{:S(2)}) collective-permute-start(bf16[16,2048]{1,0:T(8,128)(2,1)S(1)} %shard_map.82.refs_0_), channel_id=1, source_target_pairs={{0,16},{4,20},{8,24},{12,28},{16,0},{20,4},{24,8},{28,12},{1,17},{... | collective-permute-start | bytes 196616 | tf_op jit(solution)/shard_map/ppermute | solution.py:159
  30.2 6.3 %collective-permute-start.5 = (bf16[16,2048]{1,0:T(8,128)(2,1)S(1)}, bf16[16,2048]{1,0:T(8,128)(2,1)S(1)}, u32[]{:S(2)}, u32[]{:S(2)}) collective-permute-start(bf16[16,2048]{1,0:T(8,128)(2,1)S(1)} %shard_map.82.refs_0_), channel_id=1, source_target_pairs={{0,24},{4,28},{8,16},{12,20},{16,8},{20,12},{24,0},{28,4},{1,25},{... | collective-permute-start | bytes 196616 | tf_op jit(solution)/shard_map/ppermute | solution.py:159
  36.5 1.3 collective-permute-start.2
  36.5 1.5 %collective-permute-start.4 = (bf16[16,2048]{1,0:T(8,128)(2,1)S(1)}, bf16[16,2048]{1,0:T(8,128)(2,1)S(1)}, u32[]{:S(2)}, u32[]{:S(2)}) collective-permute-start(bf16[16,2048]{1,0:T(8,128)(2,1)S(1)} %collective-permute-done.3.refs_4_), channel_id=1, source_target_pairs={{0,4},{4,0},{8,12},{12,8},{16,20},{20,16},{24,28},{28,24},{1,5},{5... | collective-permute-start | bytes 196616 | tf_op jit(solution)/shard_map/ppermute | solution.py:159
  37.0 1.3 collective-permute-start.6
  37.1 14.2 %collective-permute-start.13 = (bf16[32,2048]{1,0:T(8,128)(2,1)S(1)}, bf16[32,2048]{1,0:T(8,128)(2,1)S(1)}, u32[]{:S(2)}, u32[]{:S(2)}) collective-permute-start(bf16[32,2048]{1,0:T(8,128)(2,1)S(1)} %shard_map.84.refs_0_), channel_id=1, source_target_pairs={{0,4},{4,0},{8,12},{12,8},{16,20},{20,16},{24,28},{28,24},{1,5},{5... | collective-permute-start | bytes 393224 | tf_op jit(solution)/shard_map/ppermute | solution.py:159
  37.5 14.5 %collective-permute-start.15 = (bf16[32,2048]{1,0:T(8,128)(2,1)S(1)}, bf16[32,2048]{1,0:T(8,128)(2,1)S(1)}, u32[]{:S(2)}, u32[]{:S(2)}) collective-permute-start(bf16[32,2048]{1,0:T(8,128)(2,1)S(1)} %collective-permute-done.14.refs_2_), channel_id=1, source_target_pairs={{0,4},{4,0},{8,12},{12,8},{16,20},{20,16},{24,28},{28,24},{1,5},{5... | collective-permute-start | bytes 393224 | tf_op jit(solution)/shard_map/ppermute | solution.py:159
  37.7 14.3 %collective-permute-start.17 = (bf16[32,2048]{1,0:T(8,128)(2,1)S(1)}, bf16[32,2048]{1,0:T(8,128)(2,1)S(1)}, u32[]{:S(2)}, u32[]{:S(2)}) collective-permute-start(bf16[32,2048]{1,0:T(8,128)(2,1)S(1)} %collective-permute-done.16.refs_4_), channel_id=1, source_target_pairs={{0,4},{4,0},{8,12},{12,8},{16,20},{20,16},{24,28},{28,24},{1,5},{5... | collective-permute-start | bytes 393224 | tf_op jit(solution)/shard_map/ppermute | solution.py:159
  38.0 14.0 %collective-permute-start.19 = (bf16[32,2048]{1,0:T(8,128)(2,1)S(1)}, bf16[32,2048]{1,0:T(8,128)(2,1)S(1)}, u32[]{:S(2)}, u32[]{:S(2)}) collective-permute-start(bf16[32,2048]{1,0:T(8,128)(2,1)S(1)} %collective-permute-done.18.refs_6_), channel_id=1, source_target_pairs={{0,4},{4,0},{8,12},{12,8},{16,20},{20,16},{24,28},{28,24},{1,5},{5... | collective-permute-start | bytes 393224 | tf_op jit(solution)/shard_map/ppermute | solution.py:159
  47.7 14.9 %collective-permute-start.7 = (bf16[32,4096]{1,0:T(8,128)(2,1)S(1)}, bf16[32,4096]{1,0:T(8,128)(2,1)S(1)}, u32[]{:S(2)}, u32[]{:S(2)}) collective-permute-start(bf16[32,4096]{1,0:T(8,128)(2,1)S(1)} %get-tuple-element.11), channel_id=1, source_target_pairs={{0,1},{4,5},{8,9},{12,13},{16,17},{20,21},{24,25},{28,29}} | collective-permute-start | bytes 786440 | tf_op jit(solution)/shard_map/ppermute | solution.py:198
  51.3 16.9 %collective-permute-start.10 = (bf16[32,4096]{1,0:T(8,128)(2,1)S(1)}, bf16[32,4096]{1,0:T(8,128)(2,1)S(1)}, u32[]{:S(2)}, u32[]{:S(2)}) collective-permute-start(bf16[32,4096]{1,0:T(8,128)(2,1)S(1)} %get-tuple-element.12), channel_id=1, source_target_pairs={{3,2},{7,6},{11,10},{15,14},{19,18},{23,22},{27,26},{31,30}} | collective-permute-start | bytes 786440 | tf_op jit(solution)/shard_map/ppermute | solution.py:199
  62.6 7.9 %collective-permute-start.8 = (bf16[32,4096]{1,0:T(8,128)(2,1)S(1)}, bf16[32,4096]{1,0:T(8,128)(2,1)S(1)}, u32[]{:S(2)}, u32[]{:S(2)}) collective-permute-start(bf16[32,4096]{1,0:T(8,128)(2,1)S(1)} %add_convert_fusion.7), channel_id=1, source_target_pairs={{0,1},{1,2},{4,5},{5,6},{8,9},{9,10},{12,13},{13,14},{16,17},{17,1... | collective-permute-start | bytes 786440 | tf_op jit(solution)/shard_map/ppermute | solution.py:198
  64.0 17.8 %collective-permute-start.20 = (bf16[64,4096]{1,0:T(8,128)(2,1)S(1)}, bf16[64,4096]{1,0:T(8,128)(2,1)S(1)}, u32[]{:S(2)}, u32[]{:S(2)}) collective-permute-start(bf16[64,4096]{1,0:T(8,128)(2,1)S(1)} %get-tuple-element.7), channel_id=1, source_target_pairs={{0,1},{4,5},{8,9},{12,13},{16,17},{20,21},{24,25},{28,29}} | collective-permute-start | bytes 1572872 | tf_op jit(solution)/shard_map/ppermute | solution.py:198
  67.5 20.2 %collective-permute-start.23 = (bf16[64,4096]{1,0:T(8,128)(2,1)S(1)}, bf16[64,4096]{1,0:T(8,128)(2,1)S(1)}, u32[]{:S(2)}, u32[]{:S(2)}) collective-permute-start(bf16[64,4096]{1,0:T(8,128)(2,1)S(1)} %get-tuple-element.8), channel_id=1, source_target_pairs={{3,2},{7,6},{11,10},{15,14},{19,18},{23,22},{27,26},{31,30}} | collective-permute-start | bytes 1572872 | tf_op jit(solution)/shard_map/ppermute | solution.py:199
  70.7 15.7 %collective-permute-start.11 = (bf16[32,4096]{1,0:T(8,128)(2,1)S(1)}, bf16[32,4096]{1,0:T(8,128)(2,1)S(1)}, u32[]{:S(2)}, u32[]{:S(2)}) collective-permute-start(bf16[32,4096]{1,0:T(8,128)(2,1)S(1)} %get-tuple-element.10), channel_id=1, source_target_pairs={{3,2},{2,1},{7,6},{6,5},{11,10},{10,9},{15,14},{14,13},{19,18},{18... | collective-permute-start | bytes 786440 | tf_op jit(solution)/shard_map/ppermute | solution.py:199
  71.4 27.6 %collective-permute-start.9 = (bf16[32,4096]{1,0:T(8,128)(2,1)S(1)}, bf16[32,4096]{1,0:T(8,128)(2,1)S(1)}, u32[]{:S(2)}, u32[]{:S(2)}) collective-permute-start(bf16[32,4096]{1,0:T(8,128)(2,1)S(1)} %get-tuple-element.9), channel_id=1, source_target_pairs={{0,1},{1,2},{2,3},{4,5},{5,6},{6,7},{8,9},{9,10},{10,11},{12,13},{... | collective-permute-start | bytes 786440 | tf_op jit(solution)/shard_map/ppermute | solution.py:198
  81.9 16.1 %collective-permute-start.21 = (bf16[64,4096]{1,0:T(8,128)(2,1)S(1)}, bf16[64,4096]{1,0:T(8,128)(2,1)S(1)}, u32[]{:S(2)}, u32[]{:S(2)}) collective-permute-start(bf16[64,4096]{1,0:T(8,128)(2,1)S(1)} %add_convert_fusion.3), channel_id=1, source_target_pairs={{0,1},{1,2},{4,5},{5,6},{8,9},{9,10},{12,13},{13,14},{16,17},{17,1... | collective-permute-start | bytes 1572872 | tf_op jit(solution)/shard_map/ppermute | solution.py:198
  86.4 12.6 %collective-permute-start.12 = (bf16[32,4096]{1,0:T(8,128)(2,1)S(1)}, bf16[32,4096]{1,0:T(8,128)(2,1)S(1)}, u32[]{:S(2)}, u32[]{:S(2)}) collective-permute-start(bf16[32,4096]{1,0:T(8,128)(2,1)S(1)} %add_convert_fusion.4), channel_id=1, source_target_pairs={{3,2},{2,1},{1,0},{7,6},{6,5},{5,4},{11,10},{10,9},{9,8},{15,14},{... | collective-permute-start | bytes 786440 | tf_op jit(solution)/shard_map/ppermute | solution.py:199
  98.3 5.9 %collective-permute-start.24 = (bf16[64,4096]{1,0:T(8,128)(2,1)S(1)}, bf16[64,4096]{1,0:T(8,128)(2,1)S(1)}, u32[]{:S(2)}, u32[]{:S(2)}) collective-permute-start(bf16[64,4096]{1,0:T(8,128)(2,1)S(1)} %get-tuple-element.6), channel_id=1, source_target_pairs={{3,2},{2,1},{7,6},{6,5},{11,10},{10,9},{15,14},{14,13},{19,18},{18... | collective-permute-start | bytes 1572872 | tf_op jit(solution)/shard_map/ppermute | solution.py:199
  99.1 15.8 %collective-permute-start.22 = (bf16[64,4096]{1,0:T(8,128)(2,1)S(1)}, bf16[64,4096]{1,0:T(8,128)(2,1)S(1)}, u32[]{:S(2)}, u32[]{:S(2)}) collective-permute-start(bf16[64,4096]{1,0:T(8,128)(2,1)S(1)} %get-tuple-element.5), channel_id=1, source_target_pairs={{0,1},{1,2},{2,3},{4,5},{5,6},{6,7},{8,9},{9,10},{10,11},{12,13},{... | collective-permute-start | bytes 1572872 | tf_op jit(solution)/shard_map/ppermute | solution.py:198
  104.3 24.4 %collective-permute-start.25 = (bf16[64,4096]{1,0:T(8,128)(2,1)S(1)}, bf16[64,4096]{1,0:T(8,128)(2,1)S(1)}, u32[]{:S(2)}, u32[]{:S(2)}) collective-permute-start(bf16[64,4096]{1,0:T(8,128)(2,1)S(1)} %add_convert_fusion), channel_id=1, source_target_pairs={{3,2},{2,1},{1,0},{7,6},{6,5},{5,4},{11,10},{10,9},{9,8},{15,14},{... | collective-permute-start | bytes 1572872 | tf_op jit(solution)/shard_map/ppermute | solution.py:199

commit v2 on v1

v2 whole, which is shorter than its diff:
```python
import functools
import math

import jax
import jax.numpy as jnp
from jax import lax
from jax.experimental import pallas as pl
from jax.experimental.pallas import tpu as pltpu
from jax.sharding import PartitionSpec as P

HEAD_DIM = 128
BLOCK = 16
CHUNK = 16
LOWEST = -1e30


def attend_kernel(first, rows, before, *refs):
    all_lengths, all_accepted, queries, new_keys, new_values, key_cache, value_cache, *refs = refs
    *earlier, picked = refs[:-12]
    lengths, accepted, q_buf, nk_buf, nv_buf, k_buf, v_buf, spread, mixed, small_sems, k_sems, v_sems = refs[-12:]
    draft, _, query_cols = q_buf.shape
    cache_len, key_cols = k_buf.shape[1:]
    groups, heads = key_cols // HEAD_DIM, query_cols // HEAD_DIM
    sharing = heads // groups
    scaling = HEAD_DIM ** (-0.5)
    own = pl.ds(first, rows)
    small = [(all_accepted, accepted), (all_lengths, lengths)]
    small += [(src.at[:, own], dst) for src, dst in ((queries, q_buf), (new_keys, nk_buf), (new_values, nv_buf))]
    small = [pltpu.make_async_copy(src, dst, small_sems.at[n]) for n, (src, dst) in enumerate(small)]
    keys, values = [
        [
            pltpu.make_async_copy(src.at[pl.ds(first + at, CHUNK)], dst.at[pl.ds(at, CHUNK)], sems.at[at // CHUNK])
            for at in range(0, rows, CHUNK)
        ]
        for src, dst, sems in ((key_cache, k_buf, k_sems), (value_cache, v_buf, v_sems))
    ]
    for copy in small:
        copy.start()
    for start in range(0, rows // CHUNK, BLOCK // CHUNK):
        for copy in keys[start : start + BLOCK // CHUNK] + values[start : start + BLOCK // CHUNK]:
            copy.start()
    if before:
        picked[:before, :] = earlier[0][...]
    for copy in small:
        copy.wait()
    lanes = BLOCK * heads
    nt, tn = (((1,), (1,)), ((), ())), (((0,), (0,)), ((), ()))
    lane_row = lax.broadcasted_iota(jnp.int32, (1, lanes), 1) // heads
    for block in range(0, rows, BLOCK):
        here = pl.ds(block, BLOCK)
        row = lax.broadcasted_iota(jnp.int32, (BLOCK, HEAD_DIM), 0)
        chosen = jnp.zeros((BLOCK, HEAD_DIM), jnp.int32)
        length, last = jnp.zeros((1, lanes), jnp.int32), jnp.zeros((1, lanes), jnp.int32)
        for r in range(BLOCK):
            chosen = jnp.where(row == r, accepted[first + block + r], chosen)
            last = jnp.where(lane_row == r, accepted[first + block + r], last)
            length = jnp.where(lane_row == r, lengths[first + block + r], length)
        for h in range(heads):
            cols = pl.ds(h * HEAD_DIM, HEAD_DIM)
            query = q_buf[0, here, cols].astype(jnp.float32)
            for p in range(1, draft):
                query = jnp.where(chosen == p, q_buf[p, here, cols].astype(jnp.float32), query)
            spread[:, h, :] = query
            wide = []
        for g in range(groups):
            keep = lax.broadcasted_iota(jnp.int32, spread.shape, 1) // sharing == g
            wide.append(jnp.where(keep, spread[...], 0.0).reshape(lanes, HEAD_DIM))
        query = jnp.concatenate(wide, axis=1).astype(jnp.bfloat16)

        fresh_keys = nk_buf[:, here, :].reshape(draft * BLOCK, key_cols)
        fresh_values = nv_buf[:, here, :].reshape(draft * BLOCK, key_cols)
        fresh = lax.dot_general(fresh_keys, query, nt, preferred_element_type=jnp.float32) * scaling
        slot = lax.broadcasted_iota(jnp.int32, fresh.shape, 0)
        fresh = jnp.where((slot % BLOCK == lane_row) & (slot // BLOCK <= last), fresh, LOWEST)
        past = []
        for lane in range(0, lanes, HEAD_DIM):
            part = None
            for r in range(lane // heads, (lane + HEAD_DIM) // heads):
                if r % CHUNK == 0:
                    keys[(block + r) // CHUNK].wait()
                score = lax.dot_general(
                    k_buf[block + r], query[lane : lane + HEAD_DIM], nt, preferred_element_type=jnp.float32
                )
                part = score if part is None else jnp.where(lane_row[:, lane : lane + HEAD_DIM] == r, score, part)
            past.append(part)
        past = jnp.concatenate(past, axis=1) * scaling
        past = jnp.where(lax.broadcasted_iota(jnp.int32, past.shape, 0) < length, past, LOWEST)
        peak = jnp.maximum(jnp.max(past, axis=0, keepdims=True), jnp.max(fresh, axis=0, keepdims=True))
        past, fresh = jnp.exp(past - peak), jnp.exp(fresh - peak)
        total = jnp.sum(past, axis=0, keepdims=True) + jnp.sum(fresh, axis=0, keepdims=True)
        weights = jnp.transpose(past / total)
        fresh = (fresh / total).astype(jnp.bfloat16)
        fresh = lax.dot_general(fresh, fresh_values, tn, preferred_element_type=jnp.float32)
        own_group = lax.broadcasted_iota(jnp.int32, (heads, HEAD_DIM), 0) // sharing
        for r in range(BLOCK):
            if r % CHUNK == 0:
                values[(block + r) // CHUNK].wait()
            mine = slice(r * heads, (r + 1) * heads)
            result = jnp.dot(weights[mine].astype(jnp.bfloat16), v_buf[block + r], preferred_element_type=jnp.float32)
            result = result + fresh[mine]
            kept = result[:, :HEAD_DIM]
            for g in range(1, groups):
                kept = jnp.where(own_group == g, result[:, g * HEAD_DIM : (g + 1) * HEAD_DIM], kept)
            mixed[r] = kept
        for h in range(heads):
            picked[pl.ds(before + block, BLOCK), pl.ds(h * HEAD_DIM, HEAD_DIM)] = mixed[:, h, :].astype(jnp.bfloat16)


def attend(first, rows, arrays, earlier=None, after=None):
    draft, _, query_cols = arrays[2].shape
    _, cache_len, key_cols = arrays[5].shape
    heads = query_cols // HEAD_DIM
    vmem, anywhere = pl.BlockSpec(memory_space=pltpu.VMEM), pl.BlockSpec(memory_space=pl.ANY)
    cached = 2 * rows * cache_len * key_cols
    before = 0 if earlier is None else earlier.shape[0]
    extra = [] if earlier is None else [earlier]
    tokens = [] if after is None else [after]

    def kernel(*refs):
        given = 7 + len(extra)
        attend_kernel(first, rows, before, *refs[:given], *refs[given + len(tokens) :])

    return pl.pallas_call(
        kernel,
        out_shape=jax.ShapeDtypeStruct((before + rows, query_cols), jnp.bfloat16),
        in_specs=[anywhere] * 7 + [vmem] * len(extra) + [anywhere] * len(tokens),
        out_specs=vmem,
        scratch_shapes=[
            pltpu.SMEM(arrays[0].shape, jnp.int32),
            pltpu.SMEM(arrays[1].shape, jnp.int32),
            pltpu.VMEM((draft, rows, query_cols), jnp.bfloat16),
            pltpu.VMEM((draft, rows, key_cols), jnp.bfloat16),
            pltpu.VMEM((draft, rows, key_cols), jnp.bfloat16),
            pltpu.VMEM((rows, cache_len, key_cols), jnp.bfloat16),
            pltpu.VMEM((rows, cache_len, key_cols), jnp.bfloat16),
            pltpu.VMEM((BLOCK, heads, HEAD_DIM), jnp.float32),
            pltpu.VMEM((BLOCK, heads, HEAD_DIM), jnp.float32),
            pltpu.SemaphoreType.DMA((5,)),
            pltpu.SemaphoreType.DMA((rows // CHUNK,)),
            pltpu.SemaphoreType.DMA((rows // CHUNK,)),
        ],
        compiler_params=pltpu.CompilerParams(vmem_limit_bytes=8 << 20),
        cost_estimate=pl.CostEstimate(flops=2 * heads * cached, bytes_accessed=2 * cached, transcendentals=rows * heads * cache_len),
    )(*[pltpu.with_memory_space_constraint(a, pltpu.HBM) for a in arrays], *extra, *tokens)


def head_kernel(count, first, tile, *refs):
    pieces, weight, (part, features, held, sems) = refs[:count], refs[count], refs[-4:]
    copies = [
        pltpu.make_async_copy(weight.at[:, pl.ds(first + at, tile)], held.at[n], sems.at[n])
        for n, at in enumerate(range(0, part.shape[1], tile))
    ]
    for copy in copies:
        copy.start()
    at = 0
    for piece in pieces:
        features[pl.ds(at, piece.shape[0]), :] = piece[...]
        at += piece.shape[0]
    for n, copy in enumerate(copies):
        copy.wait()
        product = jnp.dot(features[...], held[n], preferred_element_type=jnp.float32)
        part[:, pl.ds(n * tile, tile)] = product.astype(jnp.bfloat16)


def head(pieces, weight, first, cols, after=None):
    tokens = [] if after is None else [after]
    depth = weight.shape[0]
    rows = sum(piece.shape[0] for piece in pieces)
    tile = min(512, cols)
    whole = pl.BlockSpec(memory_space=pltpu.VMEM)
    return pl.pallas_call(
        functools.partial(head_kernel, len(pieces), first, tile),
        out_shape=jax.ShapeDtypeStruct((rows, cols), jnp.bfloat16),
        in_specs=[whole] * len(pieces) + [pl.BlockSpec(memory_space=pl.ANY)] * (1 + len(tokens)),
        out_specs=whole,
        scratch_shapes=[
            pltpu.VMEM((rows, depth), jnp.bfloat16),
            pltpu.VMEM((cols // tile, depth, tile), jnp.bfloat16),
            pltpu.SemaphoreType.DMA((cols // tile,)),
        ],
        compiler_params=pltpu.CompilerParams(vmem_limit_bytes=28 << 20),
        cost_estimate=pl.CostEstimate(
            flops=2 * rows * depth * cols, bytes_accessed=2 * (depth * cols + rows * depth + rows * cols), transcendentals=0
        ),
    )(*pieces, pltpu.with_memory_space_constraint(weight, pltpu.HBM), *tokens)


def swap(array, dp, bits):
    return lax.ppermute(array, "dp", [(i, i ^ bits) for i in range(dp)])


def behind(array, other):
    return lax.optimization_barrier((array, other))[0]


def shards(
    tensor, dp, queries, new_keys, new_values, key_cache, value_cache, cache_lengths, accepted, head_weight
):
    rows_dev = queries.shape[0]
    queries, new_keys, new_values = [jnp.transpose(a, (1, 0, 2)) for a in (queries, new_keys, new_values)]
    arrays = (cache_lengths, accepted, queries, new_keys, new_values, key_cache, value_cache)
    me, place = lax.axis_index("tensor"), lax.axis_index("dp")
    sources = dp // tensor
    paired = dp == 8 and tensor == 4
    cols = head_weight.shape[1]
    half = cols // 2

    first = attend(0, BLOCK, arrays)
    middle = attend(BLOCK, BLOCK, arrays, after=first)
    if paired:
        beside = behind(swap(first, dp, 2), middle)
        chips = jnp.concatenate([first, beside])
    rest = attend(2 * BLOCK, rows_dev - 2 * BLOCK, arrays, earlier=middle, after=chips if paired else middle)
    if paired:
        below = behind(swap(chips, dp, 4), rest)
        chips = jnp.concatenate([chips, below])
        pieces = [chips, swap(chips, dp, 1)]
    else:
        pieces = [lax.all_gather(first, "dp", axis=0, tiled=True)]
    spare = swap(rest, dp, 2) if paired else None

    def view(part):
        if paired:
            return part.reshape(2, tensor, -1, part.shape[-1])
        return part.reshape(1, tensor, -1, part.shape[-1])

    def chosen(shard):
        return shard ^ (lax.axis_index("dp") // 2) if paired else shard

    def add_kernel(step, parity, fresh, part, *refs):
        arrived, sent = refs[: 1 - fresh], refs[-1]
        z = lax.axis_index("tensor")
        shard = jnp.where(lax.rem(z, 2) == parity, tensor - step + z, step - tensor + z)
        at = chosen(jnp.clip(shard, 0, tensor - 1))
        if arrived:
            total = part[:, at].astype(jnp.float32) + arrived[0][...].astype(jnp.float32)
            sent[...] = total.astype(jnp.bfloat16)
        else:
            sent[...] = part[:, at]

    def add(part, step, parity, arrived, after):
        shape = part.shape[:1] + part.shape[2:]
        vmem = pl.BlockSpec(memory_space=pltpu.VMEM)
        given = [part] if arrived is None else [part, arrived]
        return pl.pallas_call(
            functools.partial(add_kernel, step, parity, 2 - len(given)),
            out_shape=jax.ShapeDtypeStruct(shape, jnp.bfloat16),
            in_specs=[vmem] * len(given) + [pl.BlockSpec(memory_space=pl.ANY)],
            out_specs=vmem,
            compiler_params=pltpu.CompilerParams(vmem_limit_bytes=8 << 20),
            cost_estimate=pl.CostEstimate(flops=0, bytes_accessed=6 * math.prod(shape), transcendentals=0),
        )(*given, after)

    def links(step, parity):
        up = [(z, z + 1) for z in range(parity, tensor - 1, 2) if z < step]
        down = [(z + 1, z) for z in range(parity, tensor - 1, 2) if tensor - 2 - z < step]
        return up + down

    parts, arrived = {}, {}

    def send(n, step, parity, after):
        if not links(step, parity):
            return after
        value = add(parts[n], step, parity, arrived.get((n, step - 1, 1 - parity)), after)
        arrived[n, step, parity] = lax.ppermute(value, "tensor", links(step, parity))
        return value

    parts[0] = view(head(pieces, head_weight, 0, cols))
    last = parts[0]
    if paired:
        last = send(0, 1, 0, last)
        last = send(0, 2, 0, last)
        chips = jnp.concatenate([rest, behind(spare, last)])
        last = send(0, 2, 1, last)
        chips = jnp.concatenate([chips, behind(swap(chips, dp, 4), last)])
        rest = [chips, swap(chips, dp, 1)]
    else:
        rest = [lax.all_gather(rest, "dp", axis=0, tiled=True)]
    last = parts[1] = view(head(rest, head_weight, 0, half, last))
    if paired:
        order = [(1, 1, 0), (1, 2, 0), (0, 3, 0), (0, 3, 1), None, (2, 1, 0), (2, 2, 0)]
        order += [(1, 2, 1), (1, 3, 1), (1, 3, 0), (2, 2, 1), (2, 3, 0), (2, 3, 1)]
    else:
        order = [None] + [(n, step, parity) for step in range(1, tensor) for n in range(3) for parity in range(2)]
    for entry in order:
        if entry is None:
            last = parts[2] = view(head(rest, head_weight, half, half, last))
        elif entry not in arrived:
            last = send(*entry, last)

    results = []
    for n in range(3):
        part = parts[n]
        total = lax.dynamic_index_in_dim(part, chosen(me), axis=1, keepdims=False).astype(jnp.float32)
        for parity in range(2):
            if (n, tensor - 1, parity) in arrived:
                total = total + arrived[n, tensor - 1, parity].astype(jnp.float32)
        if paired:
            total = jnp.where(place % 2 == 1, total[::-1], total)
        else:
            total = total.reshape(sources, -1, total.shape[-1])
        results.append(total)
    total = jnp.concatenate([results[0], jnp.concatenate(results[1:], axis=2)], axis=1)
    return total.reshape(-1, cols)


def solution(mesh):
    in_specs = (
        P("dp", None, "tensor"),
        P("dp", None, "tensor"),
        P("dp", None, "tensor"),
        P("dp", None, "tensor"),
        P("dp", None, "tensor"),
        P("dp"),
        P("dp"),
        P("tensor", "dp"),
    )
    out_specs = P("tensor", "dp")
    body = functools.partial(shards, mesh.shape["tensor"], mesh.shape["dp"])
    return jax.shard_map(body, mesh=mesh, in_specs=in_specs, out_specs=out_specs, check_vma=False)
```

time: 131 us -> 92.4 us (0.71)
  waiting for transfers between devices: 47.5 us -> 11.7 us
  local copies, waits for them, and re-layouts: 10 us -> 0 us
  starting transfers between devices: 38 us -> 45 us
    ppermute x12 -> x15, waiting for transfers between devices: 41.1 us -> 8.53 us  [send(): lax.ppermute(value, 'tensor', links(step, parity))]
    ppermute x12 -> x15, starting transfers between devices: 28.2 us -> 38.3 us  [send(): lax.ppermute(value, 'tensor', links(step, parity))]
    unnamed x14 -> x0, local copies, waits for them, and re-layouts: 9.88 us -> none
    ppermute x14 -> x6, waiting for transfers between devices: 6.44 us -> 3.19 us  [swap(): return lax.ppermute(array, 'dp', [(i, i ^ bits) for i in range(dp)])]
    ppermute x14 -> x6, starting transfers between devices: 9.8 us -> 6.71 us  [swap(): return lax.ppermute(array, 'dp', [(i, i ^ bits) for i in range(dp)])]
    pallas_call x4 -> x21, Pallas kernels: 32 us -> 31.3 us  [the longest x3 15.4 us: head(): pl.pallas_call(functools.partial(head_kernel, len(pieces), first, tile),...]
  transfers between devices with their start and end apart: 26 -> 21, of which waited for: 7 -> 4; matrix products, arithmetic and copies ran while one was open for 1% -> 1% of each run, Pallas kernels for 21% -> 30%
where the time goes in v2:
time: 92.4 us; the launch traced here: 91.2 us
  starting transfers between devices  45 us (49%)
  Pallas kernels  31.3 us (34%)
  waiting for transfers between devices  11.7 us (13%)
  other arithmetic  2.77 us (3%)
    ppermute x15, starting transfers between devices, send(): lax.ppermute(value, 'tensor', links(step, parity))  38.3 us
    pallas_call x3, Pallas kernels, head(): pl.pallas_call(functools.partial(head_kernel, len(pieces), first, tile),...  15.4 us
    pallas_call x3, Pallas kernels, attend(): pl.pallas_call(kernel, out_shape=jax.ShapeDtypeStruct((before + rows, que...  11 us
    ppermute x15, waiting for transfers between devices, send(): lax.ppermute(value, 'tensor', links(step, parity))  8.53 us
    ppermute x6, starting transfers between devices, swap(): return lax.ppermute(array, 'dp', [(i, i ^ bits) for i in range(dp)])  6.71 us
    pallas_call x15, Pallas kernels, add(): pl.pallas_call(functools.partial(add_kernel, step, parity, 2 - len(given)...  4.9 us
    ppermute x6, waiting for transfers between devices, swap(): return lax.ppermute(array, 'dp', [(i, i ^ bits) for i in range(dp)])  3.19 us
  transfers between devices with their start and end apart: 21, of which 4 were waited for; matrix products, arithmetic and copies ran while one was open for 1% of the time, Pallas kernels for 30%

profile of v2, /device:TPU:0, one launch (start us, length us, event | category | flops | bytes accessed | tf_op | source)
XLA Modules:
  0.0 91.2 jit_solution(5839298686691416851)
XLA Ops:
  0.0 3.7 %shard_map.82.refs_7_ = bf16[16,2048]{1,0:T(8,128)(2,1)S(1)} custom-call(s32[48]{0:T(128)} %refs_0_.5, s32[48]{0:T(128)} %refs_1_.5, bf16[5,48,2048]{2,1,0:T(8,128)(2,1)} %bitcast.41, bf16[5,48,256]{2,1,0:T(8,128)(2,1)} %bitcast.44, bf16[5,48,256]{2,1,0:T(8,128)(2,1)} %bitcast.47, bf16[48,256,256]{2,1,0:T(8,128)(2,1)} %refs_5_.5, bf16[48,256,256]{2,1,0:T(8,128)(2,1)} %refs_6_.5), custom_call_target="tpu_custom_call" | custom-call | flops 67108864 | bytes 4194304 | tf_op jit(solution)/shard_map/pallas_call | solution.py:123
  3.7 3.0 %collective-permute-start = (bf16[16,2048]{1,0:T(8,128)(2,1)S(1)}, bf16[16,2048]{1,0:T(8,128)(2,1)S(1)}, u32[]{:S(2)}, u32[]{:S(2)}) collective-permute-start(bf16[16,2048]{1,0:T(8,128)(2,1)S(1)} %shard_map.82.refs_7_), channel_id=1, source_target_pairs={{0,8},{4,12},{8,0},{12,4},{16,24},{20,28},{24,16},{28,20},{1,9},{5... | collective-permute-start | bytes 196616 | tf_op jit(solution)/shard_map/ppermute | solution.py:189
  6.7 3.7 %shard_map.83.refs_7_ = bf16[16,2048]{1,0:T(8,128)(2,1)S(1)} custom-call(s32[48]{0:T(128)} %refs_0_.5, s32[48]{0:T(128)} %refs_1_.5, bf16[5,48,2048]{2,1,0:T(8,128)(2,1)} %bitcast.42, bf16[5,48,256]{2,1,0:T(8,128)(2,1)} %bitcast.45, bf16[5,48,256]{2,1,0:T(8,128)(2,1)} %bitcast.48, bf16[48,256,256]{2,1,0:T(8,128)(2,1)} %refs_5_.5, ...), custom_call_target="tpu_custom_call" | custom-call | flops 67108864 | bytes 4194304 | tf_op jit(solution)/shard_map/pallas_call | solution.py:123
  10.3 0.0 collective-permute-done
  10.4 1.6 %collective-permute-start.1 = (bf16[32,2048]{1,0:T(8,128)(2,1)S(1)}, bf16[32,2048]{1,0:T(8,128)(2,1)S(1)}, u32[]{:S(2)}, u32[]{:S(2)}) collective-permute-start(bf16[32,2048]{1,0:T(8,128)(2,1)S(1)} %pad_maximum_fusion.3.refs_8_), channel_id=1, source_target_pairs={{0,16},{4,20},{8,24},{12,28},{16,0},{20,4},{24,8},{28,12},{1,17},{... | collective-permute-start | bytes 393224 | tf_op jit(solution)/shard_map/ppermute | solution.py:189
  12.0 3.7 %shard_map.84 = bf16[32,2048]{1,0:T(8,128)(2,1)S(1)} custom-call(s32[48]{0:T(128)} %refs_0_.5, s32[48]{0:T(128)} %refs_1_.5, bf16[5,48,2048]{2,1,0:T(8,128)(2,1)} %bitcast.43, bf16[5,48,256]{2,1,0:T(8,128)(2,1)} %bitcast.46, bf16[5,48,256]{2,1,0:T(8,128)(2,1)} %bitcast.49, bf16[48,256,256]{2,1,0:T(8,128)(2,1)} %refs_5_.5, bf16[48,256,256]{2,1,0:T(8,128)(2,1)} %refs_6_.5, ...), custom_call_target="tpu_custom_call" | custom-call | flops 67108864 | bytes 4194304 | tf_op jit(solution)/shard_map/pallas_call | solution.py:123
  15.6 0.0 collective-permute-done.1
  15.7 0.1 collective-permute-start.2
  15.7 0.6 collective-permute-start.5
  16.4 0.9 collective-permute-done.2.refs_1_
  17.3 6.5 %shard_map.85 = bf16[128,4096]{1,0:T(8,128)(2,1)S(1)} custom-call(bf16[64,2048]{1,0:T(8,128)(2,1)S(1)} %pad_maximum_fusion.1.refs_0_, bf16[64,2048]{1,0:T(8,128)(2,1)S(1)} %collective-permute-done.2.refs_1_, bf16[2048,4096]{1,0:T(8,128)(2,1)} %refs_2_.5), custom_call_target="tpu_custom_call" | custom-call | flops 2147483648 | bytes 18350080 | tf_op jit(solution)/shard_map/pallas_call | solution.py:171
  23.8 3.5 %collective-permute-start.3 = (bf16[2,16,4096]{2,1,0:T(8,128)(2,1)S(1)}, bf16[2,16,4096]{2,1,0:T(8,128)(2,1)S(1)}, u32[]{:S(2)}, u32[]{:S(2)}) collective-permute-start(bf16[2,16,4096]{2,1,0:T(8,128)(2,1)S(1)} %shard_map.86.refs_0_), channel_id=1, source_target_pairs={{0,1},{3,2},{4,5},{7,6},{8,9},{11,10},{12,13},{15,14},{16,17},{19,... | collective-permute-start | bytes 786440 | tf_op jit(solution)/shard_map/ppermute | solution.py:265
  27.4 0.0 collective-permute-done.5
  27.4 1.3 %collective-permute-start.6 = (bf16[64,2048]{1,0:T(8,128)(2,1)S(1)}, bf16[64,2048]{1,0:T(8,128)(2,1)S(1)}, u32[]{:S(2)}, u32[]{:S(2)}) collective-permute-start(bf16[64,2048]{1,0:T(8,128)(2,1)S(1)} %pad_maximum_fusion.2), channel_id=1, source_target_pairs={{0,16},{4,20},{8,24},{12,28},{16,0},{20,4},{24,8},{28,12},{1,17},{... | collective-permute-start | bytes 786440 | tf_op jit(solution)/shard_map/ppermute | solution.py:189
  28.7 4.4 %collective-permute-done.3.refs_0_ = bf16[2,16,4096]{2,1,0:T(8,128)(2,1)S(1)} collective-permute-done((bf16[2,16,4096]{2,1,0:T(8,128)(2,1)S(1)}, bf16[2,16,4096]{2,1,0:T(8,128)(2,1)S(1)}, u32[]{:S(2)}, u32[]{:S(2)}) %collective-permute-start.3) | collective-permute-done | bytes 262176 | tf_op jit(solution)/shard_map/ppermute | solution.py:265
  33.1 0.1 shard_map.88.refs_3_
  33.2 2.3 %collective-permute-done.6 = bf16[64,2048]{1,0:T(8,128)(2,1)S(1)} collective-permute-done((bf16[64,2048]{1,0:T(8,128)(2,1)S(1)}, bf16[64,2048]{1,0:T(8,128)(2,1)S(1)}, u32[]{:S(2)}, u32[]{:S(2)}) %collective-permute-start.6) | collective-permute-done | bytes 262176 | tf_op jit(solution)/shard_map/ppermute | solution.py:189
  35.6 0.1 collective-permute-start.7
  35.6 0.7 collective-permute-start.4
  36.3 4.9 %collective-permute-start.9 = (bf16[2,16,4096]{2,1,0:T(8,128)(2,1)S(1)}, bf16[2,16,4096]{2,1,0:T(8,128)(2,1)S(1)}, u32[]{:S(2)}, u32[]{:S(2)}) collective-permute-start(bf16[2,16,4096]{2,1,0:T(8,128)(2,1)S(1)} %shard_map.87.refs_1_), channel_id=1, source_target_pairs={{0,1},{3,2},{4,5},{7,6},{8,9},{11,10},{12,13},{15,14},{16,17},{19,... | collective-permute-start | bytes 786440 | tf_op jit(solution)/shard_map/ppermute | solution.py:265
  41.3 0.0 collective-permute-done.7.refs_1_
  41.3 4.5 %shard_map.89 = bf16[256,2048]{1,0:T(8,128)(2,1)S(1)} custom-call(bf16[128,2048]{1,0:T(8,128)(2,1)S(1)} %pad_maximum_fusion.refs_0_, bf16[128,2048]{1,0:T(8,128)(2,1)S(1)} %collective-permute-done.7.refs_1_, bf16[2048,4096]{1,0:T(8,128)(2,1)} %refs_2_.5, bf16[2,16,4096]{2,1,0:T(8,128)(2,1)S(1)} %shard_map.88.refs_3_), custom_call_target="tpu_custom_call" | custom-call | flops 2147483648 | bytes 10485760 | tf_op jit(solution)/shard_map/pallas_call | solution.py:171
  45.7 0.7 shard_map.90.refs_0_
  46.5 0.7 shard_map.91.refs_1_
  47.2 2.0 %collective-permute-start.11 = (bf16[2,32,2048]{2,1,0:T(8,128)(2,1)}, bf16[2,32,2048]{2,1,0:T(8,128)(2,1)}, u32[]{:S(2)}, u32[]{:S(2)}) collective-permute-start(bf16[2,32,2048]{2,1,0:T(8,128)(2,1)} %shard_map.90.refs_0_), channel_id=1, source_target_pairs={{0,1},{3,2},{4,5},{7,6},{8,9},{11,10},{12,13},{15,14},{16,17},{19,... | collective-permute-start | bytes 786440 | tf_op jit(solution)/shard_map/ppermute | solution.py:265
  49.2 2.0 %collective-permute-start.13 = (bf16[2,32,2048]{2,1,0:T(8,128)(2,1)}, bf16[2,32,2048]{2,1,0:T(8,128)(2,1)}, u32[]{:S(2)}, u32[]{:S(2)}) collective-permute-start(bf16[2,32,2048]{2,1,0:T(8,128)(2,1)} %shard_map.91.refs_1_), channel_id=1, source_target_pairs={{0,1},{3,2},{4,5},{7,6},{8,9},{11,10},{12,13},{15,14},{16,17},{19,... | collective-permute-start | bytes 786440 | tf_op jit(solution)/shard_map/ppermute | solution.py:265
  51.2 0.0 collective-permute-done.4.refs_0_
  51.2 0.8 shard_map.92.refs_1_
  52.0 0.0 collective-permute-done.9.refs_0_
  52.0 0.1 shard_map.93.refs_3_
  52.0 1.4 %collective-permute-start.10 = (bf16[2,16,4096]{2,1,0:T(8,128)(2,1)S(1)}, bf16[2,16,4096]{2,1,0:T(8,128)(2,1)}, u32[]{:S(2)}, u32[]{:S(2)}) collective-permute-start(bf16[2,16,4096]{2,1,0:T(8,128)(2,1)S(1)} %shard_map.93.refs_3_), channel_id=1, source_target_pairs={{1,2},{2,1},{5,6},{6,5},{9,10},{10,9},{13,14},{14,13},{17,18},{18,... | collective-permute-start | bytes 786440 | tf_op jit(solution)/shard_map/ppermute | solution.py:265
  53.4 0.0 collective-permute-start.8
  53.4 4.5 %shard_map.94 = bf16[256,2048]{1,0:T(8,128)(2,1)S(1)} custom-call(bf16[128,2048]{1,0:T(8,128)(2,1)S(1)} %pad_maximum_fusion.refs_0_, bf16[128,2048]{1,0:T(8,128)(2,1)S(1)} %collective-permute-done.7.refs_1_, bf16[2048,4096]{1,0:T(8,128)(2,1)} %refs_2_.5, bf16[2,16,4096]{2,1,0:T(8,128)(2,1)S(1)} %shard_map.93.refs_3_), custom_call_target="tpu_custom_call" | custom-call | flops 2147483648 | bytes 10485760 | tf_op jit(solution)/shard_map/pallas_call | solution.py:171
  58.0 3.9 %collective-permute-start.16 = (bf16[2,32,2048]{2,1,0:T(8,128)(2,1)S(1)}, bf16[2,32,2048]{2,1,0:T(8,128)(2,1)S(1)}, u32[]{:S(2)}, u32[]{:S(2)}) collective-permute-start(bf16[2,32,2048]{2,1,0:T(8,128)(2,1)S(1)} %shard_map.95.refs_0_), channel_id=1, source_target_pairs={{0,1},{3,2},{4,5},{7,6},{8,9},{11,10},{12,13},{15,14},{16,17},{19,... | collective-permute-start | bytes 786440 | tf_op jit(solution)/shard_map/ppermute | solution.py:265
  61.9 0.0 collective-permute-done.11.refs_0_
  61.9 1.3 %collective-permute-start.19 = (bf16[2,32,2048]{2,1,0:T(8,128)(2,1)S(1)}, bf16[2,32,2048]{2,1,0:T(8,128)(2,1)S(1)}, u32[]{:S(2)}, u32[]{:S(2)}) collective-permute-start(bf16[2,32,2048]{2,1,0:T(8,128)(2,1)S(1)} %shard_map.96.refs_1_), channel_id=1, source_target_pairs={{0,1},{3,2},{4,5},{7,6},{8,9},{11,10},{12,13},{15,14},{16,17},{19,... | collective-permute-start | bytes 786440 | tf_op jit(solution)/shard_map/ppermute | solution.py:265
  63.2 1.0 %shard_map.97.refs_1_ = bf16[2,32,2048]{2,1,0:T(8,128)(2,1)S(1)} custom-call(bf16[2,4,32,2048]{3,2,1,0:T(8,128)(2,1)S(1)} %bitcast.23, bf16[2,32,2048]{2,1,0:T(8,128)(2,1)} %collective-permute-done.11.refs_0_, bf16[2,32,2048]{2,1,0:T(8,128)(2,1)S(1)} %shard_map.96.refs_1_), custom_call_target="tpu_custom_call" | custom-call | bytes 786432 | tf_op jit(solution)/shard_map/pallas_call | solution.py:245
  64.3 0.0 collective-permute-done.13.refs_0_
  64.3 0.7 collective-permute-start.12
  65.0 1.0 %shard_map.98.refs_1_ = bf16[2,32,2048]{2,1,0:T(8,128)(2,1)S(1)} custom-call(bf16[2,4,32,2048]{3,2,1,0:T(8,128)(2,1)S(1)} %bitcast.24, bf16[2,32,2048]{2,1,0:T(8,128)(2,1)} %collective-permute-done.13.refs_0_, bf16[2,32,2048]{2,1,0:T(8,128)(2,1)S(1)} %shard_map.97.refs_1_), custom_call_target="tpu_custom_call" | custom-call | bytes 786432 | tf_op jit(solution)/shard_map/pallas_call | solution.py:245
  66.0 0.0 collective-permute-done.10
  66.0 0.7 collective-permute-start.15
  66.7 0.0 collective-permute-done.8
  66.7 1.1 %fusion.2 = f32[2,16,4096]{2,1,0:T(8,128)S(1)} fusion(bf16[2,16,4096]{2,1,0:T(8,128)(2,1)} %collective-permute-done.10, bf16[2,16,4096]{2,1,0:T(8,128)(2,1)} %collective-permute-done.8, bf16[2,4,16,4096]{3,2,1,0:T(8,128)(2,1)S(1)} %bitcast.33, s32[]{:T(128)S(6)} %select_n.47), kind=kLoop, calls=%fused_computation.10 | loop fusion | flops 655360 | bytes 1310724 | tf_op jit(solution)/shard_map/add | solution.py:297
  67.8 0.0 collective-permute-done.12.refs_0_
  67.9 0.1 shard_map.99.refs_1_
  67.9 7.0 %collective-permute-start.14 = (bf16[2,32,2048]{2,1,0:T(8,128)(2,1)S(1)}, bf16[2,32,2048]{2,1,0:T(8,128)(2,1)S(1)}, u32[]{:S(2)}, u32[]{:S(2)}) collective-permute-start(bf16[2,32,2048]{2,1,0:T(8,128)(2,1)S(1)} %shard_map.99.refs_1_), channel_id=1, source_target_pairs={{0,1},{2,3},{1,0},{3,2},{4,5},{6,7},{5,4},{7,6},{8,9},{10,11},{9,8... | collective-permute-start | bytes 786440 | tf_op jit(solution)/shard_map/ppermute | solution.py:265
  74.9 0.0 collective-permute-done.16.refs_0_
  74.9 0.1 shard_map.100.refs_1_
  75.0 0.7 collective-permute-start.17
  75.7 0.0 collective-permute-done.17.refs_0_
  75.7 0.1 shard_map.101.refs_1_
  75.8 8.9 %collective-permute-start.18 = (bf16[2,32,2048]{2,1,0:T(8,128)(2,1)S(1)}, bf16[2,32,2048]{2,1,0:T(8,128)(2,1)S(1)}, u32[]{:S(2)}, u32[]{:S(2)}) collective-permute-start(bf16[2,32,2048]{2,1,0:T(8,128)(2,1)S(1)} %shard_map.101.refs_1_), channel_id=1, source_target_pairs={{0,1},{2,3},{1,0},{3,2},{4,5},{6,7},{5,4},{7,6},{8,9},{10,11},{9,8... | collective-permute-start | bytes 786440 | tf_op jit(solution)/shard_map/ppermute | solution.py:265
  84.8 0.0 collective-permute-done.19.refs_0_
  84.8 0.1 shard_map.102
  84.9 0.7 collective-permute-start.20
  85.6 0.0 collective-permute-done.15
  85.6 0.0 collective-permute-done.14
  85.6 0.1 fusion.1
  85.7 0.0 collective-permute-done.20
  85.7 4.1 %collective-permute-done.18 = bf16[2,32,2048]{2,1,0:T(8,128)(2,1)S(1)} collective-permute-done((bf16[2,32,2048]{2,1,0:T(8,128)(2,1)S(1)}, bf16[2,32,2048]{2,1,0:T(8,128)(2,1)S(1)}, u32[]{:S(2)}, u32[]{:S(2)}) %collective-permute-start.18) | collective-permute-done | bytes 262176 | tf_op jit(solution)/shard_map/ppermute | solution.py:265
  89.8 0.1 fusion
  90.0 1.3 %maximum_maximum_fusion = f32[2,48,4096]{2,1,0:T(8,128)} fusion(f32[2,32,2048]{2,1,0:T(8,128)S(1)} %reverse_select_fusion, f32[2,32,2048]{2,1,0:T(8,128)S(1)} %reverse_select_fusion.1, f32[2,16,4096]{2,1,0:T(8,128)S(1)} %reverse_select_fusion.2), kind=kLoop, calls=%fused_computation | loop fusion | flops 786432 | bytes 3145728 | tf_op jit(solution)/shard_map/concatenate | solution.py:303
  (11 shorter events, 0.4 us)
Async XLA Ops:
  3.7 6.7 %collective-permute-start = (bf16[16,2048]{1,0:T(8,128)(2,1)S(1)}, bf16[16,2048]{1,0:T(8,128)(2,1)S(1)}, u32[]{:S(2)}, u32[]{:S(2)}) collective-permute-start(bf16[16,2048]{1,0:T(8,128)(2,1)S(1)} %shard_map.82.refs_7_), channel_id=1, source_target_pairs={{0,8},{4,12},{8,0},{12,4},{16,24},{20,28},{24,16},{28,20},{1,9},{5... | collective-permute-start | bytes 196616 | tf_op jit(solution)/shard_map/ppermute | solution.py:189
  10.4 5.3 %collective-permute-start.1 = (bf16[32,2048]{1,0:T(8,128)(2,1)S(1)}, bf16[32,2048]{1,0:T(8,128)(2,1)S(1)}, u32[]{:S(2)}, u32[]{:S(2)}) collective-permute-start(bf16[32,2048]{1,0:T(8,128)(2,1)S(1)} %pad_maximum_fusion.3.refs_8_), channel_id=1, source_target_pairs={{0,16},{4,20},{8,24},{12,28},{16,0},{20,4},{24,8},{28,12},{1,17},{... | collective-permute-start | bytes 393224 | tf_op jit(solution)/shard_map/ppermute | solution.py:189
  15.7 1.6 %collective-permute-start.2 = (bf16[64,2048]{1,0:T(8,128)(2,1)S(1)}, bf16[64,2048]{1,0:T(8,128)(2,1)S(1)}, u32[]{:S(2)}, u32[]{:S(2)}) collective-permute-start(bf16[64,2048]{1,0:T(8,128)(2,1)S(1)} %pad_maximum_fusion.1.refs_0_), channel_id=1, source_target_pairs={{0,4},{4,0},{8,12},{12,8},{16,20},{20,16},{24,28},{28,24},{1,5},{5... | collective-permute-start | bytes 786440 | tf_op jit(solution)/shard_map/ppermute | solution.py:189
  15.7 11.6 %collective-permute-start.5 = (bf16[32,2048]{1,0:T(8,128)(2,1)S(1)}, bf16[32,2048]{1,0:T(8,128)(2,1)S(1)}, u32[]{:S(2)}, u32[]{:S(2)}) collective-permute-start(bf16[32,2048]{1,0:T(8,128)(2,1)S(1)} %shard_map.84), channel_id=1, source_target_pairs={{0,8},{4,12},{8,0},{12,4},{16,24},{20,28},{24,16},{28,20},{1,9},{5... | collective-permute-start | bytes 393224 | tf_op jit(solution)/shard_map/ppermute | solution.py:189
  23.8 9.3 %collective-permute-start.3 = (bf16[2,16,4096]{2,1,0:T(8,128)(2,1)S(1)}, bf16[2,16,4096]{2,1,0:T(8,128)(2,1)S(1)}, u32[]{:S(2)}, u32[]{:S(2)}) collective-permute-start(bf16[2,16,4096]{2,1,0:T(8,128)(2,1)S(1)} %shard_map.86.refs_0_), channel_id=1, source_target_pairs={{0,1},{3,2},{4,5},{7,6},{8,9},{11,10},{12,13},{15,14},{16,17},{19,... | collective-permute-start | bytes 786440 | tf_op jit(solution)/shard_map/ppermute | solution.py:265
  27.4 8.1 %collective-permute-start.6 = (bf16[64,2048]{1,0:T(8,128)(2,1)S(1)}, bf16[64,2048]{1,0:T(8,128)(2,1)S(1)}, u32[]{:S(2)}, u32[]{:S(2)}) collective-permute-start(bf16[64,2048]{1,0:T(8,128)(2,1)S(1)} %pad_maximum_fusion.2), channel_id=1, source_target_pairs={{0,16},{4,20},{8,24},{12,28},{16,0},{20,4},{24,8},{28,12},{1,17},{... | collective-permute-start | bytes 786440 | tf_op jit(solution)/shard_map/ppermute | solution.py:189
  35.6 5.7 %collective-permute-start.7 = (bf16[128,2048]{1,0:T(8,128)(2,1)S(1)}, bf16[128,2048]{1,0:T(8,128)(2,1)S(1)}, u32[]{:S(2)}, u32[]{:S(2)}) collective-permute-start(bf16[128,2048]{1,0:T(8,128)(2,1)S(1)} %pad_maximum_fusion.refs_0_), channel_id=1, source_target_pairs={{0,4},{4,0},{8,12},{12,8},{16,20},{20,16},{24,28},{28,24},{1,5},{5... | collective-permute-start | bytes 1572872 | tf_op jit(solution)/shard_map/ppermute | solution.py:189
  35.6 15.5 %collective-permute-start.4 = (bf16[2,16,4096]{2,1,0:T(8,128)(2,1)S(1)}, bf16[2,16,4096]{2,1,0:T(8,128)(2,1)S(1)}, u32[]{:S(2)}, u32[]{:S(2)}) collective-permute-start(bf16[2,16,4096]{2,1,0:T(8,128)(2,1)S(1)} %shard_map.88.refs_3_), channel_id=1, source_target_pairs={{1,2},{2,1},{5,6},{6,5},{9,10},{10,9},{13,14},{14,13},{17,18},{18,... | collective-permute-start | bytes 786440 | tf_op jit(solution)/shard_map/ppermute | solution.py:265
  36.3 15.6 %collective-permute-start.9 = (bf16[2,16,4096]{2,1,0:T(8,128)(2,1)S(1)}, bf16[2,16,4096]{2,1,0:T(8,128)(2,1)S(1)}, u32[]{:S(2)}, u32[]{:S(2)}) collective-permute-start(bf16[2,16,4096]{2,1,0:T(8,128)(2,1)S(1)} %shard_map.87.refs_1_), channel_id=1, source_target_pairs={{0,1},{3,2},{4,5},{7,6},{8,9},{11,10},{12,13},{15,14},{16,17},{19,... | collective-permute-start | bytes 786440 | tf_op jit(solution)/shard_map/ppermute | solution.py:265
  47.2 14.7 %collective-permute-start.11 = (bf16[2,32,2048]{2,1,0:T(8,128)(2,1)}, bf16[2,32,2048]{2,1,0:T(8,128)(2,1)}, u32[]{:S(2)}, u32[]{:S(2)}) collective-permute-start(bf16[2,32,2048]{2,1,0:T(8,128)(2,1)} %shard_map.90.refs_0_), channel_id=1, source_target_pairs={{0,1},{3,2},{4,5},{7,6},{8,9},{11,10},{12,13},{15,14},{16,17},{19,... | collective-permute-start | bytes 786440 | tf_op jit(solution)/shard_map/ppermute | solution.py:265
  49.2 15.1 %collective-permute-start.13 = (bf16[2,32,2048]{2,1,0:T(8,128)(2,1)}, bf16[2,32,2048]{2,1,0:T(8,128)(2,1)}, u32[]{:S(2)}, u32[]{:S(2)}) collective-permute-start(bf16[2,32,2048]{2,1,0:T(8,128)(2,1)} %shard_map.91.refs_1_), channel_id=1, source_target_pairs={{0,1},{3,2},{4,5},{7,6},{8,9},{11,10},{12,13},{15,14},{16,17},{19,... | collective-permute-start | bytes 786440 | tf_op jit(solution)/shard_map/ppermute | solution.py:265
  52.0 14.0 %collective-permute-start.10 = (bf16[2,16,4096]{2,1,0:T(8,128)(2,1)S(1)}, bf16[2,16,4096]{2,1,0:T(8,128)(2,1)}, u32[]{:S(2)}, u32[]{:S(2)}) collective-permute-start(bf16[2,16,4096]{2,1,0:T(8,128)(2,1)S(1)} %shard_map.93.refs_3_), channel_id=1, source_target_pairs={{1,2},{2,1},{5,6},{6,5},{9,10},{10,9},{13,14},{14,13},{17,18},{18,... | collective-permute-start | bytes 786440 | tf_op jit(solution)/shard_map/ppermute | solution.py:265
  53.4 13.3 %collective-permute-start.8 = (bf16[2,16,4096]{2,1,0:T(8,128)(2,1)}, bf16[2,16,4096]{2,1,0:T(8,128)(2,1)}, u32[]{:S(2)}, u32[]{:S(2)}) collective-permute-start(bf16[2,16,4096]{2,1,0:T(8,128)(2,1)} %shard_map.92.refs_1_), channel_id=1, source_target_pairs={{0,1},{2,3},{1,0},{3,2},{4,5},{6,7},{5,4},{7,6},{8,9},{10,11},{9,8... | collective-permute-start | bytes 786440 | tf_op jit(solution)/shard_map/ppermute | solution.py:265
  58.0 16.9 %collective-permute-start.16 = (bf16[2,32,2048]{2,1,0:T(8,128)(2,1)S(1)}, bf16[2,32,2048]{2,1,0:T(8,128)(2,1)S(1)}, u32[]{:S(2)}, u32[]{:S(2)}) collective-permute-start(bf16[2,32,2048]{2,1,0:T(8,128)(2,1)S(1)} %shard_map.95.refs_0_), channel_id=1, source_target_pairs={{0,1},{3,2},{4,5},{7,6},{8,9},{11,10},{12,13},{15,14},{16,17},{19,... | collective-permute-start | bytes 786440 | tf_op jit(solution)/shard_map/ppermute | solution.py:265
  61.9 22.9 %collective-permute-start.19 = (bf16[2,32,2048]{2,1,0:T(8,128)(2,1)S(1)}, bf16[2,32,2048]{2,1,0:T(8,128)(2,1)S(1)}, u32[]{:S(2)}, u32[]{:S(2)}) collective-permute-start(bf16[2,32,2048]{2,1,0:T(8,128)(2,1)S(1)} %shard_map.96.refs_1_), channel_id=1, source_target_pairs={{0,1},{3,2},{4,5},{7,6},{8,9},{11,10},{12,13},{15,14},{16,17},{19,... | collective-permute-start | bytes 786440 | tf_op jit(solution)/shard_map/ppermute | solution.py:265
  64.3 3.6 %collective-permute-start.12 = (bf16[2,32,2048]{2,1,0:T(8,128)(2,1)S(1)}, bf16[2,32,2048]{2,1,0:T(8,128)(2,1)S(1)}, u32[]{:S(2)}, u32[]{:S(2)}) collective-permute-start(bf16[2,32,2048]{2,1,0:T(8,128)(2,1)S(1)} %shard_map.97.refs_1_), channel_id=1, source_target_pairs={{1,2},{2,1},{5,6},{6,5},{9,10},{10,9},{13,14},{14,13},{17,18},{18,... | collective-permute-start | bytes 786440 | tf_op jit(solution)/shard_map/ppermute | solution.py:265
  66.0 19.5 %collective-permute-start.15 = (bf16[2,32,2048]{2,1,0:T(8,128)(2,1)S(1)}, bf16[2,32,2048]{2,1,0:T(8,128)(2,1)S(1)}, u32[]{:S(2)}, u32[]{:S(2)}) collective-permute-start(bf16[2,32,2048]{2,1,0:T(8,128)(2,1)S(1)} %shard_map.98.refs_1_), channel_id=1, source_target_pairs={{1,2},{2,1},{5,6},{6,5},{9,10},{10,9},{13,14},{14,13},{17,18},{18,... | collective-permute-start | bytes 786440 | tf_op jit(solution)/shard_map/ppermute | solution.py:265
  67.9 17.6 %collective-permute-start.14 = (bf16[2,32,2048]{2,1,0:T(8,128)(2,1)S(1)}, bf16[2,32,2048]{2,1,0:T(8,128)(2,1)S(1)}, u32[]{:S(2)}, u32[]{:S(2)}) collective-permute-start(bf16[2,32,2048]{2,1,0:T(8,128)(2,1)S(1)} %shard_map.99.refs_1_), channel_id=1, source_target_pairs={{0,1},{2,3},{1,0},{3,2},{4,5},{6,7},{5,4},{7,6},{8,9},{10,11},{9,8... | collective-permute-start | bytes 786440 | tf_op jit(solution)/shard_map/ppermute | solution.py:265
  75.0 0.7 collective-permute-start.17
  75.8 14.0 %collective-permute-start.18 = (bf16[2,32,2048]{2,1,0:T(8,128)(2,1)S(1)}, bf16[2,32,2048]{2,1,0:T(8,128)(2,1)S(1)}, u32[]{:S(2)}, u32[]{:S(2)}) collective-permute-start(bf16[2,32,2048]{2,1,0:T(8,128)(2,1)S(1)} %shard_map.101.refs_1_), channel_id=1, source_target_pairs={{0,1},{2,3},{1,0},{3,2},{4,5},{6,7},{5,4},{7,6},{8,9},{10,11},{9,8... | collective-permute-start | bytes 786440 | tf_op jit(solution)/shard_map/ppermute | solution.py:265
  84.9 0.9 collective-permute-start.20

commit v3 on v2

--- a/solution.py
+++ b/solution.py
@@ -1,5 +1,4 @@
 import functools
-import math
 
 import jax
 import jax.numpy as jnp
@@ -12,6 +11,7 @@
 BLOCK = 16
 CHUNK = 16
 LOWEST = -1e30
+SHORT = pl.CostEstimate(flops=0, bytes_accessed=0, transcendentals=0)
 
 
 def attend_kernel(first, rows, before, *refs):
@@ -140,7 +140,7 @@
             pltpu.SemaphoreType.DMA((rows // CHUNK,)),
         ],
         compiler_params=pltpu.CompilerParams(vmem_limit_bytes=8 << 20),
-        cost_estimate=pl.CostEstimate(flops=2 * heads * cached, bytes_accessed=2 * cached, transcendentals=rows * heads * cache_len),
+        cost_estimate=SHORT,
     )(*[pltpu.with_memory_space_constraint(a, pltpu.HBM) for a in arrays], *extra, *tokens)
 
 
@@ -179,9 +179,7 @@
             pltpu.SemaphoreType.DMA((cols // tile,)),
         ],
         compiler_params=pltpu.CompilerParams(vmem_limit_bytes=28 << 20),
-        cost_estimate=pl.CostEstimate(
-            flops=2 * rows * depth * cols, bytes_accessed=2 * (depth * cols + rows * depth + rows * cols), transcendentals=0
-        ),
+        cost_estimate=SHORT,
     )(*pieces, pltpu.with_memory_space_constraint(weight, pltpu.HBM), *tokens)
 
 
@@ -199,25 +197,26 @@
     rows_dev = queries.shape[0]
     queries, new_keys, new_values = [jnp.transpose(a, (1, 0, 2)) for a in (queries, new_keys, new_values)]
     arrays = (cache_lengths, accepted, queries, new_keys, new_values, key_cache, value_cache)
-    me, place = lax.axis_index("tensor"), lax.axis_index("dp")
     sources = dp // tensor
     paired = dp == 8 and tensor == 4
     cols = head_weight.shape[1]
-    half = cols // 2
-
-    first = attend(0, BLOCK, arrays)
-    middle = attend(BLOCK, BLOCK, arrays, after=first)
-    if paired:
-        beside = behind(swap(first, dp, 2), middle)
-        chips = jnp.concatenate([first, beside])
-    rest = attend(2 * BLOCK, rows_dev - 2 * BLOCK, arrays, earlier=middle, after=chips if paired else middle)
-    if paired:
-        below = behind(swap(chips, dp, 4), rest)
-        chips = jnp.concatenate([chips, below])
-        pieces = [chips, swap(chips, dp, 1)]
-    else:
-        pieces = [lax.all_gather(first, "dp", axis=0, tiled=True)]
-    spare = swap(rest, dp, 2) if paired else None
+
+    blocks, chips, pieces, last = [], {}, {}, None
+    for n in range(rows_dev // BLOCK):
+        blocks.append(attend(n * BLOCK, BLOCK, arrays, after=last))
+        last = blocks[n]
+        if paired:
+            chips[n] = swap(blocks[n], dp, 2)
+        if paired and n == 1:
+            chips[0] = jnp.concatenate([blocks[0], behind(chips[0], last)])
+            last = chips[0]
+
+    def along_y(n, after):
+        chips[n] = jnp.concatenate([blocks[n], behind(chips[n], after)])
+
+    def along_cores(n, after):
+        both = jnp.concatenate([chips[n], behind(swap(chips[n], dp, 4), after)])
+        pieces[n] = [both, swap(both, dp, 1)]
 
     def view(part):
         if paired:
@@ -227,28 +226,29 @@
     def chosen(shard):
         return shard ^ (lax.axis_index("dp") // 2) if paired else shard
 
-    def add_kernel(step, parity, fresh, part, *refs):
-        arrived, sent = refs[: 1 - fresh], refs[-1]
+    def add_kernel(steps, parity, places, part, *refs):
+        refs, sent = list(refs[:-1]), refs[-1]
         z = lax.axis_index("tensor")
-        shard = jnp.where(lax.rem(z, 2) == parity, tensor - step + z, step - tensor + z)
-        at = chosen(jnp.clip(shard, 0, tensor - 1))
-        if arrived:
-            total = part[:, at].astype(jnp.float32) + arrived[0][...].astype(jnp.float32)
-            sent[...] = total.astype(jnp.bfloat16)
-        else:
-            sent[...] = part[:, at]
-
-    def add(part, step, parity, arrived, after):
-        shape = part.shape[:1] + part.shape[2:]
+        for n, (step, place) in enumerate(zip(steps, places)):
+            shard = jnp.where(lax.rem(z, 2) == parity, tensor - step + z, step - tensor + z)
+            at = chosen(jnp.clip(shard, 0, tensor - 1))
+            if place is None:
+                sent[n] = part[:, at]
+            else:
+                total = part[:, at].astype(jnp.float32) + refs.pop(0)[place].astype(jnp.float32)
+                sent[n] = total.astype(jnp.bfloat16)
+
+    def add(part, steps, parity, arrived, after):
+        shape = (len(steps), *part.shape[:1], *part.shape[2:])
         vmem = pl.BlockSpec(memory_space=pltpu.VMEM)
-        given = [part] if arrived is None else [part, arrived]
+        given = [part] + [array for array, _ in arrived if array is not None]
         return pl.pallas_call(
-            functools.partial(add_kernel, step, parity, 2 - len(given)),
+            functools.partial(add_kernel, steps, parity, [place for _, place in arrived]),
             out_shape=jax.ShapeDtypeStruct(shape, jnp.bfloat16),
             in_specs=[vmem] * len(given) + [pl.BlockSpec(memory_space=pl.ANY)],
             out_specs=vmem,
             compiler_params=pltpu.CompilerParams(vmem_limit_bytes=8 << 20),
-            cost_estimate=pl.CostEstimate(flops=0, bytes_accessed=6 * math.prod(shape), transcendentals=0),
+            cost_estimate=SHORT,
         )(*given, after)
 
     def links(step, parity):
@@ -256,52 +256,103 @@
         down = [(z + 1, z) for z in range(parity, tensor - 1, 2) if tensor - 2 - z < step]
         return up + down
 
-    parts, arrived = {}, {}
-
-    def send(n, step, parity, after):
-        if not links(step, parity):
-            return after
-        value = add(parts[n], step, parity, arrived.get((n, step - 1, 1 - parity)), after)
-        arrived[n, step, parity] = lax.ppermute(value, "tensor", links(step, parity))
+    parts, arrived, sums = {}, {}, {}
+
+    def multiply(n, after):
+        parts[n] = view(head(pieces[n], head_weight, 0, cols, after))
+        return parts[n]
+
+    def send(n, steps, parity, after):
+        came = [arrived.get((n, step - 1, 1 - parity), (None, None)) for step in steps]
+        value = add(parts[n], steps, parity, came, after)
+        moved = lax.ppermute(value, "tensor", links(steps[0], parity))
+        for place, step in enumerate(steps):
+            arrived[n, step, parity] = moved, place
         return value
 
-    parts[0] = view(head(pieces, head_weight, 0, cols))
-    last = parts[0]
+    def sum_kernel(first, rest):
+        total = first[:, chosen(lax.axis_index("tensor"))].astype(jnp.float32) if len(first.shape) == 4 else first[...]
+        for ref, place in rest:
+            total = total + ref[place].astype(jnp.float32)
+        return total
+
+    def ended(n, parity):
+        return [arrived[n, tensor - 1, parity]] if (n, tensor - 1, parity) in arrived else []
+
+    def finish(n, parity, after):
+        given = [sums.get(n, parts[n])] + [array for array, _ in ended(n, parity)]
+        places = [place for _, place in ended(n, parity)]
+
+        def kernel(*refs):
+            refs[-1][...] = sum_kernel(refs[0], zip(refs[1 : len(given)], places))
+
+        vmem = pl.BlockSpec(memory_space=pltpu.VMEM)
+        sums[n] = pl.pallas_call(
+            kernel,
+            out_shape=jax.ShapeDtypeStruct(parts[n].shape[:1] + parts[n].shape[2:], jnp.float32),
+            in_specs=[vmem] * len(given) + [pl.BlockSpec(memory_space=pl.ANY)],
+            out_specs=vmem,
+            compiler_params=pltpu.CompilerParams(vmem_limit_bytes=8 << 20),
+            cost_estimate=SHORT,
+        )(*given, after)
+        return sums[n]
+
+    def assemble():
+        *earlier, part = [sums.get(n, parts[n]) for n in parts]
+        came = ended(len(parts) - 1, 0) + ended(len(parts) - 1, 1)
+        given = [part] + [array for array, _ in came]
+        places = [place for _, place in came]
+
+        def kernel(*refs):
+            earlier, (part, *rest), out = refs[: len(parts) - 1], refs[len(parts) - 1 : -1], refs[-1]
+            turned = lax.rem(lax.axis_index("dp"), 2) if paired else 0
+            for n in range(len(parts)):
+                total = earlier[n][...] if n < len(earlier) else sum_kernel(part, zip(rest, places))
+                total = total.reshape(sources, BLOCK, cols)
+                for source in range(sources):
+                    out[source ^ turned, pl.ds(n * BLOCK, BLOCK)] = total[source]
+
+        vmem = pl.BlockSpec(memory_space=pltpu.VMEM)
+        out = pl.pallas_call(
+            kernel,
+            out_shape=jax.ShapeDtypeStruct((sources, len(parts) * BLOCK, cols), jnp.float32),
+            in_specs=[vmem] * (len(earlier) + len(given)),
+            out_specs=vmem,
+            compiler_params=pltpu.CompilerParams(vmem_limit_bytes=16 << 20),
+            cost_estimate=SHORT,
+        )(*earlier, *given)
+        return out.reshape(-1, cols)
+
     if paired:
-        last = send(0, 1, 0, last)
-        last = send(0, 2, 0, last)
-        chips = jnp.concatenate([rest, behind(spare, last)])
-        last = send(0, 2, 1, last)
-        chips = jnp.concatenate([chips, behind(swap(chips, dp, 4), last)])
-        rest = [chips, swap(chips, dp, 1)]
+        along_cores(0, last)
+        along_y(1, last)
+        multiply(0, chips[1])
+        last = send(0, (1, 2), 0, parts[0])
+        along_cores(1, last)
+        along_y(2, last)
+        last = multiply(1, chips[2])
+        last = send(1, (1, 2), 0, last)
+        along_cores(2, last)
+        last = multiply(2, last)
+        order = [(2, (1, 2), 0), (0, (2, 3), 1), (1, (2,), 1), (1, (3,), 1), (0, (3,), 0), (2, (2,), 1), (1, (3,), 0)]
+        order += [(2, (3,), 1), (1, 1), (0, 0), (0, 1), (2, (3,), 0)]
+        for entry in order:
+            last = finish(*entry, last) if len(entry) == 2 else send(*entry, last)
+        last = finish(1, 0, last)
     else:
-        rest = [lax.all_gather(rest, "dp", axis=0, tiled=True)]
-    last = parts[1] = view(head(rest, head_weight, 0, half, last))
-    if paired:
-        order = [(1, 1, 0), (1, 2, 0), (0, 3, 0), (0, 3, 1), None, (2, 1, 0), (2, 2, 0)]
-        order += [(1, 2, 1), (1, 3, 1), (1, 3, 0), (2, 2, 1), (2, 3, 0), (2, 3, 1)]
-    else:
-        order = [None] + [(n, step, parity) for step in range(1, tensor) for n in range(3) for parity in range(2)]
-    for entry in order:
-        if entry is None:
-            last = parts[2] = view(head(rest, head_weight, half, half, last))
-        elif entry not in arrived:
-            last = send(*entry, last)
-
-    results = []
-    for n in range(3):
-        part = parts[n]
-        total = lax.dynamic_index_in_dim(part, chosen(me), axis=1, keepdims=False).astype(jnp.float32)
-        for parity in range(2):
-            if (n, tensor - 1, parity) in arrived:
-                total = total + arrived[n, tensor - 1, parity].astype(jnp.float32)
-        if paired:
-            total = jnp.where(place % 2 == 1, total[::-1], total)
-        else:
-            total = total.reshape(sources, -1, total.shape[-1])
-        results.append(total)
-    total = jnp.concatenate([results[0], jnp.concatenate(results[1:], axis=2)], axis=1)
-    return total.reshape(-1, cols)
+        for n, block in enumerate(blocks):
+            pieces[n] = [lax.all_gather(block, "dp", axis=0, tiled=True)]
+            last = multiply(n, last)
+        for step in range(1, tensor):
+            for n in range(len(blocks)):
+                for parity in range(2):
+                    if links(step, parity):
+                        last = send(n, (step,), parity, last)
+
+    for n in range(len(parts) - 1):
+        if n not in sums:
+            last = finish(n, 1, finish(n, 0, last))
+    return assemble()
 
 
 def solution(mesh):

time: 92.4 us -> 84.7 us (0.917)
  starting transfers between devices: 45 us -> 41 us
  other arithmetic: 2.77 us -> 0.09 us
  waiting for transfers between devices: 11.7 us -> 10.1 us
  Pallas kernels: 31.3 us -> 32.8 us
    ppermute x15 -> x11, starting transfers between devices: 38.3 us -> 32 us  [send(): moved = lax.ppermute(value, 'tensor', links(steps[0], parity))]
    pallas_call x3, Pallas kernels: 15.4 us -> 19.5 us  [head(): pl.pallas_call(functools.partial(head_kernel, len(pieces), first, tile),...]
    ppermute x6 -> x9, waiting for transfers between devices: 3.19 us -> 0.03 us  [swap(): return lax.ppermute(array, 'dp', [(i, i ^ bits) for i in range(dp)])]
    pallas_call x15 -> x16, Pallas kernels: 4.9 us -> 2.4 us  [the longest x1 1.3 us: assemble(): pl.pallas_call(kernel, out_shape=jax.ShapeDtypeStruct((sources, len(parts...]
    ppermute x6 -> x9, starting transfers between devices: 6.71 us -> 8.98 us  [swap(): return lax.ppermute(array, 'dp', [(i, i ^ bits) for i in range(dp)])]
    ppermute x15 -> x11, waiting for transfers between devices: 8.53 us -> 10.1 us  [send(): moved = lax.ppermute(value, 'tensor', links(steps[0], parity))]
    add x3 -> x0, other arithmetic: 1.32 us -> none  [shards(): total = total + arrived[n, tensor - 1, parity].astype(jnp.float32)]
    concatenate x5 -> x6, other arithmetic: 1.34 us -> 0.09 us  [the longest x3 0.06 us: along_cores(): both = jnp.concatenate([chips[n], behind(swap(chips[n], dp, 4), after)])]
  transfers between devices with their start and end apart: 21 -> 20, of which waited for: 4 -> 3; matrix products, arithmetic and copies ran while one was open for 1% -> 0% of each run, Pallas kernels for 30% -> 33%
where the time goes in v3:
time: 84.7 us; the launch traced here: 84.4 us
  starting transfers between devices  41 us (48%)
  Pallas kernels  32.8 us (39%)
  waiting for transfers between devices  10.1 us (12%)
    ppermute x11, starting transfers between devices, send(): moved = lax.ppermute(value, 'tensor', links(steps[0], parity))  32 us
    pallas_call x3, Pallas kernels, head(): pl.pallas_call(functools.partial(head_kernel, len(pieces), first, tile),...  19.5 us
    pallas_call x3, Pallas kernels, attend(): pl.pallas_call(kernel, out_shape=jax.ShapeDtypeStruct((before + rows, que...  11 us
    ppermute x11, waiting for transfers between devices, send(): moved = lax.ppermute(value, 'tensor', links(steps[0], parity))  10.1 us
    ppermute x9, starting transfers between devices, swap(): return lax.ppermute(array, 'dp', [(i, i ^ bits) for i in range(dp)])  8.98 us
  transfers between devices with their start and end apart: 20, of which 3 were waited for; matrix products, arithmetic and copies ran while one was open for 0% of the time, Pallas kernels for 33%

profile of v3, /device:TPU:0, one launch (start us, length us, event | category | flops | bytes accessed | tf_op | source)
XLA Modules:
  0.0 84.4 jit_solution(375637078657665571)
XLA Ops:
  0.0 3.7 %shard_map.82.refs_7_ = bf16[16,2048]{1,0:T(8,128)(2,1)S(1)} custom-call(s32[48]{0:T(128)} %refs_0_.5, s32[48]{0:T(128)} %refs_1_.5, bf16[5,48,2048]{2,1,0:T(8,128)(2,1)} %bitcast.24, bf16[5,48,256]{2,1,0:T(8,128)(2,1)} %bitcast.27, bf16[5,48,256]{2,1,0:T(8,128)(2,1)} %bitcast.30, bf16[48,256,256]{2,1,0:T(8,128)(2,1)} %refs_5_.5, bf16[48,256,256]{2,1,0:T(8,128)(2,1)} %refs_6_.5), custom_call_target="tpu_custom_call" | custom-call | tf_op jit(solution)/shard_map/pallas_call | solution.py:123
  3.7 3.0 %collective-permute-start = (bf16[16,2048]{1,0:T(8,128)(2,1)S(1)}, bf16[16,2048]{1,0:T(8,128)(2,1)S(1)}, u32[]{:S(2)}, u32[]{:S(2)}) collective-permute-start(bf16[16,2048]{1,0:T(8,128)(2,1)S(1)} %shard_map.82.refs_7_), channel_id=1, source_target_pairs={{0,8},{4,12},{8,0},{12,4},{16,24},{20,28},{24,16},{28,20},{1,9},{5... | collective-permute-start | bytes 196616 | tf_op jit(solution)/shard_map/ppermute | solution.py:187
  6.7 3.7 %shard_map.83 = bf16[16,2048]{1,0:T(8,128)(2,1)S(1)} custom-call(s32[48]{0:T(128)} %refs_0_.5, s32[48]{0:T(128)} %refs_1_.5, bf16[5,48,2048]{2,1,0:T(8,128)(2,1)} %bitcast.25, bf16[5,48,256]{2,1,0:T(8,128)(2,1)} %bitcast.28, bf16[5,48,256]{2,1,0:T(8,128)(2,1)} %bitcast.31, bf16[48,256,256]{2,1,0:T(8,128)(2,1)} %refs_5_.5, bf16[48,256,256]{2,1,0:T(8,128)(2,1)} %refs_6_.5, ...), custom_call_target="tpu_custom_call" | custom-call | tf_op jit(solution)/shard_map/pallas_call | solution.py:123
  10.3 0.0 collective-permute-done
  10.4 1.6 %collective-permute-start.1 = (bf16[32,2048]{1,0:T(8,128)(2,1)S(1)}, bf16[32,2048]{1,0:T(8,128)(2,1)S(1)}, u32[]{:S(2)}, u32[]{:S(2)}) collective-permute-start(bf16[32,2048]{1,0:T(8,128)(2,1)S(1)} %pad_maximum_fusion.3.refs_7_), channel_id=1, source_target_pairs={{0,16},{4,20},{8,24},{12,28},{16,0},{20,4},{24,8},{28,12},{1,17},{... | collective-permute-start | bytes 393224 | tf_op jit(solution)/shard_map/ppermute | solution.py:187
  12.0 0.6 collective-permute-start.3
  12.5 3.7 %shard_map.84 = bf16[16,2048]{1,0:T(8,128)(2,1)S(1)} custom-call(s32[48]{0:T(128)} %refs_0_.5, s32[48]{0:T(128)} %refs_1_.5, bf16[5,48,2048]{2,1,0:T(8,128)(2,1)} %bitcast.26, bf16[5,48,256]{2,1,0:T(8,128)(2,1)} %bitcast.29, bf16[5,48,256]{2,1,0:T(8,128)(2,1)} %bitcast.32, bf16[48,256,256]{2,1,0:T(8,128)(2,1)} %refs_5_.5, bf16[48,256,256]{2,1,0:T(8,128)(2,1)} %refs_6_.5, ...), custom_call_target="tpu_custom_call" | custom-call | tf_op jit(solution)/shard_map/pallas_call | solution.py:123
  16.2 0.0 collective-permute-done.3
  16.2 0.0 collective-permute-done.1
  16.3 0.1 collective-permute-start.2
  16.4 0.8 collective-permute-start.7
  17.1 1.3 %collective-permute-start.5 = (bf16[16,2048]{1,0:T(8,128)(2,1)S(1)}, bf16[16,2048]{1,0:T(8,128)(2,1)S(1)}, u32[]{:S(2)}, u32[]{:S(2)}) collective-permute-start(bf16[16,2048]{1,0:T(8,128)(2,1)S(1)} %shard_map.84), channel_id=1, source_target_pairs={{0,8},{4,12},{8,0},{12,4},{16,24},{20,28},{24,16},{28,20},{1,9},{5... | collective-permute-start | bytes 196616 | tf_op jit(solution)/shard_map/ppermute | solution.py:187
  18.4 0.0 collective-permute-done.2.refs_1_
  18.4 6.5 %shard_map.85 = bf16[128,4096]{1,0:T(8,128)(2,1)S(1)} custom-call(bf16[64,2048]{1,0:T(8,128)(2,1)S(1)} %pad_maximum_fusion.refs_0_, bf16[64,2048]{1,0:T(8,128)(2,1)S(1)} %collective-permute-done.2.refs_1_, bf16[2048,4096]{1,0:T(8,128)(2,1)} %refs_2_.5, bf16[32,2048]{1,0:T(8,128)(2,1)S(1)} %pad_maximum_fusion.4.refs_3_), custom_call_target="tpu_custom_call" | custom-call | tf_op jit(solution)/shard_map/pallas_call | solution.py:171
  24.9 0.1 shard_map.86
  24.9 0.0 collective-permute-done.7
  25.0 0.1 collective-permute-start.8
  25.0 0.0 collective-permute-done.5
  25.1 1.6 %collective-permute-start.6 = (bf16[32,2048]{1,0:T(8,128)(2,1)S(1)}, bf16[32,2048]{1,0:T(8,128)(2,1)S(1)}, u32[]{:S(2)}, u32[]{:S(2)}) collective-permute-start(bf16[32,2048]{1,0:T(8,128)(2,1)S(1)} %pad_maximum_fusion.5.refs_3_), channel_id=1, source_target_pairs={{0,16},{4,20},{8,24},{12,28},{16,0},{20,4},{24,8},{28,12},{1,17},{... | collective-permute-start | bytes 393224 | tf_op jit(solution)/shard_map/ppermute | solution.py:187
  26.7 3.5 %collective-permute-start.4 = (bf16[2,2,16,4096]{3,2,1,0:T(8,128)(2,1)S(1)}, bf16[2,2,16,4096]{3,2,1,0:T(8,128)(2,1)S(1)}, u32[]{:S(2)}, u32[]{:S(2)}) collective-permute-start(bf16[2,2,16,4096]{3,2,1,0:T(8,128)(2,1)S(1)} %shard_map.86), channel_id=1, source_target_pairs={{0,1},{3,2},{4,5},{7,6},{8,9},{11,10},{12,13},{15,14},{16,17},{19,... | collective-permute-start | bytes 1572872 | tf_op jit(solution)/shard_map/ppermute | solution.py:268
  30.2 0.0 collective-permute-done.8.refs_1_
  30.2 6.5 %shard_map.87 = bf16[128,4096]{1,0:T(8,128)(2,1)S(1)} custom-call(bf16[64,2048]{1,0:T(8,128)(2,1)S(1)} %pad_maximum_fusion.1.refs_0_, bf16[64,2048]{1,0:T(8,128)(2,1)S(1)} %collective-permute-done.8.refs_1_, bf16[2048,4096]{1,0:T(8,128)(2,1)} %refs_2_.5, bf16[32,2048]{1,0:T(8,128)(2,1)S(1)} %pad_maximum_fusion.5.refs_3_), custom_call_target="tpu_custom_call" | custom-call | tf_op jit(solution)/shard_map/pallas_call | solution.py:171
  36.7 0.1 shard_map.88.refs_3_
  36.7 0.0 collective-permute-done.6
  36.8 0.1 collective-permute-start.9
  36.9 1.7 %collective-permute-start.11 = (bf16[2,2,16,4096]{3,2,1,0:T(8,128)(2,1)S(1)}, bf16[2,2,16,4096]{3,2,1,0:T(8,128)(2,1)S(1)}, u32[]{:S(2)}, u32[]{:S(2)}) collective-permute-start(bf16[2,2,16,4096]{3,2,1,0:T(8,128)(2,1)S(1)} %shard_map.88.refs_3_), channel_id=1, source_target_pairs={{0,1},{3,2},{4,5},{7,6},{8,9},{11,10},{12,13},{15,14},{16,17},{19,... | collective-permute-start | bytes 1572872 | tf_op jit(solution)/shard_map/ppermute | solution.py:268
  38.5 0.0 collective-permute-done.9.refs_1_
  38.5 6.5 %shard_map.89 = bf16[128,4096]{1,0:T(8,128)(2,1)S(1)} custom-call(bf16[64,2048]{1,0:T(8,128)(2,1)S(1)} %pad_maximum_fusion.2.refs_0_, bf16[64,2048]{1,0:T(8,128)(2,1)S(1)} %collective-permute-done.9.refs_1_, bf16[2048,4096]{1,0:T(8,128)(2,1)} %refs_2_.5, bf16[2,2,16,4096]{3,2,1,0:T(8,128)(2,1)S(1)} %shard_map.88.refs_3_), custom_call_target="tpu_custom_call" | custom-call | tf_op jit(solution)/shard_map/pallas_call | solution.py:171
  45.0 0.1 shard_map.90.refs_2_
  45.1 0.0 collective-permute-done.4.refs_0_.refs_1_
  45.1 0.1 shard_map.91.refs_1_
  45.2 0.7 collective-permute-start.10
  45.9 4.5 %collective-permute-start.14 = (bf16[2,2,16,4096]{3,2,1,0:T(8,128)(2,1)S(1)}, bf16[2,2,16,4096]{3,2,1,0:T(8,128)(2,1)S(1)}, u32[]{:S(2)}, u32[]{:S(2)}) collective-permute-start(bf16[2,2,16,4096]{3,2,1,0:T(8,128)(2,1)S(1)} %shard_map.90.refs_2_), channel_id=1, source_target_pairs={{0,1},{3,2},{4,5},{7,6},{8,9},{11,10},{12,13},{15,14},{16,17},{19,... | collective-permute-start | bytes 1572872 | tf_op jit(solution)/shard_map/ppermute | solution.py:268
  50.5 3.2 %collective-permute-done.11.refs_0_ = bf16[2,2,16,4096]{3,2,1,0:T(8,128)(2,1)S(1)} collective-permute-done((bf16[2,2,16,4096]{3,2,1,0:T(8,128)(2,1)S(1)}, bf16[2,2,16,4096]{3,2,1,0:T(8,128)(2,1)S(1)}, u32[]{:S(2)}, u32[]{:S(2)}) %collective-permute-start.11) | collective-permute-done | bytes 524320 | tf_op jit(solution)/shard_map/ppermute | solution.py:268
  53.6 0.1 shard_map.92.refs_1_
  53.7 0.7 collective-permute-start.15
  54.4 0.1 shard_map.93.refs_1_
  54.5 0.7 collective-permute-start.13
  55.2 0.0 collective-permute-done.10.refs_0_.refs_1_
  55.2 0.1 shard_map.94.refs_1_
  55.3 7.0 %collective-permute-start.12 = (bf16[1,2,16,4096]{3,2,1,0:T(8,128)(2,1)S(1)}, bf16[1,2,16,4096]{3,2,1,0:T(8,128)(2,1)S(1)}, u32[]{:S(2)}, u32[]{:S(2)}) collective-permute-start(bf16[1,2,16,4096]{3,2,1,0:T(8,128)(2,1)S(1)} %shard_map.94.refs_1_), channel_id=1, source_target_pairs={{0,1},{2,3},{1,0},{3,2},{4,5},{6,7},{5,4},{7,6},{8,9},{10,11},{9,8... | collective-permute-start | bytes 786440 | tf_op jit(solution)/shard_map/ppermute | solution.py:268
  62.3 2.6 %collective-permute-done.14.refs_0_ = bf16[2,2,16,4096]{3,2,1,0:T(8,128)(2,1)S(1)} collective-permute-done((bf16[2,2,16,4096]{3,2,1,0:T(8,128)(2,1)S(1)}, bf16[2,2,16,4096]{3,2,1,0:T(8,128)(2,1)S(1)}, u32[]{:S(2)}, u32[]{:S(2)}) %collective-permute-start.14) | collective-permute-done | bytes 524320 | tf_op jit(solution)/shard_map/ppermute | solution.py:268
  64.9 0.1 shard_map.95.refs_1_
  64.9 0.7 collective-permute-start.17
  65.6 0.0 collective-permute-done.15.refs_0_
  65.6 0.1 shard_map.96.refs_1_
  65.7 5.4 %collective-permute-start.16 = (bf16[1,2,16,4096]{3,2,1,0:T(8,128)(2,1)S(1)}, bf16[1,2,16,4096]{3,2,1,0:T(8,128)(2,1)S(1)}, u32[]{:S(2)}, u32[]{:S(2)}) collective-permute-start(bf16[1,2,16,4096]{3,2,1,0:T(8,128)(2,1)S(1)} %shard_map.96.refs_1_), channel_id=1, source_target_pairs={{0,1},{2,3},{1,0},{3,2},{4,5},{6,7},{5,4},{7,6},{8,9},{10,11},{9,8... | collective-permute-start | bytes 786440 | tf_op jit(solution)/shard_map/ppermute | solution.py:268
  71.1 0.1 shard_map.97.refs_2_
  71.2 0.7 collective-permute-start.19
  71.9 0.0 collective-permute-done.13.refs_1_
  71.9 0.1 shard_map.98.refs_2_.refs_0_
  72.0 0.0 collective-permute-done.12.refs_1_
  72.0 0.1 shard_map.99.refs_0_.refs_2_
  72.1 0.0 collective-permute-done.17.refs_0_
  72.1 0.1 shard_map.101.refs_2_
  72.2 6.5 %collective-permute-start.18 = (bf16[1,2,16,4096]{3,2,1,0:T(8,128)(2,1)S(1)}, bf16[1,2,16,4096]{3,2,1,0:T(8,128)(2,1)S(1)}, u32[]{:S(2)}, u32[]{:S(2)}) collective-permute-start(bf16[1,2,16,4096]{3,2,1,0:T(8,128)(2,1)S(1)} %shard_map.101.refs_2_), channel_id=1, source_target_pairs={{0,1},{2,3},{1,0},{3,2},{4,5},{6,7},{5,4},{7,6},{8,9},{10,11},{9,8... | collective-permute-start | bytes 786440 | tf_op jit(solution)/shard_map/ppermute | solution.py:268
  78.7 0.0 collective-permute-done.16.refs_1_
  78.8 0.0 collective-permute-done.19.refs_4_
  78.8 4.3 %collective-permute-done.18.refs_3_ = bf16[1,2,16,4096]{3,2,1,0:T(8,128)(2,1)S(1)} collective-permute-done((bf16[1,2,16,4096]{3,2,1,0:T(8,128)(2,1)S(1)}, bf16[1,2,16,4096]{3,2,1,0:T(8,128)(2,1)S(1)}, u32[]{:S(2)}, u32[]{:S(2)}) %collective-permute-start.18) | collective-permute-done | bytes 262176 | tf_op jit(solution)/shard_map/ppermute | solution.py:268
  83.1 1.3 %shard_map.103 = f32[2,48,4096]{2,1,0:T(8,128)} custom-call(f32[2,16,4096]{2,1,0:T(8,128)S(1)} %shard_map.100.refs_1_.refs_0_, f32[2,16,4096]{2,1,0:T(8,128)S(1)} %shard_map.102.refs_1_, bf16[2,4,16,4096]{3,2,1,0:T(8,128)(2,1)S(1)} %bitcast.18, bf16[1,2,16,4096]{3,2,1,0:T(8,128)(2,1)S(1)} %collective-permute-done.18.refs_3_, ...), custom_call_target="tpu_custom_call" | custom-call | tf_op jit(solution)/shard_map/pallas_call | solution.py:316
  (8 shorter events, 0.2 us)
Async XLA Ops:
  3.7 6.7 %collective-permute-start = (bf16[16,2048]{1,0:T(8,128)(2,1)S(1)}, bf16[16,2048]{1,0:T(8,128)(2,1)S(1)}, u32[]{:S(2)}, u32[]{:S(2)}) collective-permute-start(bf16[16,2048]{1,0:T(8,128)(2,1)S(1)} %shard_map.82.refs_7_), channel_id=1, source_target_pairs={{0,8},{4,12},{8,0},{12,4},{16,24},{20,28},{24,16},{28,20},{1,9},{5... | collective-permute-start | bytes 196616 | tf_op jit(solution)/shard_map/ppermute | solution.py:187
  10.4 5.9 %collective-permute-start.1 = (bf16[32,2048]{1,0:T(8,128)(2,1)S(1)}, bf16[32,2048]{1,0:T(8,128)(2,1)S(1)}, u32[]{:S(2)}, u32[]{:S(2)}) collective-permute-start(bf16[32,2048]{1,0:T(8,128)(2,1)S(1)} %pad_maximum_fusion.3.refs_7_), channel_id=1, source_target_pairs={{0,16},{4,20},{8,24},{12,28},{16,0},{20,4},{24,8},{28,12},{1,17},{... | collective-permute-start | bytes 393224 | tf_op jit(solution)/shard_map/ppermute | solution.py:187
  12.0 4.3 %collective-permute-start.3 = (bf16[16,2048]{1,0:T(8,128)(2,1)S(1)}, bf16[16,2048]{1,0:T(8,128)(2,1)S(1)}, u32[]{:S(2)}, u32[]{:S(2)}) collective-permute-start(bf16[16,2048]{1,0:T(8,128)(2,1)S(1)} %shard_map.83), channel_id=1, source_target_pairs={{0,8},{4,12},{8,0},{12,4},{16,24},{20,28},{24,16},{28,20},{1,9},{5... | collective-permute-start | bytes 196616 | tf_op jit(solution)/shard_map/ppermute | solution.py:187
  16.3 2.1 %collective-permute-start.2 = (bf16[64,2048]{1,0:T(8,128)(2,1)S(1)}, bf16[64,2048]{1,0:T(8,128)(2,1)S(1)}, u32[]{:S(2)}, u32[]{:S(2)}) collective-permute-start(bf16[64,2048]{1,0:T(8,128)(2,1)S(1)} %pad_maximum_fusion.refs_0_), channel_id=1, source_target_pairs={{0,4},{4,0},{8,12},{12,8},{16,20},{20,16},{24,28},{28,24},{1,5},{5... | collective-permute-start | bytes 786440 | tf_op jit(solution)/shard_map/ppermute | solution.py:187
  16.4 8.6 %collective-permute-start.7 = (bf16[32,2048]{1,0:T(8,128)(2,1)S(1)}, bf16[32,2048]{1,0:T(8,128)(2,1)S(1)}, u32[]{:S(2)}, u32[]{:S(2)}) collective-permute-start(bf16[32,2048]{1,0:T(8,128)(2,1)S(1)} %pad_maximum_fusion.4.refs_3_), channel_id=1, source_target_pairs={{0,16},{4,20},{8,24},{12,28},{16,0},{20,4},{24,8},{28,12},{1,17},{... | collective-permute-start | bytes 393224 | tf_op jit(solution)/shard_map/ppermute | solution.py:187
  17.1 7.9 %collective-permute-start.5 = (bf16[16,2048]{1,0:T(8,128)(2,1)S(1)}, bf16[16,2048]{1,0:T(8,128)(2,1)S(1)}, u32[]{:S(2)}, u32[]{:S(2)}) collective-permute-start(bf16[16,2048]{1,0:T(8,128)(2,1)S(1)} %shard_map.84), channel_id=1, source_target_pairs={{0,8},{4,12},{8,0},{12,4},{16,24},{20,28},{24,16},{28,20},{1,9},{5... | collective-permute-start | bytes 196616 | tf_op jit(solution)/shard_map/ppermute | solution.py:187
  25.0 5.2 %collective-permute-start.8 = (bf16[64,2048]{1,0:T(8,128)(2,1)S(1)}, bf16[64,2048]{1,0:T(8,128)(2,1)S(1)}, u32[]{:S(2)}, u32[]{:S(2)}) collective-permute-start(bf16[64,2048]{1,0:T(8,128)(2,1)S(1)} %pad_maximum_fusion.1.refs_0_), channel_id=1, source_target_pairs={{0,4},{4,0},{8,12},{12,8},{16,20},{20,16},{24,28},{28,24},{1,5},{5... | collective-permute-start | bytes 786440 | tf_op jit(solution)/shard_map/ppermute | solution.py:187
  25.1 11.7 %collective-permute-start.6 = (bf16[32,2048]{1,0:T(8,128)(2,1)S(1)}, bf16[32,2048]{1,0:T(8,128)(2,1)S(1)}, u32[]{:S(2)}, u32[]{:S(2)}) collective-permute-start(bf16[32,2048]{1,0:T(8,128)(2,1)S(1)} %pad_maximum_fusion.5.refs_3_), channel_id=1, source_target_pairs={{0,16},{4,20},{8,24},{12,28},{16,0},{20,4},{24,8},{28,12},{1,17},{... | collective-permute-start | bytes 393224 | tf_op jit(solution)/shard_map/ppermute | solution.py:187
  26.7 18.4 %collective-permute-start.4 = (bf16[2,2,16,4096]{3,2,1,0:T(8,128)(2,1)S(1)}, bf16[2,2,16,4096]{3,2,1,0:T(8,128)(2,1)S(1)}, u32[]{:S(2)}, u32[]{:S(2)}) collective-permute-start(bf16[2,2,16,4096]{3,2,1,0:T(8,128)(2,1)S(1)} %shard_map.86), channel_id=1, source_target_pairs={{0,1},{3,2},{4,5},{7,6},{8,9},{11,10},{12,13},{15,14},{16,17},{19,... | collective-permute-start | bytes 1572872 | tf_op jit(solution)/shard_map/ppermute | solution.py:268
  36.8 1.7 %collective-permute-start.9 = (bf16[64,2048]{1,0:T(8,128)(2,1)S(1)}, bf16[64,2048]{1,0:T(8,128)(2,1)S(1)}, u32[]{:S(2)}, u32[]{:S(2)}) collective-permute-start(bf16[64,2048]{1,0:T(8,128)(2,1)S(1)} %pad_maximum_fusion.2.refs_0_), channel_id=1, source_target_pairs={{0,4},{4,0},{8,12},{12,8},{16,20},{20,16},{24,28},{28,24},{1,5},{5... | collective-permute-start | bytes 786440 | tf_op jit(solution)/shard_map/ppermute | solution.py:187
  36.9 16.8 %collective-permute-start.11 = (bf16[2,2,16,4096]{3,2,1,0:T(8,128)(2,1)S(1)}, bf16[2,2,16,4096]{3,2,1,0:T(8,128)(2,1)S(1)}, u32[]{:S(2)}, u32[]{:S(2)}) collective-permute-start(bf16[2,2,16,4096]{3,2,1,0:T(8,128)(2,1)S(1)} %shard_map.88.refs_3_), channel_id=1, source_target_pairs={{0,1},{3,2},{4,5},{7,6},{8,9},{11,10},{12,13},{15,14},{16,17},{19,... | collective-permute-start | bytes 1572872 | tf_op jit(solution)/shard_map/ppermute | solution.py:268
  45.2 9.9 %collective-permute-start.10 = (bf16[2,2,16,4096]{3,2,1,0:T(8,128)(2,1)S(1)}, bf16[2,2,16,4096]{3,2,1,0:T(8,128)(2,1)S(1)}, u32[]{:S(2)}, u32[]{:S(2)}) collective-permute-start(bf16[2,2,16,4096]{3,2,1,0:T(8,128)(2,1)S(1)} %shard_map.91.refs_1_), channel_id=1, source_target_pairs={{1,2},{2,1},{5,6},{6,5},{9,10},{10,9},{13,14},{14,13},{17,18},{18,... | collective-permute-start | bytes 1572872 | tf_op jit(solution)/shard_map/ppermute | solution.py:268
  45.9 18.9 %collective-permute-start.14 = (bf16[2,2,16,4096]{3,2,1,0:T(8,128)(2,1)S(1)}, bf16[2,2,16,4096]{3,2,1,0:T(8,128)(2,1)S(1)}, u32[]{:S(2)}, u32[]{:S(2)}) collective-permute-start(bf16[2,2,16,4096]{3,2,1,0:T(8,128)(2,1)S(1)} %shard_map.90.refs_2_), channel_id=1, source_target_pairs={{0,1},{3,2},{4,5},{7,6},{8,9},{11,10},{12,13},{15,14},{16,17},{19,... | collective-permute-start | bytes 1572872 | tf_op jit(solution)/shard_map/ppermute | solution.py:268
  53.7 11.9 %collective-permute-start.15 = (bf16[1,2,16,4096]{3,2,1,0:T(8,128)(2,1)S(1)}, bf16[1,2,16,4096]{3,2,1,0:T(8,128)(2,1)S(1)}, u32[]{:S(2)}, u32[]{:S(2)}) collective-permute-start(bf16[1,2,16,4096]{3,2,1,0:T(8,128)(2,1)S(1)} %shard_map.92.refs_1_), channel_id=1, source_target_pairs={{1,2},{2,1},{5,6},{6,5},{9,10},{10,9},{13,14},{14,13},{17,18},{18,... | collective-permute-start | bytes 786440 | tf_op jit(solution)/shard_map/ppermute | solution.py:268
  54.5 17.4 %collective-permute-start.13 = (bf16[1,2,16,4096]{3,2,1,0:T(8,128)(2,1)S(1)}, bf16[1,2,16,4096]{3,2,1,0:T(8,128)(2,1)S(1)}, u32[]{:S(2)}, u32[]{:S(2)}) collective-permute-start(bf16[1,2,16,4096]{3,2,1,0:T(8,128)(2,1)S(1)} %shard_map.93.refs_1_), channel_id=1, source_target_pairs={{1,2},{2,1},{5,6},{6,5},{9,10},{10,9},{13,14},{14,13},{17,18},{18,... | collective-permute-start | bytes 786440 | tf_op jit(solution)/shard_map/ppermute | solution.py:268
  55.3 16.7 %collective-permute-start.12 = (bf16[1,2,16,4096]{3,2,1,0:T(8,128)(2,1)S(1)}, bf16[1,2,16,4096]{3,2,1,0:T(8,128)(2,1)S(1)}, u32[]{:S(2)}, u32[]{:S(2)}) collective-permute-start(bf16[1,2,16,4096]{3,2,1,0:T(8,128)(2,1)S(1)} %shard_map.94.refs_1_), channel_id=1, source_target_pairs={{0,1},{2,3},{1,0},{3,2},{4,5},{6,7},{5,4},{7,6},{8,9},{10,11},{9,8... | collective-permute-start | bytes 786440 | tf_op jit(solution)/shard_map/ppermute | solution.py:268
  64.9 7.2 %collective-permute-start.17 = (bf16[1,2,16,4096]{3,2,1,0:T(8,128)(2,1)S(1)}, bf16[1,2,16,4096]{3,2,1,0:T(8,128)(2,1)S(1)}, u32[]{:S(2)}, u32[]{:S(2)}) collective-permute-start(bf16[1,2,16,4096]{3,2,1,0:T(8,128)(2,1)S(1)} %shard_map.95.refs_1_), channel_id=1, source_target_pairs={{1,2},{2,1},{5,6},{6,5},{9,10},{10,9},{13,14},{14,13},{17,18},{18,... | collective-permute-start | bytes 786440 | tf_op jit(solution)/shard_map/ppermute | solution.py:268
  65.7 13.0 %collective-permute-start.16 = (bf16[1,2,16,4096]{3,2,1,0:T(8,128)(2,1)S(1)}, bf16[1,2,16,4096]{3,2,1,0:T(8,128)(2,1)S(1)}, u32[]{:S(2)}, u32[]{:S(2)}) collective-permute-start(bf16[1,2,16,4096]{3,2,1,0:T(8,128)(2,1)S(1)} %shard_map.96.refs_1_), channel_id=1, source_target_pairs={{0,1},{2,3},{1,0},{3,2},{4,5},{6,7},{5,4},{7,6},{8,9},{10,11},{9,8... | collective-permute-start | bytes 786440 | tf_op jit(solution)/shard_map/ppermute | solution.py:268
  71.2 7.6 %collective-permute-start.19 = (bf16[1,2,16,4096]{3,2,1,0:T(8,128)(2,1)S(1)}, bf16[1,2,16,4096]{3,2,1,0:T(8,128)(2,1)S(1)}, u32[]{:S(2)}, u32[]{:S(2)}) collective-permute-start(bf16[1,2,16,4096]{3,2,1,0:T(8,128)(2,1)S(1)} %shard_map.97.refs_2_), channel_id=1, source_target_pairs={{1,2},{2,1},{5,6},{6,5},{9,10},{10,9},{13,14},{14,13},{17,18},{18,... | collective-permute-start | bytes 786440 | tf_op jit(solution)/shard_map/ppermute | solution.py:268
  72.2 10.9 %collective-permute-start.18 = (bf16[1,2,16,4096]{3,2,1,0:T(8,128)(2,1)S(1)}, bf16[1,2,16,4096]{3,2,1,0:T(8,128)(2,1)S(1)}, u32[]{:S(2)}, u32[]{:S(2)}) collective-permute-start(bf16[1,2,16,4096]{3,2,1,0:T(8,128)(2,1)S(1)} %shard_map.101.refs_2_), channel_id=1, source_target_pairs={{0,1},{2,3},{1,0},{3,2},{4,5},{6,7},{5,4},{7,6},{8,9},{10,11},{9,8... | collective-permute-start | bytes 786440 | tf_op jit(solution)/shard_map/ppermute | solution.py:268

commit v4 on v3

--- a/solution.py
+++ b/solution.py
@@ -11,13 +11,16 @@
 BLOCK = 16
 CHUNK = 16
 LOWEST = -1e30
-SHORT = pl.CostEstimate(flops=0, bytes_accessed=0, transcendentals=0)
-
-
-def attend_kernel(first, rows, before, *refs):
+SHORT = pl.CostEstimate(flops=1, bytes_accessed=1, transcendentals=0)
+
+
+def attend_kernel(first, rows, columns, *refs):
     all_lengths, all_accepted, queries, new_keys, new_values, key_cache, value_cache, *refs = refs
-    *earlier, picked = refs[:-12]
-    lengths, accepted, q_buf, nk_buf, nv_buf, k_buf, v_buf, spread, mixed, small_sems, k_sems, v_sems = refs[-12:]
+    if columns is None:
+        picked, *scratch = refs
+    else:
+        weight, picked, held, *scratch, held_sem = refs
+    lengths, accepted, q_buf, nk_buf, nv_buf, k_buf, v_buf, spread, mixed, small_sems, k_sems, v_sems = scratch
     draft, _, query_cols = q_buf.shape
     cache_len, key_cols = k_buf.shape[1:]
     groups, heads = key_cols // HEAD_DIM, query_cols // HEAD_DIM
@@ -39,8 +42,9 @@
     for start in range(0, rows // CHUNK, BLOCK // CHUNK):
         for copy in keys[start : start + BLOCK // CHUNK] + values[start : start + BLOCK // CHUNK]:
             copy.start()
-    if before:
-        picked[:before, :] = earlier[0][...]
+    if columns is not None:
+        held_copy = pltpu.make_async_copy(weight.at[:, pl.ds(*columns)], held, held_sem)
+        held_copy.start()
     for copy in small:
         copy.wait()
     lanes = BLOCK * heads
@@ -103,28 +107,30 @@
                 kept = jnp.where(own_group == g, result[:, g * HEAD_DIM : (g + 1) * HEAD_DIM], kept)
             mixed[r] = kept
         for h in range(heads):
-            picked[pl.ds(before + block, BLOCK), pl.ds(h * HEAD_DIM, HEAD_DIM)] = mixed[:, h, :].astype(jnp.bfloat16)
-
-
-def attend(first, rows, arrays, earlier=None, after=None):
+            picked[here, pl.ds(h * HEAD_DIM, HEAD_DIM)] = mixed[:, h, :].astype(jnp.bfloat16)
+    if columns is not None:
+        held_copy.wait()
+
+
+def attend(first, rows, arrays, after=None, weight=None, columns=None):
     draft, _, query_cols = arrays[2].shape
     _, cache_len, key_cols = arrays[5].shape
     heads = query_cols // HEAD_DIM
     vmem, anywhere = pl.BlockSpec(memory_space=pltpu.VMEM), pl.BlockSpec(memory_space=pl.ANY)
-    cached = 2 * rows * cache_len * key_cols
-    before = 0 if earlier is None else earlier.shape[0]
-    extra = [] if earlier is None else [earlier]
     tokens = [] if after is None else [after]
+    given = [*arrays] if columns is None else [*arrays, weight]
+    shapes = [jax.ShapeDtypeStruct((rows, query_cols), jnp.bfloat16)]
+    if columns is not None:
+        shapes.append(pltpu.VMEM((weight.shape[0], columns[1]), jnp.bfloat16))
 
     def kernel(*refs):
-        given = 7 + len(extra)
-        attend_kernel(first, rows, before, *refs[:given], *refs[given + len(tokens) :])
+        attend_kernel(first, rows, columns, *refs[: len(given)], *refs[len(given) + len(tokens) :])
 
     return pl.pallas_call(
         kernel,
-        out_shape=jax.ShapeDtypeStruct((before + rows, query_cols), jnp.bfloat16),
-        in_specs=[anywhere] * 7 + [vmem] * len(extra) + [anywhere] * len(tokens),
-        out_specs=vmem,
+        out_shape=shapes,
+        in_specs=[anywhere] * (len(given) + len(tokens)),
+        out_specs=[vmem] * len(shapes),
         scratch_shapes=[
             pltpu.SMEM(arrays[0].shape, jnp.int32),
             pltpu.SMEM(arrays[1].shape, jnp.int32),
@@ -138,49 +144,63 @@
             pltpu.SemaphoreType.DMA((5,)),
             pltpu.SemaphoreType.DMA((rows // CHUNK,)),
             pltpu.SemaphoreType.DMA((rows // CHUNK,)),
-        ],
+        ]
+        + ([] if columns is None else [pltpu.SemaphoreType.DMA]),
         compiler_params=pltpu.CompilerParams(vmem_limit_bytes=8 << 20),
         cost_estimate=SHORT,
-    )(*[pltpu.with_memory_space_constraint(a, pltpu.HBM) for a in arrays], *extra, *tokens)
-
-
-def head_kernel(count, first, tile, *refs):
-    pieces, weight, (part, features, held, sems) = refs[:count], refs[count], refs[-4:]
-    copies = [
-        pltpu.make_async_copy(weight.at[:, pl.ds(first + at, tile)], held.at[n], sems.at[n])
-        for n, at in enumerate(range(0, part.shape[1], tile))
-    ]
-    for copy in copies:
-        copy.start()
+    )(*[pltpu.with_memory_space_constraint(a, pltpu.HBM) for a in given], *tokens)
+
+
+def head_kernel(count, columns, *refs):
+    pieces, refs = refs[:count], refs[count:]
+    if columns is None:
+        *weights, part, features = refs
+    else:
+        *weights, weight, part, held, features, held_sem = refs
+        held_copy = pltpu.make_async_copy(weight.at[:, pl.ds(*columns)], held, held_sem)
+        held_copy.start()
+        weights.append(held)
     at = 0
     for piece in pieces:
         features[pl.ds(at, piece.shape[0]), :] = piece[...]
         at += piece.shape[0]
-    for n, copy in enumerate(copies):
-        copy.wait()
-        product = jnp.dot(features[...], held[n], preferred_element_type=jnp.float32)
-        part[:, pl.ds(n * tile, tile)] = product.astype(jnp.bfloat16)
-
-
-def head(pieces, weight, first, cols, after=None):
-    tokens = [] if after is None else [after]
-    depth = weight.shape[0]
+    at = 0
+    for n, weight in enumerate(weights):
+        if columns is not None and n == len(weights) - 1:
+            held_copy.wait()
+        tile = min(512, weight.shape[1])
+        for start in range(0, weight.shape[1], tile):
+            product = jnp.dot(features[...], weight[:, pl.ds(start, tile)], preferred_element_type=jnp.float32)
+            part[:, pl.ds(at + start, tile)] = product.astype(jnp.bfloat16)
+        at += weight.shape[1]
+
+
+def head(pieces, weights, after, weight=None, columns=None):
+    depth = weights[0].shape[0]
     rows = sum(piece.shape[0] for piece in pieces)
-    tile = min(512, cols)
-    whole = pl.BlockSpec(memory_space=pltpu.VMEM)
+    cols = sum(weight.shape[1] for weight in weights) + (0 if columns is None else columns[1])
+    vmem, anywhere = pl.BlockSpec(memory_space=pltpu.VMEM), pl.BlockSpec(memory_space=pl.ANY)
+    given = [*pieces, *[pltpu.with_memory_space_constraint(weight, pltpu.VMEM) for weight in weights]]
+    specs = [vmem] * len(given)
+    shapes = [jax.ShapeDtypeStruct((rows, cols), jnp.bfloat16)]
+    if columns is not None:
+        given.append(pltpu.with_memory_space_constraint(weight, pltpu.HBM))
+        specs.append(anywhere)
+        shapes.append(pltpu.VMEM((depth, columns[1]), jnp.bfloat16))
+
+    def kernel(*refs):
+        head_kernel(len(pieces), columns, *refs[: len(given)], *refs[len(given) + 1 :])
+
     return pl.pallas_call(
-        functools.partial(head_kernel, len(pieces), first, tile),
-        out_shape=jax.ShapeDtypeStruct((rows, cols), jnp.bfloat16),
-        in_specs=[whole] * len(pieces) + [pl.BlockSpec(memory_space=pl.ANY)] * (1 + len(tokens)),
-        out_specs=whole,
-        scratch_shapes=[
-            pltpu.VMEM((rows, depth), jnp.bfloat16),
-            pltpu.VMEM((cols // tile, depth, tile), jnp.bfloat16),
-            pltpu.SemaphoreType.DMA((cols // tile,)),
-        ],
-        compiler_params=pltpu.CompilerParams(vmem_limit_bytes=28 << 20),
+        kernel,
+        out_shape=shapes,
+        in_specs=[*specs, anywhere],
+        out_specs=[vmem] * len(shapes),
+        scratch_shapes=[pltpu.VMEM((rows, depth), jnp.bfloat16)]
+        + ([] if columns is None else [pltpu.SemaphoreType.DMA]),
+        compiler_params=pltpu.CompilerParams(vmem_limit_bytes=8 << 20),
         cost_estimate=SHORT,
-    )(*pieces, pltpu.with_memory_space_constraint(weight, pltpu.HBM), *tokens)
+    )(*given, after)
 
 
 def swap(array, dp, bits):
@@ -201,15 +221,21 @@
     paired = dp == 8 and tensor == 4
     cols = head_weight.shape[1]
 
-    blocks, chips, pieces, last = [], {}, {}, None
-    for n in range(rows_dev // BLOCK):
-        blocks.append(attend(n * BLOCK, BLOCK, arrays, after=last))
-        last = blocks[n]
+    groups = rows_dev // BLOCK
+    share = cols // (groups + 1)
+    first, weight = attend(0, BLOCK, arrays, None, head_weight, (0, share))
+    blocks, weights, chips, pieces, last = [first], [weight], {}, {}, first
+    for n in range(1, groups):
         if paired:
-            chips[n] = swap(blocks[n], dp, 2)
+            chips[n - 1] = swap(blocks[n - 1], dp, 2)
+        block, weight = attend(n * BLOCK, BLOCK, arrays, last, head_weight, (n * share, share))
+        blocks.append(block)
+        weights.append(weight)
+        last = block
         if paired and n == 1:
-            chips[0] = jnp.concatenate([blocks[0], behind(chips[0], last)])
-            last = chips[0]
+            last = chips[0] = jnp.concatenate([first, behind(chips[0], block)])
+    if paired:
+        chips[groups - 1] = swap(blocks[-1], dp, 2)
 
     def along_y(n, after):
         chips[n] = jnp.concatenate([blocks[n], behind(chips[n], after)])
@@ -226,24 +252,28 @@
     def chosen(shard):
         return shard ^ (lax.axis_index("dp") // 2) if paired else shard
 
-    def add_kernel(steps, parity, places, part, *refs):
-        refs, sent = list(refs[:-1]), refs[-1]
+    def add_kernel(parity, sources, *refs):
+        *refs, sent = refs
         z = lax.axis_index("tensor")
-        for n, (step, place) in enumerate(zip(steps, places)):
+        for n, (part, step, arrived, place) in enumerate(sources):
             shard = jnp.where(lax.rem(z, 2) == parity, tensor - step + z, step - tensor + z)
             at = chosen(jnp.clip(shard, 0, tensor - 1))
-            if place is None:
-                sent[n] = part[:, at]
+            if arrived is None:
+                sent[n] = refs[part][:, at]
             else:
-                total = part[:, at].astype(jnp.float32) + refs.pop(0)[place].astype(jnp.float32)
+                total = refs[part][:, at].astype(jnp.float32) + refs[arrived][place].astype(jnp.float32)
                 sent[n] = total.astype(jnp.bfloat16)
 
-    def add(part, steps, parity, arrived, after):
-        shape = (len(steps), *part.shape[:1], *part.shape[2:])
+    def add(terms, parity, after):
+        part = terms[0][0]
+        shape = (len(terms), *part.shape[:1], *part.shape[2:])
         vmem = pl.BlockSpec(memory_space=pltpu.VMEM)
-        given = [part] + [array for array, _ in arrived if array is not None]
+        given, sources = [], []
+        for part, step, array, place in terms:
+            sources.append((len(given), step, None if array is None else len(given) + 1, place))
+            given += [part] if array is None else [part, array]
         return pl.pallas_call(
-            functools.partial(add_kernel, steps, parity, [place for _, place in arrived]),
+            lambda *refs: add_kernel(parity, sources, *refs[: len(given)], refs[-1]),
             out_shape=jax.ShapeDtypeStruct(shape, jnp.bfloat16),
             in_specs=[vmem] * len(given) + [pl.BlockSpec(memory_space=pl.ANY)],
             out_specs=vmem,
@@ -259,14 +289,19 @@
     parts, arrived, sums = {}, {}, {}
 
     def multiply(n, after):
-        parts[n] = view(head(pieces[n], head_weight, 0, cols, after))
+        if n == 0:
+            part, weight = head(pieces[n], weights, after, head_weight, (groups * share, cols - groups * share))
+            weights.append(weight)
+        else:
+            (part,) = head(pieces[n], weights, after)
+        parts[n] = view(part)
         return parts[n]
 
-    def send(n, steps, parity, after):
-        came = [arrived.get((n, step - 1, 1 - parity), (None, None)) for step in steps]
-        value = add(parts[n], steps, parity, came, after)
-        moved = lax.ppermute(value, "tensor", links(steps[0], parity))
-        for place, step in enumerate(steps):
+    def send(entries, parity, after):
+        terms = [(parts[n], step, *arrived.get((n, step - 1, 1 - parity), (None, None))) for n, step in entries]
+        value = add(terms, parity, after)
+        moved = lax.ppermute(value, "tensor", links(entries[0][1], parity))
+        for place, (n, step) in enumerate(entries):
             arrived[n, step, parity] = moved, place
         return value
 
@@ -325,19 +360,26 @@
 
     if paired:
         along_cores(0, last)
+        multiply(0, pieces[0][1])
+        last = send([(0, 1), (0, 2)], 0, parts[0])
         along_y(1, last)
-        multiply(0, chips[1])
-        last = send(0, (1, 2), 0, parts[0])
         along_cores(1, last)
         along_y(2, last)
-        last = multiply(1, chips[2])
-        last = send(1, (1, 2), 0, last)
+        last = multiply(1, last)
+        last = send([(1, 1), (1, 2)], 0, last)
+        last = send([(0, 2), (0, 3)], 1, last)
         along_cores(2, last)
         last = multiply(2, last)
-        order = [(2, (1, 2), 0), (0, (2, 3), 1), (1, (2,), 1), (1, (3,), 1), (0, (3,), 0), (2, (2,), 1), (1, (3,), 0)]
-        order += [(2, (3,), 1), (1, 1), (0, 0), (0, 1), (2, (3,), 0)]
-        for entry in order:
-            last = finish(*entry, last) if len(entry) == 2 else send(*entry, last)
+        last = send([(2, 1), (2, 2)], 0, last)
+        last = send([(1, 2)], 1, last)
+        last = send([(1, 3)], 1, last)
+        last = send([(0, 3), (1, 3)], 0, last)
+        last = send([(2, 2)], 1, last)
+        last = send([(2, 3)], 1, last)
+        last = finish(0, 1, last)
+        last = finish(1, 1, last)
+        last = send([(2, 3)], 0, last)
+        last = finish(0, 0, last)
         last = finish(1, 0, last)
     else:
         for n, block in enumerate(blocks):
@@ -347,7 +389,7 @@
             for n in range(len(blocks)):
                 for parity in range(2):
                     if links(step, parity):
-                        last = send(n, (step,), parity, last)
+                        last = send([(n, step)], parity, last)
 
     for n in range(len(parts) - 1):
         if n not in sums:

time: 84.7 us -> 80 us (0.945)
  Pallas kernels: 32.8 us -> 21.3 us
  starting transfers between devices: 41 us -> 45.5 us
  waiting for transfers between devices: 10.1 us -> 12.4 us
    pallas_call x17 -> x16, Pallas kernels: 31.3 us -> 19.8 us  [the longest x3 11.2 us: attend(): pl.pallas_call(kernel, out_shape=shapes, in_specs=[anywhere] * (len(given...]
    ppermute x9, waiting for transfers between devices: 0.03 us -> 6.08 us  [swap(): return lax.ppermute(array, 'dp', [(i, i ^ bits) for i in range(dp)])]
    ppermute x11 -> x10, starting transfers between devices: 32 us -> 37.2 us  [send(): moved = lax.ppermute(value, 'tensor', links(entries[0][1], parity))]
    ppermute x11 -> x10, waiting for transfers between devices: 10.1 us -> 6.31 us  [send(): moved = lax.ppermute(value, 'tensor', links(entries[0][1], parity))]
  transfers between devices with their start and end apart: 20 -> 19, of which waited for: 3 -> 7; matrix products, arithmetic and copies ran while one was open for 0% -> 0% of each run, Pallas kernels for 33% -> 20%
where the time goes in v4:
time: 80 us; the launch traced here: 79.7 us
  starting transfers between devices  45.5 us (57%)
  Pallas kernels  21.3 us (27%)
  waiting for transfers between devices  12.4 us (16%)
    ppermute x10, starting transfers between devices, send(): moved = lax.ppermute(value, 'tensor', links(entries[0][1], parity))  37.2 us
    pallas_call x3, Pallas kernels, attend(): pl.pallas_call(kernel, out_shape=shapes, in_specs=[anywhere] * (len(given...  11.2 us
    ppermute x9, starting transfers between devices, swap(): return lax.ppermute(array, 'dp', [(i, i ^ bits) for i in range(dp)])  8.31 us
    pallas_call x3, Pallas kernels, head(): pl.pallas_call(kernel, out_shape=shapes, in_specs=[*specs, anywhere], out...  7.76 us
    ppermute x10, waiting for transfers between devices, send(): moved = lax.ppermute(value, 'tensor', links(entries[0][1], parity))  6.31 us
    ppermute x9, waiting for transfers between devices, swap(): return lax.ppermute(array, 'dp', [(i, i ^ bits) for i in range(dp)])  6.08 us
  transfers between devices with their start and end apart: 19, of which 7 were waited for; matrix products, arithmetic and copies ran while one was open for 0% of the time, Pallas kernels for 20%

profile of v4, /device:TPU:0, one launch (start us, length us, event | category | flops | bytes accessed | tf_op | source)
XLA Modules:
  0.0 79.7 jit_solution(232899685551514569)
XLA Ops:
  0.0 3.7 %shard_map.82 = (bf16[16,2048]{1,0:T(8,128)(2,1)S(1)}, bf16[2048,1024]{1,0:T(8,128)(2,1)S(1)}) custom-call(s32[48]{0:T(128)} %refs_0_.5, s32[48]{0:T(128)} %refs_1_.5, bf16[5,48,2048]{2,1,0:T(8,128)(2,1)} %bitcast.28, bf16[5,48,256]{2,1,0:T(8,128)(2,1)} %bitcast.31, bf16[5,48,256]{2,1,0:T(8,128)(2,1)} %bitcast.34, bf16[48,256,256]{2,1,0:T(8,128)(2,1)} %refs_5_.6, ...), custom_call_target="tpu_custom_call" | custom-call | flops 1 | bytes 1 | tf_op jit(solution)/shard_map/pallas_call | solution.py:129
  3.7 3.0 %collective-permute-start = (bf16[16,2048]{1,0:T(8,128)(2,1)S(1)}, bf16[16,2048]{1,0:T(8,128)(2,1)S(1)}, u32[]{:S(2)}, u32[]{:S(2)}) collective-permute-start(bf16[16,2048]{1,0:T(8,128)(2,1)S(1)} %get-tuple-element.19.refs_8_), channel_id=1, source_target_pairs={{0,8},{4,12},{8,0},{12,4},{16,24},{20,28},{24,16},{28,20},{1,9},{5... | collective-permute-start | bytes 196616 | tf_op jit(solution)/shard_map/ppermute | solution.py:207
  6.7 3.8 %shard_map.83 = (bf16[16,2048]{1,0:T(8,128)(2,1)S(1)}, bf16[2048,1024]{1,0:T(8,128)(2,1)S(1)}) custom-call(s32[48]{0:T(128)} %refs_0_.5, s32[48]{0:T(128)} %refs_1_.5, bf16[5,48,2048]{2,1,0:T(8,128)(2,1)} %bitcast.29, bf16[5,48,256]{2,1,0:T(8,128)(2,1)} %bitcast.32, bf16[5,48,256]{2,1,0:T(8,128)(2,1)} %bitcast.35, bf16[48,256,256]{2,1,0:T(8,128)(2,1)} %refs_5_.6, ...), custom_call_target="tpu_custom_call" | custom-call | flops 1 | bytes 1 | tf_op jit(solution)/shard_map/pallas_call | solution.py:129
  10.5 0.0 collective-permute-done
  10.5 1.6 %collective-permute-start.1 = (bf16[32,2048]{1,0:T(8,128)(2,1)S(1)}, bf16[32,2048]{1,0:T(8,128)(2,1)S(1)}, u32[]{:S(2)}, u32[]{:S(2)}) collective-permute-start(bf16[32,2048]{1,0:T(8,128)(2,1)S(1)} %get-tuple-element.33.refs_8_), channel_id=1, source_target_pairs={{0,16},{4,20},{8,24},{12,28},{16,0},{20,4},{24,8},{28,12},{1,17},{... | collective-permute-start | bytes 393224 | tf_op jit(solution)/shard_map/ppermute | solution.py:207
  12.1 0.5 collective-permute-start.4
  12.7 3.7 %shard_map.84 = (bf16[16,2048]{1,0:T(8,128)(2,1)S(1)}, bf16[2048,1024]{1,0:T(8,128)(2,1)S(1)}) custom-call(s32[48]{0:T(128)} %refs_0_.5, s32[48]{0:T(128)} %refs_1_.5, bf16[5,48,2048]{2,1,0:T(8,128)(2,1)} %bitcast.30, bf16[5,48,256]{2,1,0:T(8,128)(2,1)} %bitcast.33, bf16[5,48,256]{2,1,0:T(8,128)(2,1)} %bitcast.36, bf16[48,256,256]{2,1,0:T(8,128)(2,1)} %refs_5_.6, ...), custom_call_target="tpu_custom_call" | custom-call | flops 1 | bytes 1 | tf_op jit(solution)/shard_map/pallas_call | solution.py:129
  16.4 0.0 collective-permute-done.1
  16.4 0.1 collective-permute-start.2
  16.5 1.6 %collective-permute-start.8 = (bf16[16,2048]{1,0:T(8,128)(2,1)S(1)}, bf16[16,2048]{1,0:T(8,128)(2,1)S(1)}, u32[]{:S(2)}, u32[]{:S(2)}) collective-permute-start(bf16[16,2048]{1,0:T(8,128)(2,1)S(1)} %get-tuple-element.22), channel_id=1, source_target_pairs={{0,8},{4,12},{8,0},{12,4},{16,24},{20,28},{24,16},{28,20},{1,9},{5... | collective-permute-start | bytes 196616 | tf_op jit(solution)/shard_map/ppermute | solution.py:207
  18.1 0.0 collective-permute-done.2.refs_1_.refs_6_
  18.1 3.0 %shard_map.85 = (bf16[128,4096]{1,0:T(8,128)(2,1)S(1)}, bf16[2048,1024]{1,0:T(8,128)(2,1)S(1)}) custom-call(bf16[64,2048]{1,0:T(8,128)(2,1)S(1)} %constant_dynamic-update-slice_fusion.2.refs_0_, bf16[64,2048]{1,0:T(8,128)(2,1)S(1)} %collective-permute-done.2.refs_1_.refs_6_, bf16[2048,1024]{1,0:T(8,128)(2,1)S(1)} %get-tuple-element.24.refs_2_, ...), custom_call_target="tpu_custom_call" | custom-call | flops 1 | bytes 1 | tf_op jit(solution)/shard_map/pallas_call | solution.py:194
  21.0 0.1 shard_map.86.refs_6_
  21.1 3.5 %collective-permute-start.3 = (bf16[2,2,16,4096]{3,2,1,0:T(8,128)(2,1)S(1)}, bf16[2,2,16,4096]{3,2,1,0:T(8,128)(2,1)S(1)}, u32[]{:S(2)}, u32[]{:S(2)}) collective-permute-start(bf16[2,2,16,4096]{3,2,1,0:T(8,128)(2,1)S(1)} %shard_map.86.refs_6_), channel_id=1, source_target_pairs={{0,1},{3,2},{4,5},{7,6},{8,9},{11,10},{12,13},{15,14},{16,17},{19,... | collective-permute-start | bytes 1572872 | tf_op jit(solution)/shard_map/ppermute | solution.py:303
  24.6 0.0 collective-permute-done.8
  24.6 0.0 collective-permute-done.4
  24.7 0.7 collective-permute-start.5
  25.4 4.6 %collective-permute-done.5 = bf16[32,2048]{1,0:T(8,128)(2,1)S(1)} collective-permute-done((bf16[32,2048]{1,0:T(8,128)(2,1)S(1)}, bf16[32,2048]{1,0:T(8,128)(2,1)S(1)}, u32[]{:S(2)}, u32[]{:S(2)}) %collective-permute-start.5) | collective-permute-done | bytes 131104 | tf_op jit(solution)/shard_map/ppermute | solution.py:207
  30.0 0.1 collective-permute-start.6
  30.1 0.7 collective-permute-start.9
  30.8 0.8 %collective-permute-done.6.refs_1_ = bf16[64,2048]{1,0:T(8,128)(2,1)S(1)} collective-permute-done((bf16[64,2048]{1,0:T(8,128)(2,1)S(1)}, bf16[64,2048]{1,0:T(8,128)(2,1)S(1)}, u32[]{:S(2)}, u32[]{:S(2)}) %collective-permute-start.6) | collective-permute-done | bytes 262176 | tf_op jit(solution)/shard_map/ppermute | solution.py:207
  31.6 2.4 %shard_map.87 = bf16[128,4096]{1,0:T(8,128)(2,1)S(1)} custom-call(bf16[64,2048]{1,0:T(8,128)(2,1)S(1)} %constant_dynamic-update-slice_fusion.5.refs_0_, bf16[64,2048]{1,0:T(8,128)(2,1)S(1)} %collective-permute-done.6.refs_1_, bf16[2048,1024]{1,0:T(8,128)(2,1)S(1)} %get-tuple-element.24.refs_2_, bf16[2048,1024]{1,0:T(8,128)(2,1)S(1)} %get-tuple-element.25.refs_3_, ...), custom_call_target="tpu_custom_call" | custom-call | flops 1 | bytes 1 | tf_op jit(solution)/shard_map/pallas_call | solution.py:194
  34.0 0.1 shard_map.88.refs_4_
  34.1 1.6 %collective-permute-start.12 = (bf16[2,2,16,4096]{3,2,1,0:T(8,128)(2,1)S(1)}, bf16[2,2,16,4096]{3,2,1,0:T(8,128)(2,1)S(1)}, u32[]{:S(2)}, u32[]{:S(2)}) collective-permute-start(bf16[2,2,16,4096]{3,2,1,0:T(8,128)(2,1)S(1)} %shard_map.88.refs_4_), channel_id=1, source_target_pairs={{0,1},{3,2},{4,5},{7,6},{8,9},{11,10},{12,13},{15,14},{16,17},{19,... | collective-permute-start | bytes 1572872 | tf_op jit(solution)/shard_map/ppermute | solution.py:303
  35.7 0.5 collective-permute-done.3.refs_1_.refs_3_
  36.2 0.1 shard_map.89.refs_6_
  36.3 0.0 collective-permute-done.9
  36.3 0.1 collective-permute-start.10
  36.4 0.9 %collective-permute-start.7 = (bf16[2,2,16,4096]{3,2,1,0:T(8,128)(2,1)S(1)}, bf16[2,2,16,4096]{3,2,1,0:T(8,128)(2,1)S(1)}, u32[]{:S(2)}, u32[]{:S(2)}) collective-permute-start(bf16[2,2,16,4096]{3,2,1,0:T(8,128)(2,1)S(1)} %shard_map.89.refs_6_), channel_id=1, source_target_pairs={{1,2},{2,1},{5,6},{6,5},{9,10},{10,9},{13,14},{14,13},{17,18},{18,... | collective-permute-start | bytes 1572872 | tf_op jit(solution)/shard_map/ppermute | solution.py:303
  37.3 0.6 collective-permute-done.10.refs_1_
  38.0 2.4 %shard_map.90 = bf16[128,4096]{1,0:T(8,128)(2,1)S(1)} custom-call(bf16[64,2048]{1,0:T(8,128)(2,1)S(1)} %constant_dynamic-update-slice_fusion.8.refs_0_, bf16[64,2048]{1,0:T(8,128)(2,1)S(1)} %collective-permute-done.10.refs_1_, bf16[2048,1024]{1,0:T(8,128)(2,1)S(1)} %get-tuple-element.24.refs_2_, bf16[2048,1024]{1,0:T(8,128)(2,1)S(1)} %get-tuple-element.25.refs_3_, ...), custom_call_target="tpu_custom_call" | custom-call | flops 1 | bytes 1 | tf_op jit(solution)/shard_map/pallas_call | solution.py:194
  40.4 0.1 shard_map.91.refs_2_
  40.4 6.6 %collective-permute-start.11 = (bf16[2,2,16,4096]{3,2,1,0:T(8,128)(2,1)S(1)}, bf16[2,2,16,4096]{3,2,1,0:T(8,128)(2,1)S(1)}, u32[]{:S(2)}, u32[]{:S(2)}) collective-permute-start(bf16[2,2,16,4096]{3,2,1,0:T(8,128)(2,1)S(1)} %shard_map.91.refs_2_), channel_id=1, source_target_pairs={{0,1},{3,2},{4,5},{7,6},{8,9},{11,10},{12,13},{15,14},{16,17},{19,... | collective-permute-start | bytes 1572872 | tf_op jit(solution)/shard_map/ppermute | solution.py:303
  47.0 0.3 collective-permute-done.12.refs_1_
  47.3 0.1 shard_map.92.refs_2_
  47.4 0.7 collective-permute-start.13
  48.1 0.1 shard_map.93.refs_4_
  48.2 0.7 collective-permute-start.16
  48.8 0.0 collective-permute-done.7.refs_1_
  48.9 0.0 collective-permute-done.13.refs_3_
  48.9 0.2 shard_map.94.refs_2_
  49.0 12.3 %collective-permute-start.14 = (bf16[2,2,16,4096]{3,2,1,0:T(8,128)(2,1)S(1)}, bf16[2,2,16,4096]{3,2,1,0:T(8,128)(2,1)S(1)}, u32[]{:S(2)}, u32[]{:S(2)}) collective-permute-start(bf16[2,2,16,4096]{3,2,1,0:T(8,128)(2,1)S(1)} %shard_map.94.refs_2_), channel_id=1, source_target_pairs={{0,1},{2,3},{1,0},{3,2},{4,5},{6,7},{5,4},{7,6},{8,9},{10,11},{9,8... | collective-permute-start | bytes 1572872 | tf_op jit(solution)/shard_map/ppermute | solution.py:303
  61.4 0.0 collective-permute-done.11.refs_1_
  61.4 0.1 shard_map.95.refs_2_
  61.4 0.7 collective-permute-start.15
  62.1 0.1 shard_map.96.refs_2_
  62.2 0.7 collective-permute-start.18
  62.9 0.1 shard_map.97.refs_2_.refs_0_
  63.0 0.0 collective-permute-done.16.refs_1_
  63.0 0.1 shard_map.98.refs_2_.refs_0_
  63.1 0.0 collective-permute-done.15.refs_1_
  63.1 0.1 shard_map.99.refs_2_
  63.2 9.6 %collective-permute-start.17 = (bf16[1,2,16,4096]{3,2,1,0:T(8,128)(2,1)S(1)}, bf16[1,2,16,4096]{3,2,1,0:T(8,128)(2,1)S(1)}, u32[]{:S(2)}, u32[]{:S(2)}) collective-permute-start(bf16[1,2,16,4096]{3,2,1,0:T(8,128)(2,1)S(1)} %shard_map.99.refs_2_), channel_id=1, source_target_pairs={{0,1},{2,3},{1,0},{3,2},{4,5},{6,7},{5,4},{7,6},{8,9},{10,11},{9,8... | collective-permute-start | bytes 786440 | tf_op jit(solution)/shard_map/ppermute | solution.py:303
  72.8 0.2 collective-permute-done.14.refs_1_
  73.1 0.0 collective-permute-done.18.refs_4_
  73.1 5.3 %collective-permute-done.17.refs_3_ = bf16[1,2,16,4096]{3,2,1,0:T(8,128)(2,1)S(1)} collective-permute-done((bf16[1,2,16,4096]{3,2,1,0:T(8,128)(2,1)S(1)}, bf16[1,2,16,4096]{3,2,1,0:T(8,128)(2,1)S(1)}, u32[]{:S(2)}, u32[]{:S(2)}) %collective-permute-start.17) | collective-permute-done | bytes 262176 | tf_op jit(solution)/shard_map/ppermute | solution.py:303
  78.4 1.3 %shard_map.102 = f32[2,48,4096]{2,1,0:T(8,128)} custom-call(f32[2,16,4096]{2,1,0:T(8,128)S(1)} %shard_map.100.refs_2_.refs_0_, f32[2,16,4096]{2,1,0:T(8,128)S(1)} %shard_map.101.refs_1_, bf16[2,4,16,4096]{3,2,1,0:T(8,128)(2,1)S(1)} %bitcast.20, bf16[1,2,16,4096]{3,2,1,0:T(8,128)(2,1)S(1)} %collective-permute-done.17.refs_3_, ...), custom_call_target="tpu_custom_call" | custom-call | flops 1 | bytes 1 | tf_op jit(solution)/shard_map/pallas_call | solution.py:351
  (13 shorter events, 0.2 us)
Async XLA Ops:
  3.7 6.8 %collective-permute-start = (bf16[16,2048]{1,0:T(8,128)(2,1)S(1)}, bf16[16,2048]{1,0:T(8,128)(2,1)S(1)}, u32[]{:S(2)}, u32[]{:S(2)}) collective-permute-start(bf16[16,2048]{1,0:T(8,128)(2,1)S(1)} %get-tuple-element.19.refs_8_), channel_id=1, source_target_pairs={{0,8},{4,12},{8,0},{12,4},{16,24},{20,28},{24,16},{28,20},{1,9},{5... | collective-permute-start | bytes 196616 | tf_op jit(solution)/shard_map/ppermute | solution.py:207
  10.5 5.8 %collective-permute-start.1 = (bf16[32,2048]{1,0:T(8,128)(2,1)S(1)}, bf16[32,2048]{1,0:T(8,128)(2,1)S(1)}, u32[]{:S(2)}, u32[]{:S(2)}) collective-permute-start(bf16[32,2048]{1,0:T(8,128)(2,1)S(1)} %get-tuple-element.33.refs_8_), channel_id=1, source_target_pairs={{0,16},{4,20},{8,24},{12,28},{16,0},{20,4},{24,8},{28,12},{1,17},{... | collective-permute-start | bytes 393224 | tf_op jit(solution)/shard_map/ppermute | solution.py:207
  12.1 12.5 %collective-permute-start.4 = (bf16[16,2048]{1,0:T(8,128)(2,1)S(1)}, bf16[16,2048]{1,0:T(8,128)(2,1)S(1)}, u32[]{:S(2)}, u32[]{:S(2)}) collective-permute-start(bf16[16,2048]{1,0:T(8,128)(2,1)S(1)} %get-tuple-element.20), channel_id=1, source_target_pairs={{0,8},{4,12},{8,0},{12,4},{16,24},{20,28},{24,16},{28,20},{1,9},{5... | collective-permute-start | bytes 196616 | tf_op jit(solution)/shard_map/ppermute | solution.py:207
  16.4 1.7 %collective-permute-start.2 = (bf16[64,2048]{1,0:T(8,128)(2,1)S(1)}, bf16[64,2048]{1,0:T(8,128)(2,1)S(1)}, u32[]{:S(2)}, u32[]{:S(2)}) collective-permute-start(bf16[64,2048]{1,0:T(8,128)(2,1)S(1)} %constant_dynamic-update-slice_fusion.2.refs_0_), channel_id=1, source_target_pairs={{0,4},{4,0},{8,12},{12,8},{16,20},{20,16},{24,28},{28,24},{1,5},{5... | collective-permute-start | bytes 786440 | tf_op jit(solution)/shard_map/ppermute | solution.py:207
  16.5 8.1 %collective-permute-start.8 = (bf16[16,2048]{1,0:T(8,128)(2,1)S(1)}, bf16[16,2048]{1,0:T(8,128)(2,1)S(1)}, u32[]{:S(2)}, u32[]{:S(2)}) collective-permute-start(bf16[16,2048]{1,0:T(8,128)(2,1)S(1)} %get-tuple-element.22), channel_id=1, source_target_pairs={{0,8},{4,12},{8,0},{12,4},{16,24},{20,28},{24,16},{28,20},{1,9},{5... | collective-permute-start | bytes 196616 | tf_op jit(solution)/shard_map/ppermute | solution.py:207
  21.1 15.1 %collective-permute-start.3 = (bf16[2,2,16,4096]{3,2,1,0:T(8,128)(2,1)S(1)}, bf16[2,2,16,4096]{3,2,1,0:T(8,128)(2,1)S(1)}, u32[]{:S(2)}, u32[]{:S(2)}) collective-permute-start(bf16[2,2,16,4096]{3,2,1,0:T(8,128)(2,1)S(1)} %shard_map.86.refs_6_), channel_id=1, source_target_pairs={{0,1},{3,2},{4,5},{7,6},{8,9},{11,10},{12,13},{15,14},{16,17},{19,... | collective-permute-start | bytes 1572872 | tf_op jit(solution)/shard_map/ppermute | solution.py:303
  24.7 5.3 %collective-permute-start.5 = (bf16[32,2048]{1,0:T(8,128)(2,1)S(1)}, bf16[32,2048]{1,0:T(8,128)(2,1)S(1)}, u32[]{:S(2)}, u32[]{:S(2)}) collective-permute-start(bf16[32,2048]{1,0:T(8,128)(2,1)S(1)} %pad_maximum_fusion), channel_id=1, source_target_pairs={{0,16},{4,20},{8,24},{12,28},{16,0},{20,4},{24,8},{28,12},{1,17},{... | collective-permute-start | bytes 393224 | tf_op jit(solution)/shard_map/ppermute | solution.py:207
  30.0 1.6 %collective-permute-start.6 = (bf16[64,2048]{1,0:T(8,128)(2,1)S(1)}, bf16[64,2048]{1,0:T(8,128)(2,1)S(1)}, u32[]{:S(2)}, u32[]{:S(2)}) collective-permute-start(bf16[64,2048]{1,0:T(8,128)(2,1)S(1)} %constant_dynamic-update-slice_fusion.5.refs_0_), channel_id=1, source_target_pairs={{0,4},{4,0},{8,12},{12,8},{16,20},{20,16},{24,28},{28,24},{1,5},{5... | collective-permute-start | bytes 786440 | tf_op jit(solution)/shard_map/ppermute | solution.py:207
  30.1 6.2 %collective-permute-start.9 = (bf16[32,2048]{1,0:T(8,128)(2,1)S(1)}, bf16[32,2048]{1,0:T(8,128)(2,1)S(1)}, u32[]{:S(2)}, u32[]{:S(2)}) collective-permute-start(bf16[32,2048]{1,0:T(8,128)(2,1)S(1)} %pad_maximum_fusion.1), channel_id=1, source_target_pairs={{0,16},{4,20},{8,24},{12,28},{16,0},{20,4},{24,8},{28,12},{1,17},{... | collective-permute-start | bytes 393224 | tf_op jit(solution)/shard_map/ppermute | solution.py:207
  34.1 13.2 %collective-permute-start.12 = (bf16[2,2,16,4096]{3,2,1,0:T(8,128)(2,1)S(1)}, bf16[2,2,16,4096]{3,2,1,0:T(8,128)(2,1)S(1)}, u32[]{:S(2)}, u32[]{:S(2)}) collective-permute-start(bf16[2,2,16,4096]{3,2,1,0:T(8,128)(2,1)S(1)} %shard_map.88.refs_4_), channel_id=1, source_target_pairs={{0,1},{3,2},{4,5},{7,6},{8,9},{11,10},{12,13},{15,14},{16,17},{19,... | collective-permute-start | bytes 1572872 | tf_op jit(solution)/shard_map/ppermute | solution.py:303
  36.3 1.6 %collective-permute-start.10 = (bf16[64,2048]{1,0:T(8,128)(2,1)S(1)}, bf16[64,2048]{1,0:T(8,128)(2,1)S(1)}, u32[]{:S(2)}, u32[]{:S(2)}) collective-permute-start(bf16[64,2048]{1,0:T(8,128)(2,1)S(1)} %constant_dynamic-update-slice_fusion.8.refs_0_), channel_id=1, source_target_pairs={{0,4},{4,0},{8,12},{12,8},{16,20},{20,16},{24,28},{28,24},{1,5},{5... | collective-permute-start | bytes 786440 | tf_op jit(solution)/shard_map/ppermute | solution.py:207
  36.4 12.4 %collective-permute-start.7 = (bf16[2,2,16,4096]{3,2,1,0:T(8,128)(2,1)S(1)}, bf16[2,2,16,4096]{3,2,1,0:T(8,128)(2,1)S(1)}, u32[]{:S(2)}, u32[]{:S(2)}) collective-permute-start(bf16[2,2,16,4096]{3,2,1,0:T(8,128)(2,1)S(1)} %shard_map.89.refs_6_), channel_id=1, source_target_pairs={{1,2},{2,1},{5,6},{6,5},{9,10},{10,9},{13,14},{14,13},{17,18},{18,... | collective-permute-start | bytes 1572872 | tf_op jit(solution)/shard_map/ppermute | solution.py:303
  40.4 20.9 %collective-permute-start.11 = (bf16[2,2,16,4096]{3,2,1,0:T(8,128)(2,1)S(1)}, bf16[2,2,16,4096]{3,2,1,0:T(8,128)(2,1)S(1)}, u32[]{:S(2)}, u32[]{:S(2)}) collective-permute-start(bf16[2,2,16,4096]{3,2,1,0:T(8,128)(2,1)S(1)} %shard_map.91.refs_2_), channel_id=1, source_target_pairs={{0,1},{3,2},{4,5},{7,6},{8,9},{11,10},{12,13},{15,14},{16,17},{19,... | collective-permute-start | bytes 1572872 | tf_op jit(solution)/shard_map/ppermute | solution.py:303
  47.4 1.5 %collective-permute-start.13 = (bf16[1,2,16,4096]{3,2,1,0:T(8,128)(2,1)S(1)}, bf16[1,2,16,4096]{3,2,1,0:T(8,128)(2,1)S(1)}, u32[]{:S(2)}, u32[]{:S(2)}) collective-permute-start(bf16[1,2,16,4096]{3,2,1,0:T(8,128)(2,1)S(1)} %shard_map.92.refs_2_), channel_id=1, source_target_pairs={{1,2},{2,1},{5,6},{6,5},{9,10},{10,9},{13,14},{14,13},{17,18},{18,... | collective-permute-start | bytes 786440 | tf_op jit(solution)/shard_map/ppermute | solution.py:303
  48.2 14.8 %collective-permute-start.16 = (bf16[1,2,16,4096]{3,2,1,0:T(8,128)(2,1)S(1)}, bf16[1,2,16,4096]{3,2,1,0:T(8,128)(2,1)S(1)}, u32[]{:S(2)}, u32[]{:S(2)}) collective-permute-start(bf16[1,2,16,4096]{3,2,1,0:T(8,128)(2,1)S(1)} %shard_map.93.refs_4_), channel_id=1, source_target_pairs={{1,2},{2,1},{5,6},{6,5},{9,10},{10,9},{13,14},{14,13},{17,18},{18,... | collective-permute-start | bytes 786440 | tf_op jit(solution)/shard_map/ppermute | solution.py:303
  49.0 24.0 %collective-permute-start.14 = (bf16[2,2,16,4096]{3,2,1,0:T(8,128)(2,1)S(1)}, bf16[2,2,16,4096]{3,2,1,0:T(8,128)(2,1)S(1)}, u32[]{:S(2)}, u32[]{:S(2)}) collective-permute-start(bf16[2,2,16,4096]{3,2,1,0:T(8,128)(2,1)S(1)} %shard_map.94.refs_2_), channel_id=1, source_target_pairs={{0,1},{2,3},{1,0},{3,2},{4,5},{6,7},{5,4},{7,6},{8,9},{10,11},{9,8... | collective-permute-start | bytes 1572872 | tf_op jit(solution)/shard_map/ppermute | solution.py:303
  61.4 1.6 %collective-permute-start.15 = (bf16[1,2,16,4096]{3,2,1,0:T(8,128)(2,1)S(1)}, bf16[1,2,16,4096]{3,2,1,0:T(8,128)(2,1)S(1)}, u32[]{:S(2)}, u32[]{:S(2)}) collective-permute-start(bf16[1,2,16,4096]{3,2,1,0:T(8,128)(2,1)S(1)} %shard_map.95.refs_2_), channel_id=1, source_target_pairs={{1,2},{2,1},{5,6},{6,5},{9,10},{10,9},{13,14},{14,13},{17,18},{18,... | collective-permute-start | bytes 786440 | tf_op jit(solution)/shard_map/ppermute | solution.py:303
  62.2 10.9 %collective-permute-start.18 = (bf16[1,2,16,4096]{3,2,1,0:T(8,128)(2,1)S(1)}, bf16[1,2,16,4096]{3,2,1,0:T(8,128)(2,1)S(1)}, u32[]{:S(2)}, u32[]{:S(2)}) collective-permute-start(bf16[1,2,16,4096]{3,2,1,0:T(8,128)(2,1)S(1)} %shard_map.96.refs_2_), channel_id=1, source_target_pairs={{1,2},{2,1},{5,6},{6,5},{9,10},{10,9},{13,14},{14,13},{17,18},{18,... | collective-permute-start | bytes 786440 | tf_op jit(solution)/shard_map/ppermute | solution.py:303
  63.2 15.2 %collective-permute-start.17 = (bf16[1,2,16,4096]{3,2,1,0:T(8,128)(2,1)S(1)}, bf16[1,2,16,4096]{3,2,1,0:T(8,128)(2,1)S(1)}, u32[]{:S(2)}, u32[]{:S(2)}) collective-permute-start(bf16[1,2,16,4096]{3,2,1,0:T(8,128)(2,1)S(1)} %shard_map.99.refs_2_), channel_id=1, source_target_pairs={{0,1},{2,3},{1,0},{3,2},{4,5},{6,7},{5,4},{7,6},{8,9},{10,11},{9,8... | collective-permute-start | bytes 786440 | tf_op jit(solution)/shard_map/ppermute | solution.py:303

commit v5 on v4

--- a/solution.py
+++ b/solution.py
@@ -12,6 +12,36 @@
 CHUNK = 16
 LOWEST = -1e30
 SHORT = pl.CostEstimate(flops=1, bytes_accessed=1, transcendentals=0)
+
+
+ORDER = [
+    ("cores", 0),
+    ("below", 1),
+    ("ends", 0),
+    ("send", [(0, 1), (0, 2)], 0),
+    ("between", 0),
+    ("beside", 2),
+    ("cores", 1),
+    ("below", 2),
+    ("head", 1),
+    ("send", [(1, 1), (1, 2)], 0),
+    ("send", [(0, 2), (0, 3)], 1),
+    ("cores", 2),
+    ("head", 2),
+    ("send", [(2, 1)], 0),
+    ("send", [(2, 2)], 0),
+    ("send", [(1, 2)], 1),
+    ("send", [(0, 3)], 0),
+    ("send", [(2, 2)], 1),
+    ("send", [(1, 3)], 0),
+    ("send", [(1, 3)], 1),
+    ("send", [(2, 3)], 1),
+    ("finish", 0, 1),
+    ("finish", 0, 0),
+    ("send", [(2, 3)], 0),
+    ("finish", 1, 1),
+    ("finish", 1, 0),
+]
 
 
 def attend_kernel(first, rows, columns, *refs):
@@ -151,53 +181,51 @@
     )(*[pltpu.with_memory_space_constraint(a, pltpu.HBM) for a in given], *tokens)
 
 
-def head_kernel(count, columns, *refs):
-    pieces, refs = refs[:count], refs[count:]
-    if columns is None:
-        *weights, part, features = refs
-    else:
-        *weights, weight, part, held, features, held_sem = refs
-        held_copy = pltpu.make_async_copy(weight.at[:, pl.ds(*columns)], held, held_sem)
-        held_copy.start()
-        weights.append(held)
+def multiply_pieces(pieces, weights, part, features):
     at = 0
     for piece in pieces:
         features[pl.ds(at, piece.shape[0]), :] = piece[...]
         at += piece.shape[0]
     at = 0
-    for n, weight in enumerate(weights):
-        if columns is not None and n == len(weights) - 1:
-            held_copy.wait()
-        tile = min(512, weight.shape[1])
-        for start in range(0, weight.shape[1], tile):
+    for weight in weights:
+        for start in range(0, weight.shape[1], 512):
+            tile = min(512, weight.shape[1] - start)
             product = jnp.dot(features[...], weight[:, pl.ds(start, tile)], preferred_element_type=jnp.float32)
             part[:, pl.ds(at + start, tile)] = product.astype(jnp.bfloat16)
         at += weight.shape[1]
 
 
-def head(pieces, weights, after, weight=None, columns=None):
+def head(pieces, weights, after, works=None, otherwise=None):
     depth = weights[0].shape[0]
     rows = sum(piece.shape[0] for piece in pieces)
-    cols = sum(weight.shape[1] for weight in weights) + (0 if columns is None else columns[1])
+    cols = sum(weight.shape[1] for weight in weights)
     vmem, anywhere = pl.BlockSpec(memory_space=pltpu.VMEM), pl.BlockSpec(memory_space=pl.ANY)
     given = [*pieces, *[pltpu.with_memory_space_constraint(weight, pltpu.VMEM) for weight in weights]]
-    specs = [vmem] * len(given)
-    shapes = [jax.ShapeDtypeStruct((rows, cols), jnp.bfloat16)]
-    if columns is not None:
-        given.append(pltpu.with_memory_space_constraint(weight, pltpu.HBM))
-        specs.append(anywhere)
-        shapes.append(pltpu.VMEM((depth, columns[1]), jnp.bfloat16))
+    given += [] if otherwise is None else [otherwise]
 
     def kernel(*refs):
-        head_kernel(len(pieces), columns, *refs[: len(given)], *refs[len(given) + 1 :])
+        sides = refs[len(pieces) : len(pieces) + len(weights)]
+        part, features = refs[-2:]
+        if works is None:
+            multiply_pieces(refs[: len(pieces)], sides, part, features)
+        else:
+
+            @pl.when(works())
+            def _():
+                multiply_pieces(refs[: len(pieces)], sides, part, features)
+
+            if otherwise is not None:
+
+                @pl.when(jnp.logical_not(works()))
+                def _():
+                    part[...] = refs[len(given) - 1][...]
 
     return pl.pallas_call(
         kernel,
-        out_shape=shapes,
-        in_specs=[*specs, anywhere],
-        out_specs=[vmem] * len(shapes),
-        scratch_shapes=[pltpu.VMEM((rows, depth), jnp.bfloat16)]
-        + ([] if columns is None else [pltpu.SemaphoreType.DMA]),
+        out_shape=jax.ShapeDtypeStruct((rows, cols), jnp.bfloat16),
+        in_specs=[vmem] * len(given) + [anywhere],
+        out_specs=vmem,
+        scratch_shapes=[pltpu.VMEM((rows, depth), jnp.bfloat16)],
         compiler_params=pltpu.CompilerParams(vmem_limit_bytes=8 << 20),
         cost_estimate=SHORT,
     )(*given, after)
@@ -222,20 +250,19 @@
     cols = head_weight.shape[1]
 
     groups = rows_dev // BLOCK
-    share = cols // (groups + 1)
-    first, weight = attend(0, BLOCK, arrays, None, head_weight, (0, share))
+    unit = cols // 8
+    columns = [(0, 2 * unit), (2 * unit, 3 * unit), (5 * unit, 3 * unit)]
+    first, weight = attend(0, BLOCK, arrays, None, head_weight, columns[0])
     blocks, weights, chips, pieces, last = [first], [weight], {}, {}, first
     for n in range(1, groups):
         if paired:
             chips[n - 1] = swap(blocks[n - 1], dp, 2)
-        block, weight = attend(n * BLOCK, BLOCK, arrays, last, head_weight, (n * share, share))
+        block, weight = attend(n * BLOCK, BLOCK, arrays, last, head_weight, columns[n])
         blocks.append(block)
         weights.append(weight)
         last = block
         if paired and n == 1:
             last = chips[0] = jnp.concatenate([first, behind(chips[0], block)])
-    if paired:
-        chips[groups - 1] = swap(blocks[-1], dp, 2)
 
     def along_y(n, after):
         chips[n] = jnp.concatenate([blocks[n], behind(chips[n], after)])
@@ -288,13 +315,11 @@
 
     parts, arrived, sums = {}, {}, {}
 
-    def multiply(n, after):
-        if n == 0:
-            part, weight = head(pieces[n], weights, after, head_weight, (groups * share, cols - groups * share))
-            weights.append(weight)
-        else:
-            (part,) = head(pieces[n], weights, after)
-        parts[n] = view(part)
+    def at_end():
+        return (lax.axis_index("tensor") == 0) | (lax.axis_index("tensor") == tensor - 1)
+
+    def multiply(n, after, works=None, otherwise=None):
+        parts[n] = view(head(pieces[n], weights, after, works, otherwise))
         return parts[n]
 
     def send(entries, parity, after):
@@ -359,28 +384,23 @@
         return out.reshape(-1, cols)
 
     if paired:
-        along_cores(0, last)
-        multiply(0, pieces[0][1])
-        last = send([(0, 1), (0, 2)], 0, parts[0])
-        along_y(1, last)
-        along_cores(1, last)
-        along_y(2, last)
-        last = multiply(1, last)
-        last = send([(1, 1), (1, 2)], 0, last)
-        last = send([(0, 2), (0, 3)], 1, last)
-        along_cores(2, last)
-        last = multiply(2, last)
-        last = send([(2, 1), (2, 2)], 0, last)
-        last = send([(1, 2)], 1, last)
-        last = send([(1, 3)], 1, last)
-        last = send([(0, 3), (1, 3)], 0, last)
-        last = send([(2, 2)], 1, last)
-        last = send([(2, 3)], 1, last)
-        last = finish(0, 1, last)
-        last = finish(1, 1, last)
-        last = send([(2, 3)], 0, last)
-        last = finish(0, 0, last)
-        last = finish(1, 0, last)
+        for step, *what in ORDER:
+            if step == "beside":
+                chips[what[0]] = swap(behind(blocks[what[0]], last), dp, 2)
+            elif step == "below":
+                along_y(what[0], last)
+            elif step == "cores":
+                along_cores(what[0], last)
+            elif step == "ends":
+                last = multiply(what[0], last, at_end)
+            elif step == "between":
+                last = multiply(what[0], last, lambda: ~at_end(), parts[what[0]].reshape(-1, cols))
+            elif step == "head":
+                last = multiply(what[0], last)
+            elif step == "send":
+                last = send(*what, last)
+            else:
+                last = finish(*what, last)
     else:
         for n, block in enumerate(blocks):
             pieces[n] = [lax.all_gather(block, "dp", axis=0, tiled=True)]

time: 80 us -> 78.6 us (0.982)
  starting transfers between devices: 45.5 us -> 38.7 us
  waiting for transfers between devices: 12.4 us -> 17.1 us
    ppermute x10 -> x12, starting transfers between devices: 37.2 us -> 30.5 us  [send(): moved = lax.ppermute(value, 'tensor', links(entries[0][1], parity))]
    ppermute x10 -> x12, waiting for transfers between devices: 6.31 us -> 12.2 us  [send(): moved = lax.ppermute(value, 'tensor', links(entries[0][1], parity))]
    pallas_call x3, Pallas kernels: 11.2 us -> 12.4 us  [attend(): pl.pallas_call(kernel, out_shape=shapes, in_specs=[anywhere] * (len(given...]
    ppermute x9, waiting for transfers between devices: 6.08 us -> 4.88 us  [swap(): return lax.ppermute(array, 'dp', [(i, i ^ bits) for i in range(dp)])]
    pallas_call x3 -> x4, Pallas kernels: 7.76 us -> 7.14 us  [head(): pl.pallas_call(kernel, out_shape=jax.ShapeDtypeStruct((rows, cols), jnp.b...]
  transfers between devices with their start and end apart: 19 -> 21, of which waited for: 7 -> 9; matrix products, arithmetic and copies ran while one was open for 0% -> 0% of each run, Pallas kernels for 20% -> 22%
where the time goes in v5:
time: 78.6 us; the launch traced here: 78.4 us
  starting transfers between devices  38.7 us (49%)
  Pallas kernels  22 us (28%)
  waiting for transfers between devices  17.1 us (22%)
    ppermute x12, starting transfers between devices, send(): moved = lax.ppermute(value, 'tensor', links(entries[0][1], parity))  30.5 us
    pallas_call x3, Pallas kernels, attend(): pl.pallas_call(kernel, out_shape=shapes, in_specs=[anywhere] * (len(given...  12.4 us
    ppermute x12, waiting for transfers between devices, send(): moved = lax.ppermute(value, 'tensor', links(entries[0][1], parity))  12.2 us
    ppermute x9, starting transfers between devices, swap(): return lax.ppermute(array, 'dp', [(i, i ^ bits) for i in range(dp)])  8.27 us
    pallas_call x4, Pallas kernels, head(): pl.pallas_call(kernel, out_shape=jax.ShapeDtypeStruct((rows, cols), jnp.b...  7.14 us
    ppermute x9, waiting for transfers between devices, swap(): return lax.ppermute(array, 'dp', [(i, i ^ bits) for i in range(dp)])  4.88 us
  transfers between devices with their start and end apart: 21, of which 9 were waited for; matrix products, arithmetic and copies ran while one was open for 0% of the time, Pallas kernels for 22%

profile of v5, /device:TPU:0, one launch (start us, length us, event | category | flops | bytes accessed | tf_op | source)
XLA Modules:
  0.0 78.4 jit_solution(6215040666569073255)
XLA Ops:
  0.0 3.7 %shard_map.82 = (bf16[16,2048]{1,0:T(8,128)(2,1)S(1)}, bf16[2048,1024]{1,0:T(8,128)(2,1)S(1)}) custom-call(s32[48]{0:T(128)} %refs_0_.5, s32[48]{0:T(128)} %refs_1_.5, bf16[5,48,2048]{2,1,0:T(8,128)(2,1)} %bitcast.30, bf16[5,48,256]{2,1,0:T(8,128)(2,1)} %bitcast.33, bf16[5,48,256]{2,1,0:T(8,128)(2,1)} %bitcast.36, bf16[48,256,256]{2,1,0:T(8,128)(2,1)} %refs_5_.5, ...), custom_call_target="tpu_custom_call" | custom-call | flops 1 | bytes 1 | tf_op jit(solution)/shard_map/pallas_call | solution.py:159
  3.7 3.0 %collective-permute-start = (bf16[16,2048]{1,0:T(8,128)(2,1)S(1)}, bf16[16,2048]{1,0:T(8,128)(2,1)S(1)}, u32[]{:S(2)}, u32[]{:S(2)}) collective-permute-start(bf16[16,2048]{1,0:T(8,128)(2,1)S(1)} %get-tuple-element.18.refs_8_), channel_id=1, source_target_pairs={{0,8},{4,12},{8,0},{12,4},{16,24},{20,28},{24,16},{28,20},{1,9},{5... | collective-permute-start | bytes 196616 | tf_op jit(solution)/shard_map/ppermute | solution.py:235
  6.7 4.5 %shard_map.83 = (bf16[16,2048]{1,0:T(8,128)(2,1)S(1)}, bf16[2048,1536]{1,0:T(8,128)(2,1)S(1)}) custom-call(s32[48]{0:T(128)} %refs_0_.5, s32[48]{0:T(128)} %refs_1_.5, bf16[5,48,2048]{2,1,0:T(8,128)(2,1)} %bitcast.31, bf16[5,48,256]{2,1,0:T(8,128)(2,1)} %bitcast.34, bf16[5,48,256]{2,1,0:T(8,128)(2,1)} %bitcast.37, bf16[48,256,256]{2,1,0:T(8,128)(2,1)} %refs_5_.5, ...), custom_call_target="tpu_custom_call" | custom-call | flops 1 | bytes 1 | tf_op jit(solution)/shard_map/pallas_call | solution.py:159
  11.2 0.1 collective-permute-start.4
  11.3 0.0 collective-permute-done
  11.3 2.1 %collective-permute-start.1 = (bf16[32,2048]{1,0:T(8,128)(2,1)S(1)}, bf16[32,2048]{1,0:T(8,128)(2,1)S(1)}, u32[]{:S(2)}, u32[]{:S(2)}) collective-permute-start(bf16[32,2048]{1,0:T(8,128)(2,1)S(1)} %get-tuple-element.31.refs_8_), channel_id=1, source_target_pairs={{0,16},{4,20},{8,24},{12,28},{16,0},{20,4},{24,8},{28,12},{1,17},{... | collective-permute-start | bytes 393224 | tf_op jit(solution)/shard_map/ppermute | solution.py:235
  13.4 4.3 %shard_map.84 = (bf16[16,2048]{1,0:T(8,128)(2,1)S(1)}, bf16[2048,1536]{1,0:T(8,128)(2,1)S(1)}) custom-call(s32[48]{0:T(128)} %refs_0_.5, s32[48]{0:T(128)} %refs_1_.5, bf16[5,48,2048]{2,1,0:T(8,128)(2,1)} %bitcast.32, bf16[5,48,256]{2,1,0:T(8,128)(2,1)} %bitcast.35, bf16[5,48,256]{2,1,0:T(8,128)(2,1)} %bitcast.38, bf16[48,256,256]{2,1,0:T(8,128)(2,1)} %refs_5_.5, ...), custom_call_target="tpu_custom_call" | custom-call | flops 1 | bytes 1 | tf_op jit(solution)/shard_map/pallas_call | solution.py:159
  17.7 0.0 collective-permute-done.4
  17.7 0.0 collective-permute-done.1
  17.8 0.1 collective-permute-start.2
  17.9 0.7 collective-permute-start.5
  18.6 0.8 %collective-permute-done.2.refs_1_ = bf16[64,2048]{1,0:T(8,128)(2,1)S(1)} collective-permute-done((bf16[64,2048]{1,0:T(8,128)(2,1)S(1)}, bf16[64,2048]{1,0:T(8,128)(2,1)S(1)}, u32[]{:S(2)}, u32[]{:S(2)}) %collective-permute-start.2) | collective-permute-done | bytes 262176 | tf_op jit(solution)/shard_map/ppermute | solution.py:235
  19.4 2.3 %shard_map.85.refs_5_ = bf16[128,4096]{1,0:T(8,128)(2,1)S(1)} custom-call(bf16[64,2048]{1,0:T(8,128)(2,1)S(1)} %constant_dynamic-update-slice_fusion.2.refs_0_, bf16[64,2048]{1,0:T(8,128)(2,1)S(1)} %collective-permute-done.2.refs_1_, bf16[2048,1024]{1,0:T(8,128)(2,1)S(1)} %get-tuple-element.23.refs_2_, bf16[2048,1536]{1,0:T(8,128)(2,1)S(1)} %get-tuple-element.24.refs_3_, ...), custom_call_target="tpu_custom_call" | custom-call | flops 1 | bytes 1 | tf_op jit(solution)/shard_map/pallas_call | solution.py:223
  21.7 0.1 shard_map.86.refs_6_
  21.8 1.3 %collective-permute-start.3 = (bf16[2,2,16,4096]{3,2,1,0:T(8,128)(2,1)S(1)}, bf16[2,2,16,4096]{3,2,1,0:T(8,128)(2,1)S(1)}, u32[]{:S(2)}, u32[]{:S(2)}) collective-permute-start(bf16[2,2,16,4096]{3,2,1,0:T(8,128)(2,1)S(1)} %shard_map.86.refs_6_), channel_id=1, source_target_pairs={{0,1},{3,2},{4,5},{7,6},{8,9},{11,10},{12,13},{15,14},{16,17},{19,... | collective-permute-start | bytes 1572872 | tf_op jit(solution)/shard_map/ppermute | solution.py:328
  23.1 0.1 shard_map.87
  23.2 0.6 collective-permute-done.5
  23.8 1.5 %collective-permute-start.8 = (bf16[16,2048]{1,0:T(8,128)(2,1)S(1)}, bf16[16,2048]{1,0:T(8,128)(2,1)S(1)}, u32[]{:S(2)}, u32[]{:S(2)}) collective-permute-start(bf16[16,2048]{1,0:T(8,128)(2,1)S(1)} %get-tuple-element.28.refs_5_), channel_id=1, source_target_pairs={{0,8},{4,12},{8,0},{12,4},{16,24},{20,28},{24,16},{28,20},{1,9},{5... | collective-permute-start | bytes 196616 | tf_op jit(solution)/shard_map/ppermute | solution.py:235
  25.3 0.1 collective-permute-start.6
  25.3 2.7 %collective-permute-done.8 = bf16[16,2048]{1,0:T(8,128)(2,1)S(1)} collective-permute-done((bf16[16,2048]{1,0:T(8,128)(2,1)S(1)}, bf16[16,2048]{1,0:T(8,128)(2,1)S(1)}, u32[]{:S(2)}, u32[]{:S(2)}) %collective-permute-start.8) | collective-permute-done | bytes 65568 | tf_op jit(solution)/shard_map/ppermute | solution.py:235
  28.0 0.7 collective-permute-start.9
  28.7 0.0 collective-permute-done.6.refs_1_
  28.7 2.4 %shard_map.88 = bf16[128,4096]{1,0:T(8,128)(2,1)S(1)} custom-call(bf16[64,2048]{1,0:T(8,128)(2,1)S(1)} %constant_dynamic-update-slice_fusion.5.refs_0_, bf16[64,2048]{1,0:T(8,128)(2,1)S(1)} %collective-permute-done.6.refs_1_, bf16[2048,1024]{1,0:T(8,128)(2,1)S(1)} %get-tuple-element.23.refs_2_, bf16[2048,1536]{1,0:T(8,128)(2,1)S(1)} %get-tuple-element.24.refs_3_, ...), custom_call_target="tpu_custom_call" | custom-call | flops 1 | bytes 1 | tf_op jit(solution)/shard_map/pallas_call | solution.py:223
  31.1 0.1 shard_map.89.refs_4_
  31.2 3.5 %collective-permute-start.12 = (bf16[2,2,16,4096]{3,2,1,0:T(8,128)(2,1)S(1)}, bf16[2,2,16,4096]{3,2,1,0:T(8,128)(2,1)S(1)}, u32[]{:S(2)}, u32[]{:S(2)}) collective-permute-start(bf16[2,2,16,4096]{3,2,1,0:T(8,128)(2,1)S(1)} %shard_map.89.refs_4_), channel_id=1, source_target_pairs={{0,1},{3,2},{4,5},{7,6},{8,9},{11,10},{12,13},{15,14},{16,17},{19,... | collective-permute-start | bytes 1572872 | tf_op jit(solution)/shard_map/ppermute | solution.py:328
  34.7 0.6 collective-permute-done.3.refs_1_.refs_3_
  35.3 0.1 shard_map.90.refs_5_
  35.5 0.0 collective-permute-done.9
  35.5 0.1 collective-permute-start.10
  35.6 0.7 collective-permute-start.7
  36.3 0.8 %collective-permute-done.10.refs_1_ = bf16[64,2048]{1,0:T(8,128)(2,1)S(1)} collective-permute-done((bf16[64,2048]{1,0:T(8,128)(2,1)S(1)}, bf16[64,2048]{1,0:T(8,128)(2,1)S(1)}, u32[]{:S(2)}, u32[]{:S(2)}) %collective-permute-start.10) | collective-permute-done | bytes 262176 | tf_op jit(solution)/shard_map/ppermute | solution.py:235
  37.1 2.4 %shard_map.91 = bf16[128,4096]{1,0:T(8,128)(2,1)S(1)} custom-call(bf16[64,2048]{1,0:T(8,128)(2,1)S(1)} %constant_dynamic-update-slice_fusion.8.refs_0_, bf16[64,2048]{1,0:T(8,128)(2,1)S(1)} %collective-permute-done.10.refs_1_, bf16[2048,1024]{1,0:T(8,128)(2,1)S(1)} %get-tuple-element.23.refs_2_, bf16[2048,1536]{1,0:T(8,128)(2,1)S(1)} %get-tuple-element.24.refs_3_, ...), custom_call_target="tpu_custom_call" | custom-call | flops 1 | bytes 1 | tf_op jit(solution)/shard_map/pallas_call | solution.py:223
  39.5 7.5 %collective-permute-start.14 = (bf16[1,2,16,4096]{3,2,1,0:T(8,128)(2,1)S(1)}, bf16[1,2,16,4096]{3,2,1,0:T(8,128)(2,1)S(1)}, u32[]{:S(2)}, u32[]{:S(2)}) collective-permute-start(bf16[1,2,16,4096]{3,2,1,0:T(8,128)(2,1)S(1)} %shard_map.92.refs_1_), channel_id=1, source_target_pairs={{0,1},{3,2},{4,5},{7,6},{8,9},{11,10},{12,13},{15,14},{16,17},{19,... | collective-permute-start | bytes 786440 | tf_op jit(solution)/shard_map/ppermute | solution.py:328
  47.1 0.0 collective-permute-done.12.refs_1_
  47.1 0.1 shard_map.94.refs_2_
  47.2 0.7 collective-permute-start.13
  47.8 7.8 %collective-permute-start.11 = (bf16[1,2,16,4096]{3,2,1,0:T(8,128)(2,1)S(1)}, bf16[1,2,16,4096]{3,2,1,0:T(8,128)(2,1)S(1)}, u32[]{:S(2)}, u32[]{:S(2)}) collective-permute-start(bf16[1,2,16,4096]{3,2,1,0:T(8,128)(2,1)S(1)} %shard_map.93.refs_2_), channel_id=1, source_target_pairs={{0,1},{3,2},{4,5},{7,6},{8,9},{11,10},{12,13},{15,14},{16,17},{19,... | collective-permute-start | bytes 786440 | tf_op jit(solution)/shard_map/ppermute | solution.py:328
  55.7 0.0 collective-permute-done.7.refs_1_
  55.7 0.1 shard_map.95.refs_2_
  55.8 0.1 collective-permute-start.15
  55.8 0.0 collective-permute-done.14.refs_1_
  55.9 0.1 shard_map.96.refs_2_
  55.9 0.7 collective-permute-start.17
  56.6 0.0 collective-permute-done.13.refs_1_
  56.6 0.1 shard_map.97.refs_2_
  56.7 4.3 %collective-permute-start.18 = (bf16[1,2,16,4096]{3,2,1,0:T(8,128)(2,1)S(1)}, bf16[1,2,16,4096]{3,2,1,0:T(8,128)(2,1)S(1)}, u32[]{:S(2)}, u32[]{:S(2)}) collective-permute-start(bf16[1,2,16,4096]{3,2,1,0:T(8,128)(2,1)S(1)} %shard_map.97.refs_2_), channel_id=1, source_target_pairs={{0,1},{2,3},{1,0},{3,2},{4,5},{6,7},{5,4},{7,6},{8,9},{10,11},{9,8... | collective-permute-start | bytes 786440 | tf_op jit(solution)/shard_map/ppermute | solution.py:328
  61.0 0.1 shard_map.98.refs_2_
  61.1 0.7 collective-permute-start.16
  61.8 0.6 collective-permute-done.11.refs_1_
  62.4 0.1 shard_map.99.refs_2_
  62.5 0.7 collective-permute-start.20
  63.2 0.1 shard_map.100.refs_0_.refs_2_
  63.2 4.8 %collective-permute-done.15.refs_1_ = bf16[1,2,16,4096]{3,2,1,0:T(8,128)(2,1)S(1)} collective-permute-done((bf16[1,2,16,4096]{3,2,1,0:T(8,128)(2,1)S(1)}, bf16[1,2,16,4096]{3,2,1,0:T(8,128)(2,1)S(1)}, u32[]{:S(2)}, u32[]{:S(2)}) %collective-permute-start.15) | collective-permute-done | bytes 262176 | tf_op jit(solution)/shard_map/ppermute | solution.py:328
  68.1 0.0 collective-permute-done.17.refs_1_
  68.1 0.1 shard_map.102.refs_2_
  68.2 2.5 %collective-permute-start.19 = (bf16[1,2,16,4096]{3,2,1,0:T(8,128)(2,1)S(1)}, bf16[1,2,16,4096]{3,2,1,0:T(8,128)(2,1)S(1)}, u32[]{:S(2)}, u32[]{:S(2)}) collective-permute-start(bf16[1,2,16,4096]{3,2,1,0:T(8,128)(2,1)S(1)} %shard_map.102.refs_2_), channel_id=1, source_target_pairs={{0,1},{2,3},{1,0},{3,2},{4,5},{6,7},{5,4},{7,6},{8,9},{10,11},{9,8... | collective-permute-start | bytes 786440 | tf_op jit(solution)/shard_map/ppermute | solution.py:328
  70.7 0.0 collective-permute-done.16.refs_1_
  70.7 0.1 shard_map.103.refs_0_.refs_2_
  70.8 2.8 %collective-permute-done.18.refs_1_ = bf16[1,2,16,4096]{3,2,1,0:T(8,128)(2,1)S(1)} collective-permute-done((bf16[1,2,16,4096]{3,2,1,0:T(8,128)(2,1)S(1)}, bf16[1,2,16,4096]{3,2,1,0:T(8,128)(2,1)S(1)}, u32[]{:S(2)}, u32[]{:S(2)}) %collective-permute-start.18) | collective-permute-done | bytes 262176 | tf_op jit(solution)/shard_map/ppermute | solution.py:328
  73.7 0.0 collective-permute-done.20.refs_4_
  73.7 3.4 %collective-permute-done.19.refs_3_ = bf16[1,2,16,4096]{3,2,1,0:T(8,128)(2,1)S(1)} collective-permute-done((bf16[1,2,16,4096]{3,2,1,0:T(8,128)(2,1)S(1)}, bf16[1,2,16,4096]{3,2,1,0:T(8,128)(2,1)S(1)}, u32[]{:S(2)}, u32[]{:S(2)}) %collective-permute-start.19) | collective-permute-done | bytes 262176 | tf_op jit(solution)/shard_map/ppermute | solution.py:328
  77.1 1.3 %shard_map.105 = f32[2,48,4096]{2,1,0:T(8,128)} custom-call(f32[2,16,4096]{2,1,0:T(8,128)S(1)} %shard_map.101.refs_2_.refs_0_, f32[2,16,4096]{2,1,0:T(8,128)S(1)} %shard_map.104.refs_1_, bf16[2,4,16,4096]{3,2,1,0:T(8,128)(2,1)S(1)} %bitcast.21, bf16[1,2,16,4096]{3,2,1,0:T(8,128)(2,1)S(1)} %collective-permute-done.19.refs_3_, ...), custom_call_target="tpu_custom_call" | custom-call | flops 1 | bytes 1 | tf_op jit(solution)/shard_map/pallas_call | solution.py:376
  (15 shorter events, 0.3 us)
Async XLA Ops:
  3.7 7.6 %collective-permute-start = (bf16[16,2048]{1,0:T(8,128)(2,1)S(1)}, bf16[16,2048]{1,0:T(8,128)(2,1)S(1)}, u32[]{:S(2)}, u32[]{:S(2)}) collective-permute-start(bf16[16,2048]{1,0:T(8,128)(2,1)S(1)} %get-tuple-element.18.refs_8_), channel_id=1, source_target_pairs={{0,8},{4,12},{8,0},{12,4},{16,24},{20,28},{24,16},{28,20},{1,9},{5... | collective-permute-start | bytes 196616 | tf_op jit(solution)/shard_map/ppermute | solution.py:235
  11.2 6.5 %collective-permute-start.4 = (bf16[16,2048]{1,0:T(8,128)(2,1)S(1)}, bf16[16,2048]{1,0:T(8,128)(2,1)S(1)}, u32[]{:S(2)}, u32[]{:S(2)}) collective-permute-start(bf16[16,2048]{1,0:T(8,128)(2,1)S(1)} %get-tuple-element.19), channel_id=1, source_target_pairs={{0,8},{4,12},{8,0},{12,4},{16,24},{20,28},{24,16},{28,20},{1,9},{5... | collective-permute-start | bytes 196616 | tf_op jit(solution)/shard_map/ppermute | solution.py:235
  11.3 6.4 %collective-permute-start.1 = (bf16[32,2048]{1,0:T(8,128)(2,1)S(1)}, bf16[32,2048]{1,0:T(8,128)(2,1)S(1)}, u32[]{:S(2)}, u32[]{:S(2)}) collective-permute-start(bf16[32,2048]{1,0:T(8,128)(2,1)S(1)} %get-tuple-element.31.refs_8_), channel_id=1, source_target_pairs={{0,16},{4,20},{8,24},{12,28},{16,0},{20,4},{24,8},{28,12},{1,17},{... | collective-permute-start | bytes 393224 | tf_op jit(solution)/shard_map/ppermute | solution.py:235
  17.8 1.6 %collective-permute-start.2 = (bf16[64,2048]{1,0:T(8,128)(2,1)S(1)}, bf16[64,2048]{1,0:T(8,128)(2,1)S(1)}, u32[]{:S(2)}, u32[]{:S(2)}) collective-permute-start(bf16[64,2048]{1,0:T(8,128)(2,1)S(1)} %constant_dynamic-update-slice_fusion.2.refs_0_), channel_id=1, source_target_pairs={{0,4},{4,0},{8,12},{12,8},{16,20},{20,16},{24,28},{28,24},{1,5},{5... | collective-permute-start | bytes 786440 | tf_op jit(solution)/shard_map/ppermute | solution.py:235
  17.9 5.9 %collective-permute-start.5 = (bf16[32,2048]{1,0:T(8,128)(2,1)S(1)}, bf16[32,2048]{1,0:T(8,128)(2,1)S(1)}, u32[]{:S(2)}, u32[]{:S(2)}) collective-permute-start(bf16[32,2048]{1,0:T(8,128)(2,1)S(1)} %pad_maximum_fusion), channel_id=1, source_target_pairs={{0,16},{4,20},{8,24},{12,28},{16,0},{20,4},{24,8},{28,12},{1,17},{... | collective-permute-start | bytes 393224 | tf_op jit(solution)/shard_map/ppermute | solution.py:235
  21.8 13.5 %collective-permute-start.3 = (bf16[2,2,16,4096]{3,2,1,0:T(8,128)(2,1)S(1)}, bf16[2,2,16,4096]{3,2,1,0:T(8,128)(2,1)S(1)}, u32[]{:S(2)}, u32[]{:S(2)}) collective-permute-start(bf16[2,2,16,4096]{3,2,1,0:T(8,128)(2,1)S(1)} %shard_map.86.refs_6_), channel_id=1, source_target_pairs={{0,1},{3,2},{4,5},{7,6},{8,9},{11,10},{12,13},{15,14},{16,17},{19,... | collective-permute-start | bytes 1572872 | tf_op jit(solution)/shard_map/ppermute | solution.py:328
  23.8 4.3 %collective-permute-start.8 = (bf16[16,2048]{1,0:T(8,128)(2,1)S(1)}, bf16[16,2048]{1,0:T(8,128)(2,1)S(1)}, u32[]{:S(2)}, u32[]{:S(2)}) collective-permute-start(bf16[16,2048]{1,0:T(8,128)(2,1)S(1)} %get-tuple-element.28.refs_5_), channel_id=1, source_target_pairs={{0,8},{4,12},{8,0},{12,4},{16,24},{20,28},{24,16},{28,20},{1,9},{5... | collective-permute-start | bytes 196616 | tf_op jit(solution)/shard_map/ppermute | solution.py:235
  25.3 3.5 %collective-permute-start.6 = (bf16[64,2048]{1,0:T(8,128)(2,1)S(1)}, bf16[64,2048]{1,0:T(8,128)(2,1)S(1)}, u32[]{:S(2)}, u32[]{:S(2)}) collective-permute-start(bf16[64,2048]{1,0:T(8,128)(2,1)S(1)} %constant_dynamic-update-slice_fusion.5.refs_0_), channel_id=1, source_target_pairs={{0,4},{4,0},{8,12},{12,8},{16,20},{20,16},{24,28},{28,24},{1,5},{5... | collective-permute-start | bytes 786440 | tf_op jit(solution)/shard_map/ppermute | solution.py:235
  28.0 7.4 %collective-permute-start.9 = (bf16[32,2048]{1,0:T(8,128)(2,1)S(1)}, bf16[32,2048]{1,0:T(8,128)(2,1)S(1)}, u32[]{:S(2)}, u32[]{:S(2)}) collective-permute-start(bf16[32,2048]{1,0:T(8,128)(2,1)S(1)} %pad_maximum_fusion.1), channel_id=1, source_target_pairs={{0,16},{4,20},{8,24},{12,28},{16,0},{20,4},{24,8},{28,12},{1,17},{... | collective-permute-start | bytes 393224 | tf_op jit(solution)/shard_map/ppermute | solution.py:235
  31.2 15.9 %collective-permute-start.12 = (bf16[2,2,16,4096]{3,2,1,0:T(8,128)(2,1)S(1)}, bf16[2,2,16,4096]{3,2,1,0:T(8,128)(2,1)S(1)}, u32[]{:S(2)}, u32[]{:S(2)}) collective-permute-start(bf16[2,2,16,4096]{3,2,1,0:T(8,128)(2,1)S(1)} %shard_map.89.refs_4_), channel_id=1, source_target_pairs={{0,1},{3,2},{4,5},{7,6},{8,9},{11,10},{12,13},{15,14},{16,17},{19,... | collective-permute-start | bytes 1572872 | tf_op jit(solution)/shard_map/ppermute | solution.py:328
  35.5 1.6 %collective-permute-start.10 = (bf16[64,2048]{1,0:T(8,128)(2,1)S(1)}, bf16[64,2048]{1,0:T(8,128)(2,1)S(1)}, u32[]{:S(2)}, u32[]{:S(2)}) collective-permute-start(bf16[64,2048]{1,0:T(8,128)(2,1)S(1)} %constant_dynamic-update-slice_fusion.8.refs_0_), channel_id=1, source_target_pairs={{0,4},{4,0},{8,12},{12,8},{16,20},{20,16},{24,28},{28,24},{1,5},{5... | collective-permute-start | bytes 786440 | tf_op jit(solution)/shard_map/ppermute | solution.py:235
  35.6 20.1 %collective-permute-start.7 = (bf16[2,2,16,4096]{3,2,1,0:T(8,128)(2,1)S(1)}, bf16[2,2,16,4096]{3,2,1,0:T(8,128)(2,1)S(1)}, u32[]{:S(2)}, u32[]{:S(2)}) collective-permute-start(bf16[2,2,16,4096]{3,2,1,0:T(8,128)(2,1)S(1)} %shard_map.90.refs_5_), channel_id=1, source_target_pairs={{1,2},{2,1},{5,6},{6,5},{9,10},{10,9},{13,14},{14,13},{17,18},{18,... | collective-permute-start | bytes 1572872 | tf_op jit(solution)/shard_map/ppermute | solution.py:328
  39.5 16.3 %collective-permute-start.14 = (bf16[1,2,16,4096]{3,2,1,0:T(8,128)(2,1)S(1)}, bf16[1,2,16,4096]{3,2,1,0:T(8,128)(2,1)S(1)}, u32[]{:S(2)}, u32[]{:S(2)}) collective-permute-start(bf16[1,2,16,4096]{3,2,1,0:T(8,128)(2,1)S(1)} %shard_map.92.refs_1_), channel_id=1, source_target_pairs={{0,1},{3,2},{4,5},{7,6},{8,9},{11,10},{12,13},{15,14},{16,17},{19,... | collective-permute-start | bytes 786440 | tf_op jit(solution)/shard_map/ppermute | solution.py:328
  47.2 9.5 %collective-permute-start.13 = (bf16[1,2,16,4096]{3,2,1,0:T(8,128)(2,1)S(1)}, bf16[1,2,16,4096]{3,2,1,0:T(8,128)(2,1)S(1)}, u32[]{:S(2)}, u32[]{:S(2)}) collective-permute-start(bf16[1,2,16,4096]{3,2,1,0:T(8,128)(2,1)S(1)} %shard_map.94.refs_2_), channel_id=1, source_target_pairs={{1,2},{2,1},{5,6},{6,5},{9,10},{10,9},{13,14},{14,13},{17,18},{18,... | collective-permute-start | bytes 786440 | tf_op jit(solution)/shard_map/ppermute | solution.py:328
  47.8 14.5 %collective-permute-start.11 = (bf16[1,2,16,4096]{3,2,1,0:T(8,128)(2,1)S(1)}, bf16[1,2,16,4096]{3,2,1,0:T(8,128)(2,1)S(1)}, u32[]{:S(2)}, u32[]{:S(2)}) collective-permute-start(bf16[1,2,16,4096]{3,2,1,0:T(8,128)(2,1)S(1)} %shard_map.93.refs_2_), channel_id=1, source_target_pairs={{0,1},{3,2},{4,5},{7,6},{8,9},{11,10},{12,13},{15,14},{16,17},{19,... | collective-permute-start | bytes 786440 | tf_op jit(solution)/shard_map/ppermute | solution.py:328
  55.8 12.2 %collective-permute-start.15 = (bf16[1,2,16,4096]{3,2,1,0:T(8,128)(2,1)S(1)}, bf16[1,2,16,4096]{3,2,1,0:T(8,128)(2,1)S(1)}, u32[]{:S(2)}, u32[]{:S(2)}) collective-permute-start(bf16[1,2,16,4096]{3,2,1,0:T(8,128)(2,1)S(1)} %shard_map.95.refs_2_), channel_id=1, source_target_pairs={{0,1},{2,3},{1,0},{3,2},{4,5},{6,7},{5,4},{7,6},{8,9},{10,11},{9,8... | collective-permute-start | bytes 786440 | tf_op jit(solution)/shard_map/ppermute | solution.py:328
  55.9 12.1 %collective-permute-start.17 = (bf16[1,2,16,4096]{3,2,1,0:T(8,128)(2,1)S(1)}, bf16[1,2,16,4096]{3,2,1,0:T(8,128)(2,1)S(1)}, u32[]{:S(2)}, u32[]{:S(2)}) collective-permute-start(bf16[1,2,16,4096]{3,2,1,0:T(8,128)(2,1)S(1)} %shard_map.96.refs_2_), channel_id=1, source_target_pairs={{1,2},{2,1},{5,6},{6,5},{9,10},{10,9},{13,14},{14,13},{17,18},{18,... | collective-permute-start | bytes 786440 | tf_op jit(solution)/shard_map/ppermute | solution.py:328
  56.7 16.9 %collective-permute-start.18 = (bf16[1,2,16,4096]{3,2,1,0:T(8,128)(2,1)S(1)}, bf16[1,2,16,4096]{3,2,1,0:T(8,128)(2,1)S(1)}, u32[]{:S(2)}, u32[]{:S(2)}) collective-permute-start(bf16[1,2,16,4096]{3,2,1,0:T(8,128)(2,1)S(1)} %shard_map.97.refs_2_), channel_id=1, source_target_pairs={{0,1},{2,3},{1,0},{3,2},{4,5},{6,7},{5,4},{7,6},{8,9},{10,11},{9,8... | collective-permute-start | bytes 786440 | tf_op jit(solution)/shard_map/ppermute | solution.py:328
  61.1 9.6 %collective-permute-start.16 = (bf16[1,2,16,4096]{3,2,1,0:T(8,128)(2,1)S(1)}, bf16[1,2,16,4096]{3,2,1,0:T(8,128)(2,1)S(1)}, u32[]{:S(2)}, u32[]{:S(2)}) collective-permute-start(bf16[1,2,16,4096]{3,2,1,0:T(8,128)(2,1)S(1)} %shard_map.98.refs_2_), channel_id=1, source_target_pairs={{1,2},{2,1},{5,6},{6,5},{9,10},{10,9},{13,14},{14,13},{17,18},{18,... | collective-permute-start | bytes 786440 | tf_op jit(solution)/shard_map/ppermute | solution.py:328
  62.5 11.2 %collective-permute-start.20 = (bf16[1,2,16,4096]{3,2,1,0:T(8,128)(2,1)S(1)}, bf16[1,2,16,4096]{3,2,1,0:T(8,128)(2,1)S(1)}, u32[]{:S(2)}, u32[]{:S(2)}) collective-permute-start(bf16[1,2,16,4096]{3,2,1,0:T(8,128)(2,1)S(1)} %shard_map.99.refs_2_), channel_id=1, source_target_pairs={{1,2},{2,1},{5,6},{6,5},{9,10},{10,9},{13,14},{14,13},{17,18},{18,... | collective-permute-start | bytes 786440 | tf_op jit(solution)/shard_map/ppermute | solution.py:328
  68.2 8.9 %collective-permute-start.19 = (bf16[1,2,16,4096]{3,2,1,0:T(8,128)(2,1)S(1)}, bf16[1,2,16,4096]{3,2,1,0:T(8,128)(2,1)S(1)}, u32[]{:S(2)}, u32[]{:S(2)}) collective-permute-start(bf16[1,2,16,4096]{3,2,1,0:T(8,128)(2,1)S(1)} %shard_map.102.refs_2_), channel_id=1, source_target_pairs={{0,1},{2,3},{1,0},{3,2},{4,5},{6,7},{5,4},{7,6},{8,9},{10,11},{9,8... | collective-permute-start | bytes 786440 | tf_op jit(solution)/shard_map/ppermute | solution.py:328

commit v6 on v5

--- a/solution.py
+++ b/solution.py
@@ -33,9 +33,9 @@
     ("send", [(1, 2)], 1),
     ("send", [(0, 3)], 0),
     ("send", [(2, 2)], 1),
+    ("send", [(2, 3)], 1),
     ("send", [(1, 3)], 0),
     ("send", [(1, 3)], 1),
-    ("send", [(2, 3)], 1),
     ("finish", 0, 1),
     ("finish", 0, 0),
     ("send", [(2, 3)], 0),

time: 78.6 us -> 77.7 us (0.989)
  waiting for transfers between devices: 17.1 us -> 16.1 us
    ppermute x12, waiting for transfers between devices: 12.2 us -> 11.2 us  [send(): moved = lax.ppermute(value, 'tensor', links(entries[0][1], parity))]
  transfers between devices with their start and end apart: 21 -> 21, of which waited for: 9 -> 8; matrix products, arithmetic and copies ran while one was open for 0% -> 0% of each run, Pallas kernels for 22% -> 22%
where the time goes in v6:
time: 77.7 us; the launch traced here: 77.4 us
  starting transfers between devices  38.8 us (50%)
  Pallas kernels  22 us (28%)
  waiting for transfers between devices  16.1 us (21%)
    ppermute x12, starting transfers between devices, send(): moved = lax.ppermute(value, 'tensor', links(entries[0][1], parity))  30.5 us
    pallas_call x3, Pallas kernels, attend(): pl.pallas_call(kernel, out_shape=shapes, in_specs=[anywhere] * (len(given...  12.4 us
    ppermute x12, waiting for transfers between devices, send(): moved = lax.ppermute(value, 'tensor', links(entries[0][1], parity))  11.2 us
    ppermute x9, starting transfers between devices, swap(): return lax.ppermute(array, 'dp', [(i, i ^ bits) for i in range(dp)])  8.27 us
    pallas_call x4, Pallas kernels, head(): pl.pallas_call(kernel, out_shape=jax.ShapeDtypeStruct((rows, cols), jnp.b...  7.14 us
    ppermute x9, waiting for transfers between devices, swap(): return lax.ppermute(array, 'dp', [(i, i ^ bits) for i in range(dp)])  4.88 us
  transfers between devices with their start and end apart: 21, of which 8 were waited for; matrix products, arithmetic and copies ran while one was open for 0% of the time, Pallas kernels for 22%

profile of v6, /device:TPU:0, one launch (start us, length us, event | category | flops | bytes accessed | tf_op | source)
XLA Modules:
  0.0 77.4 jit_solution(391582230799994334)
XLA Ops:
  0.0 3.7 %shard_map.82 = (bf16[16,2048]{1,0:T(8,128)(2,1)S(1)}, bf16[2048,1024]{1,0:T(8,128)(2,1)S(1)}) custom-call(s32[48]{0:T(128)} %refs_0_.5, s32[48]{0:T(128)} %refs_1_.5, bf16[5,48,2048]{2,1,0:T(8,128)(2,1)} %bitcast.30, bf16[5,48,256]{2,1,0:T(8,128)(2,1)} %bitcast.33, bf16[5,48,256]{2,1,0:T(8,128)(2,1)} %bitcast.36, bf16[48,256,256]{2,1,0:T(8,128)(2,1)} %refs_5_.5, ...), custom_call_target="tpu_custom_call" | custom-call | flops 1 | bytes 1 | tf_op jit(solution)/shard_map/pallas_call | solution.py:159
  3.7 3.0 %collective-permute-start = (bf16[16,2048]{1,0:T(8,128)(2,1)S(1)}, bf16[16,2048]{1,0:T(8,128)(2,1)S(1)}, u32[]{:S(2)}, u32[]{:S(2)}) collective-permute-start(bf16[16,2048]{1,0:T(8,128)(2,1)S(1)} %get-tuple-element.18.refs_8_), channel_id=1, source_target_pairs={{0,8},{4,12},{8,0},{12,4},{16,24},{20,28},{24,16},{28,20},{1,9},{5... | collective-permute-start | bytes 196616 | tf_op jit(solution)/shard_map/ppermute | solution.py:235
  6.7 4.5 %shard_map.83 = (bf16[16,2048]{1,0:T(8,128)(2,1)S(1)}, bf16[2048,1536]{1,0:T(8,128)(2,1)S(1)}) custom-call(s32[48]{0:T(128)} %refs_0_.5, s32[48]{0:T(128)} %refs_1_.5, bf16[5,48,2048]{2,1,0:T(8,128)(2,1)} %bitcast.31, bf16[5,48,256]{2,1,0:T(8,128)(2,1)} %bitcast.34, bf16[5,48,256]{2,1,0:T(8,128)(2,1)} %bitcast.37, bf16[48,256,256]{2,1,0:T(8,128)(2,1)} %refs_5_.5, ...), custom_call_target="tpu_custom_call" | custom-call | flops 1 | bytes 1 | tf_op jit(solution)/shard_map/pallas_call | solution.py:159
  11.2 0.1 collective-permute-start.4
  11.3 0.0 collective-permute-done
  11.3 2.1 %collective-permute-start.1 = (bf16[32,2048]{1,0:T(8,128)(2,1)S(1)}, bf16[32,2048]{1,0:T(8,128)(2,1)S(1)}, u32[]{:S(2)}, u32[]{:S(2)}) collective-permute-start(bf16[32,2048]{1,0:T(8,128)(2,1)S(1)} %get-tuple-element.31.refs_8_), channel_id=1, source_target_pairs={{0,16},{4,20},{8,24},{12,28},{16,0},{20,4},{24,8},{28,12},{1,17},{... | collective-permute-start | bytes 393224 | tf_op jit(solution)/shard_map/ppermute | solution.py:235
  13.4 4.3 %shard_map.84 = (bf16[16,2048]{1,0:T(8,128)(2,1)S(1)}, bf16[2048,1536]{1,0:T(8,128)(2,1)S(1)}) custom-call(s32[48]{0:T(128)} %refs_0_.5, s32[48]{0:T(128)} %refs_1_.5, bf16[5,48,2048]{2,1,0:T(8,128)(2,1)} %bitcast.32, bf16[5,48,256]{2,1,0:T(8,128)(2,1)} %bitcast.35, bf16[5,48,256]{2,1,0:T(8,128)(2,1)} %bitcast.38, bf16[48,256,256]{2,1,0:T(8,128)(2,1)} %refs_5_.5, ...), custom_call_target="tpu_custom_call" | custom-call | flops 1 | bytes 1 | tf_op jit(solution)/shard_map/pallas_call | solution.py:159
  17.7 0.0 collective-permute-done.4
  17.7 0.0 collective-permute-done.1
  17.8 0.1 collective-permute-start.2
  17.9 0.7 collective-permute-start.5
  18.6 0.8 %collective-permute-done.2.refs_1_ = bf16[64,2048]{1,0:T(8,128)(2,1)S(1)} collective-permute-done((bf16[64,2048]{1,0:T(8,128)(2,1)S(1)}, bf16[64,2048]{1,0:T(8,128)(2,1)S(1)}, u32[]{:S(2)}, u32[]{:S(2)}) %collective-permute-start.2) | collective-permute-done | bytes 262176 | tf_op jit(solution)/shard_map/ppermute | solution.py:235
  19.4 2.3 %shard_map.85.refs_5_ = bf16[128,4096]{1,0:T(8,128)(2,1)S(1)} custom-call(bf16[64,2048]{1,0:T(8,128)(2,1)S(1)} %constant_dynamic-update-slice_fusion.2.refs_0_, bf16[64,2048]{1,0:T(8,128)(2,1)S(1)} %collective-permute-done.2.refs_1_, bf16[2048,1024]{1,0:T(8,128)(2,1)S(1)} %get-tuple-element.23.refs_2_, bf16[2048,1536]{1,0:T(8,128)(2,1)S(1)} %get-tuple-element.24.refs_3_, ...), custom_call_target="tpu_custom_call" | custom-call | flops 1 | bytes 1 | tf_op jit(solution)/shard_map/pallas_call | solution.py:223
  21.7 0.1 shard_map.86.refs_6_
  21.8 1.3 %collective-permute-start.3 = (bf16[2,2,16,4096]{3,2,1,0:T(8,128)(2,1)S(1)}, bf16[2,2,16,4096]{3,2,1,0:T(8,128)(2,1)S(1)}, u32[]{:S(2)}, u32[]{:S(2)}) collective-permute-start(bf16[2,2,16,4096]{3,2,1,0:T(8,128)(2,1)S(1)} %shard_map.86.refs_6_), channel_id=1, source_target_pairs={{0,1},{3,2},{4,5},{7,6},{8,9},{11,10},{12,13},{15,14},{16,17},{19,... | collective-permute-start | bytes 1572872 | tf_op jit(solution)/shard_map/ppermute | solution.py:328
  23.1 0.1 shard_map.87
  23.2 0.6 collective-permute-done.5
  23.8 1.5 %collective-permute-start.9 = (bf16[16,2048]{1,0:T(8,128)(2,1)S(1)}, bf16[16,2048]{1,0:T(8,128)(2,1)S(1)}, u32[]{:S(2)}, u32[]{:S(2)}) collective-permute-start(bf16[16,2048]{1,0:T(8,128)(2,1)S(1)} %get-tuple-element.28.refs_5_), channel_id=1, source_target_pairs={{0,8},{4,12},{8,0},{12,4},{16,24},{20,28},{24,16},{28,20},{1,9},{5... | collective-permute-start | bytes 196616 | tf_op jit(solution)/shard_map/ppermute | solution.py:235
  25.3 0.1 collective-permute-start.6
  25.3 2.7 %collective-permute-done.9 = bf16[16,2048]{1,0:T(8,128)(2,1)S(1)} collective-permute-done((bf16[16,2048]{1,0:T(8,128)(2,1)S(1)}, bf16[16,2048]{1,0:T(8,128)(2,1)S(1)}, u32[]{:S(2)}, u32[]{:S(2)}) %collective-permute-start.9) | collective-permute-done | bytes 65568 | tf_op jit(solution)/shard_map/ppermute | solution.py:235
  28.0 0.7 collective-permute-start.10
  28.7 0.0 collective-permute-done.6.refs_1_
  28.7 2.4 %shard_map.88 = bf16[128,4096]{1,0:T(8,128)(2,1)S(1)} custom-call(bf16[64,2048]{1,0:T(8,128)(2,1)S(1)} %constant_dynamic-update-slice_fusion.5.refs_0_, bf16[64,2048]{1,0:T(8,128)(2,1)S(1)} %collective-permute-done.6.refs_1_, bf16[2048,1024]{1,0:T(8,128)(2,1)S(1)} %get-tuple-element.23.refs_2_, bf16[2048,1536]{1,0:T(8,128)(2,1)S(1)} %get-tuple-element.24.refs_3_, ...), custom_call_target="tpu_custom_call" | custom-call | flops 1 | bytes 1 | tf_op jit(solution)/shard_map/pallas_call | solution.py:223
  31.1 0.1 shard_map.89.refs_4_
  31.2 3.5 %collective-permute-start.8 = (bf16[2,2,16,4096]{3,2,1,0:T(8,128)(2,1)S(1)}, bf16[2,2,16,4096]{3,2,1,0:T(8,128)(2,1)S(1)}, u32[]{:S(2)}, u32[]{:S(2)}) collective-permute-start(bf16[2,2,16,4096]{3,2,1,0:T(8,128)(2,1)S(1)} %shard_map.89.refs_4_), channel_id=1, source_target_pairs={{0,1},{3,2},{4,5},{7,6},{8,9},{11,10},{12,13},{15,14},{16,17},{19,... | collective-permute-start | bytes 1572872 | tf_op jit(solution)/shard_map/ppermute | solution.py:328
  34.7 0.6 collective-permute-done.3.refs_1_.refs_3_
  35.3 0.1 shard_map.90.refs_5_
  35.5 0.0 collective-permute-done.10
  35.5 0.1 collective-permute-start.11
  35.6 0.7 collective-permute-start.7
  36.3 0.8 %collective-permute-done.11.refs_1_ = bf16[64,2048]{1,0:T(8,128)(2,1)S(1)} collective-permute-done((bf16[64,2048]{1,0:T(8,128)(2,1)S(1)}, bf16[64,2048]{1,0:T(8,128)(2,1)S(1)}, u32[]{:S(2)}, u32[]{:S(2)}) %collective-permute-start.11) | collective-permute-done | bytes 262176 | tf_op jit(solution)/shard_map/ppermute | solution.py:235
  37.1 2.4 %shard_map.91 = bf16[128,4096]{1,0:T(8,128)(2,1)S(1)} custom-call(bf16[64,2048]{1,0:T(8,128)(2,1)S(1)} %constant_dynamic-update-slice_fusion.8.refs_0_, bf16[64,2048]{1,0:T(8,128)(2,1)S(1)} %collective-permute-done.11.refs_1_, bf16[2048,1024]{1,0:T(8,128)(2,1)S(1)} %get-tuple-element.23.refs_2_, bf16[2048,1536]{1,0:T(8,128)(2,1)S(1)} %get-tuple-element.24.refs_3_, ...), custom_call_target="tpu_custom_call" | custom-call | flops 1 | bytes 1 | tf_op jit(solution)/shard_map/pallas_call | solution.py:223
  39.5 7.5 %collective-permute-start.14 = (bf16[1,2,16,4096]{3,2,1,0:T(8,128)(2,1)S(1)}, bf16[1,2,16,4096]{3,2,1,0:T(8,128)(2,1)S(1)}, u32[]{:S(2)}, u32[]{:S(2)}) collective-permute-start(bf16[1,2,16,4096]{3,2,1,0:T(8,128)(2,1)S(1)} %shard_map.92.refs_1_), channel_id=1, source_target_pairs={{0,1},{3,2},{4,5},{7,6},{8,9},{11,10},{12,13},{15,14},{16,17},{19,... | collective-permute-start | bytes 786440 | tf_op jit(solution)/shard_map/ppermute | solution.py:328
  47.1 1.3 %collective-permute-start.13 = (bf16[1,2,16,4096]{3,2,1,0:T(8,128)(2,1)S(1)}, bf16[1,2,16,4096]{3,2,1,0:T(8,128)(2,1)S(1)}, u32[]{:S(2)}, u32[]{:S(2)}) collective-permute-start(bf16[1,2,16,4096]{3,2,1,0:T(8,128)(2,1)S(1)} %shard_map.93.refs_2_), channel_id=1, source_target_pairs={{0,1},{3,2},{4,5},{7,6},{8,9},{11,10},{12,13},{15,14},{16,17},{19,... | collective-permute-start | bytes 786440 | tf_op jit(solution)/shard_map/ppermute | solution.py:328
  48.4 0.0 collective-permute-done.8.refs_1_
  48.4 0.1 shard_map.94.refs_2_
  48.5 0.7 collective-permute-start.12
  49.2 0.0 collective-permute-done.7.refs_1_
  49.2 0.1 shard_map.95.refs_2_
  49.3 6.3 %collective-permute-start.15 = (bf16[1,2,16,4096]{3,2,1,0:T(8,128)(2,1)S(1)}, bf16[1,2,16,4096]{3,2,1,0:T(8,128)(2,1)S(1)}, u32[]{:S(2)}, u32[]{:S(2)}) collective-permute-start(bf16[1,2,16,4096]{3,2,1,0:T(8,128)(2,1)S(1)} %shard_map.95.refs_2_), channel_id=1, source_target_pairs={{0,1},{2,3},{1,0},{3,2},{4,5},{6,7},{5,4},{7,6},{8,9},{10,11},{9,8... | collective-permute-start | bytes 786440 | tf_op jit(solution)/shard_map/ppermute | solution.py:328
  55.6 0.0 collective-permute-done.14.refs_1_
  55.6 0.1 shard_map.96.refs_2_
  55.7 0.7 collective-permute-start.17
  56.4 2.9 %collective-permute-done.13.refs_1_ = bf16[1,2,16,4096]{3,2,1,0:T(8,128)(2,1)S(1)} collective-permute-done((bf16[1,2,16,4096]{3,2,1,0:T(8,128)(2,1)S(1)}, bf16[1,2,16,4096]{3,2,1,0:T(8,128)(2,1)S(1)}, u32[]{:S(2)}, u32[]{:S(2)}) %collective-permute-start.13) | collective-permute-done | bytes 262176 | tf_op jit(solution)/shard_map/ppermute | solution.py:328
  59.3 0.1 shard_map.97.refs_2_
  59.3 0.7 collective-permute-start.20
  60.0 0.0 collective-permute-done.12.refs_1_
  60.0 0.1 shard_map.98.refs_2_
  60.1 5.0 %collective-permute-start.18 = (bf16[1,2,16,4096]{3,2,1,0:T(8,128)(2,1)S(1)}, bf16[1,2,16,4096]{3,2,1,0:T(8,128)(2,1)S(1)}, u32[]{:S(2)}, u32[]{:S(2)}) collective-permute-start(bf16[1,2,16,4096]{3,2,1,0:T(8,128)(2,1)S(1)} %shard_map.98.refs_2_), channel_id=1, source_target_pairs={{0,1},{2,3},{1,0},{3,2},{4,5},{6,7},{5,4},{7,6},{8,9},{10,11},{9,8... | collective-permute-start | bytes 786440 | tf_op jit(solution)/shard_map/ppermute | solution.py:328
  65.1 0.1 shard_map.99.refs_2_
  65.2 0.7 collective-permute-start.16
  65.9 0.1 shard_map.100.refs_0_.refs_2_
  66.0 0.0 collective-permute-done.15.refs_1_
  66.1 0.0 collective-permute-done.17.refs_1_
  66.1 0.1 shard_map.102.refs_2_
  66.2 2.1 %collective-permute-start.19 = (bf16[1,2,16,4096]{3,2,1,0:T(8,128)(2,1)S(1)}, bf16[1,2,16,4096]{3,2,1,0:T(8,128)(2,1)S(1)}, u32[]{:S(2)}, u32[]{:S(2)}) collective-permute-start(bf16[1,2,16,4096]{3,2,1,0:T(8,128)(2,1)S(1)} %shard_map.102.refs_2_), channel_id=1, source_target_pairs={{0,1},{2,3},{1,0},{3,2},{4,5},{6,7},{5,4},{7,6},{8,9},{10,11},{9,8... | collective-permute-start | bytes 786440 | tf_op jit(solution)/shard_map/ppermute | solution.py:328
  68.3 0.0 collective-permute-done.16.refs_1_
  68.3 0.1 shard_map.103.refs_0_.refs_2_
  68.3 4.0 %collective-permute-done.18.refs_1_ = bf16[1,2,16,4096]{3,2,1,0:T(8,128)(2,1)S(1)} collective-permute-done((bf16[1,2,16,4096]{3,2,1,0:T(8,128)(2,1)S(1)}, bf16[1,2,16,4096]{3,2,1,0:T(8,128)(2,1)S(1)}, u32[]{:S(2)}, u32[]{:S(2)}) %collective-permute-start.18) | collective-permute-done | bytes 262176 | tf_op jit(solution)/shard_map/ppermute | solution.py:328
  72.4 0.0 collective-permute-done.20.refs_4_
  72.4 3.7 %collective-permute-done.19.refs_3_ = bf16[1,2,16,4096]{3,2,1,0:T(8,128)(2,1)S(1)} collective-permute-done((bf16[1,2,16,4096]{3,2,1,0:T(8,128)(2,1)S(1)}, bf16[1,2,16,4096]{3,2,1,0:T(8,128)(2,1)S(1)}, u32[]{:S(2)}, u32[]{:S(2)}) %collective-permute-start.19) | collective-permute-done | bytes 262176 | tf_op jit(solution)/shard_map/ppermute | solution.py:328
  76.1 1.3 %shard_map.105 = f32[2,48,4096]{2,1,0:T(8,128)} custom-call(f32[2,16,4096]{2,1,0:T(8,128)S(1)} %shard_map.101.refs_2_.refs_0_, f32[2,16,4096]{2,1,0:T(8,128)S(1)} %shard_map.104.refs_1_, bf16[2,4,16,4096]{3,2,1,0:T(8,128)(2,1)S(1)} %bitcast.21, bf16[1,2,16,4096]{3,2,1,0:T(8,128)(2,1)S(1)} %collective-permute-done.19.refs_3_, ...), custom_call_target="tpu_custom_call" | custom-call | flops 1 | bytes 1 | tf_op jit(solution)/shard_map/pallas_call | solution.py:376
  (15 shorter events, 0.3 us)
Async XLA Ops:
  3.7 7.6 %collective-permute-start = (bf16[16,2048]{1,0:T(8,128)(2,1)S(1)}, bf16[16,2048]{1,0:T(8,128)(2,1)S(1)}, u32[]{:S(2)}, u32[]{:S(2)}) collective-permute-start(bf16[16,2048]{1,0:T(8,128)(2,1)S(1)} %get-tuple-element.18.refs_8_), channel_id=1, source_target_pairs={{0,8},{4,12},{8,0},{12,4},{16,24},{20,28},{24,16},{28,20},{1,9},{5... | collective-permute-start | bytes 196616 | tf_op jit(solution)/shard_map/ppermute | solution.py:235
  11.2 6.5 %collective-permute-start.4 = (bf16[16,2048]{1,0:T(8,128)(2,1)S(1)}, bf16[16,2048]{1,0:T(8,128)(2,1)S(1)}, u32[]{:S(2)}, u32[]{:S(2)}) collective-permute-start(bf16[16,2048]{1,0:T(8,128)(2,1)S(1)} %get-tuple-element.19), channel_id=1, source_target_pairs={{0,8},{4,12},{8,0},{12,4},{16,24},{20,28},{24,16},{28,20},{1,9},{5... | collective-permute-start | bytes 196616 | tf_op jit(solution)/shard_map/ppermute | solution.py:235
  11.3 6.4 %collective-permute-start.1 = (bf16[32,2048]{1,0:T(8,128)(2,1)S(1)}, bf16[32,2048]{1,0:T(8,128)(2,1)S(1)}, u32[]{:S(2)}, u32[]{:S(2)}) collective-permute-start(bf16[32,2048]{1,0:T(8,128)(2,1)S(1)} %get-tuple-element.31.refs_8_), channel_id=1, source_target_pairs={{0,16},{4,20},{8,24},{12,28},{16,0},{20,4},{24,8},{28,12},{1,17},{... | collective-permute-start | bytes 393224 | tf_op jit(solution)/shard_map/ppermute | solution.py:235
  17.8 1.6 %collective-permute-start.2 = (bf16[64,2048]{1,0:T(8,128)(2,1)S(1)}, bf16[64,2048]{1,0:T(8,128)(2,1)S(1)}, u32[]{:S(2)}, u32[]{:S(2)}) collective-permute-start(bf16[64,2048]{1,0:T(8,128)(2,1)S(1)} %constant_dynamic-update-slice_fusion.2.refs_0_), channel_id=1, source_target_pairs={{0,4},{4,0},{8,12},{12,8},{16,20},{20,16},{24,28},{28,24},{1,5},{5... | collective-permute-start | bytes 786440 | tf_op jit(solution)/shard_map/ppermute | solution.py:235
  17.9 5.9 %collective-permute-start.5 = (bf16[32,2048]{1,0:T(8,128)(2,1)S(1)}, bf16[32,2048]{1,0:T(8,128)(2,1)S(1)}, u32[]{:S(2)}, u32[]{:S(2)}) collective-permute-start(bf16[32,2048]{1,0:T(8,128)(2,1)S(1)} %pad_maximum_fusion), channel_id=1, source_target_pairs={{0,16},{4,20},{8,24},{12,28},{16,0},{20,4},{24,8},{28,12},{1,17},{... | collective-permute-start | bytes 393224 | tf_op jit(solution)/shard_map/ppermute | solution.py:235
  21.8 13.5 %collective-permute-start.3 = (bf16[2,2,16,4096]{3,2,1,0:T(8,128)(2,1)S(1)}, bf16[2,2,16,4096]{3,2,1,0:T(8,128)(2,1)S(1)}, u32[]{:S(2)}, u32[]{:S(2)}) collective-permute-start(bf16[2,2,16,4096]{3,2,1,0:T(8,128)(2,1)S(1)} %shard_map.86.refs_6_), channel_id=1, source_target_pairs={{0,1},{3,2},{4,5},{7,6},{8,9},{11,10},{12,13},{15,14},{16,17},{19,... | collective-permute-start | bytes 1572872 | tf_op jit(solution)/shard_map/ppermute | solution.py:328
  23.8 4.3 %collective-permute-start.9 = (bf16[16,2048]{1,0:T(8,128)(2,1)S(1)}, bf16[16,2048]{1,0:T(8,128)(2,1)S(1)}, u32[]{:S(2)}, u32[]{:S(2)}) collective-permute-start(bf16[16,2048]{1,0:T(8,128)(2,1)S(1)} %get-tuple-element.28.refs_5_), channel_id=1, source_target_pairs={{0,8},{4,12},{8,0},{12,4},{16,24},{20,28},{24,16},{28,20},{1,9},{5... | collective-permute-start | bytes 196616 | tf_op jit(solution)/shard_map/ppermute | solution.py:235
  25.3 3.5 %collective-permute-start.6 = (bf16[64,2048]{1,0:T(8,128)(2,1)S(1)}, bf16[64,2048]{1,0:T(8,128)(2,1)S(1)}, u32[]{:S(2)}, u32[]{:S(2)}) collective-permute-start(bf16[64,2048]{1,0:T(8,128)(2,1)S(1)} %constant_dynamic-update-slice_fusion.5.refs_0_), channel_id=1, source_target_pairs={{0,4},{4,0},{8,12},{12,8},{16,20},{20,16},{24,28},{28,24},{1,5},{5... | collective-permute-start | bytes 786440 | tf_op jit(solution)/shard_map/ppermute | solution.py:235
  28.0 7.4 %collective-permute-start.10 = (bf16[32,2048]{1,0:T(8,128)(2,1)S(1)}, bf16[32,2048]{1,0:T(8,128)(2,1)S(1)}, u32[]{:S(2)}, u32[]{:S(2)}) collective-permute-start(bf16[32,2048]{1,0:T(8,128)(2,1)S(1)} %pad_maximum_fusion.1), channel_id=1, source_target_pairs={{0,16},{4,20},{8,24},{12,28},{16,0},{20,4},{24,8},{28,12},{1,17},{... | collective-permute-start | bytes 393224 | tf_op jit(solution)/shard_map/ppermute | solution.py:235
  31.2 17.2 %collective-permute-start.8 = (bf16[2,2,16,4096]{3,2,1,0:T(8,128)(2,1)S(1)}, bf16[2,2,16,4096]{3,2,1,0:T(8,128)(2,1)S(1)}, u32[]{:S(2)}, u32[]{:S(2)}) collective-permute-start(bf16[2,2,16,4096]{3,2,1,0:T(8,128)(2,1)S(1)} %shard_map.89.refs_4_), channel_id=1, source_target_pairs={{0,1},{3,2},{4,5},{7,6},{8,9},{11,10},{12,13},{15,14},{16,17},{19,... | collective-permute-start | bytes 1572872 | tf_op jit(solution)/shard_map/ppermute | solution.py:328
  35.5 1.6 %collective-permute-start.11 = (bf16[64,2048]{1,0:T(8,128)(2,1)S(1)}, bf16[64,2048]{1,0:T(8,128)(2,1)S(1)}, u32[]{:S(2)}, u32[]{:S(2)}) collective-permute-start(bf16[64,2048]{1,0:T(8,128)(2,1)S(1)} %constant_dynamic-update-slice_fusion.8.refs_0_), channel_id=1, source_target_pairs={{0,4},{4,0},{8,12},{12,8},{16,20},{20,16},{24,28},{28,24},{1,5},{5... | collective-permute-start | bytes 786440 | tf_op jit(solution)/shard_map/ppermute | solution.py:235
  35.6 13.6 %collective-permute-start.7 = (bf16[2,2,16,4096]{3,2,1,0:T(8,128)(2,1)S(1)}, bf16[2,2,16,4096]{3,2,1,0:T(8,128)(2,1)S(1)}, u32[]{:S(2)}, u32[]{:S(2)}) collective-permute-start(bf16[2,2,16,4096]{3,2,1,0:T(8,128)(2,1)S(1)} %shard_map.90.refs_5_), channel_id=1, source_target_pairs={{1,2},{2,1},{5,6},{6,5},{9,10},{10,9},{13,14},{14,13},{17,18},{18,... | collective-permute-start | bytes 1572872 | tf_op jit(solution)/shard_map/ppermute | solution.py:328
  39.5 16.1 %collective-permute-start.14 = (bf16[1,2,16,4096]{3,2,1,0:T(8,128)(2,1)S(1)}, bf16[1,2,16,4096]{3,2,1,0:T(8,128)(2,1)S(1)}, u32[]{:S(2)}, u32[]{:S(2)}) collective-permute-start(bf16[1,2,16,4096]{3,2,1,0:T(8,128)(2,1)S(1)} %shard_map.92.refs_1_), channel_id=1, source_target_pairs={{0,1},{3,2},{4,5},{7,6},{8,9},{11,10},{12,13},{15,14},{16,17},{19,... | collective-permute-start | bytes 786440 | tf_op jit(solution)/shard_map/ppermute | solution.py:328
  47.1 12.2 %collective-permute-start.13 = (bf16[1,2,16,4096]{3,2,1,0:T(8,128)(2,1)S(1)}, bf16[1,2,16,4096]{3,2,1,0:T(8,128)(2,1)S(1)}, u32[]{:S(2)}, u32[]{:S(2)}) collective-permute-start(bf16[1,2,16,4096]{3,2,1,0:T(8,128)(2,1)S(1)} %shard_map.93.refs_2_), channel_id=1, source_target_pairs={{0,1},{3,2},{4,5},{7,6},{8,9},{11,10},{12,13},{15,14},{16,17},{19,... | collective-permute-start | bytes 786440 | tf_op jit(solution)/shard_map/ppermute | solution.py:328
  48.5 11.6 %collective-permute-start.12 = (bf16[1,2,16,4096]{3,2,1,0:T(8,128)(2,1)S(1)}, bf16[1,2,16,4096]{3,2,1,0:T(8,128)(2,1)S(1)}, u32[]{:S(2)}, u32[]{:S(2)}) collective-permute-start(bf16[1,2,16,4096]{3,2,1,0:T(8,128)(2,1)S(1)} %shard_map.94.refs_2_), channel_id=1, source_target_pairs={{1,2},{2,1},{5,6},{6,5},{9,10},{10,9},{13,14},{14,13},{17,18},{18,... | collective-permute-start | bytes 786440 | tf_op jit(solution)/shard_map/ppermute | solution.py:328
  49.3 16.7 %collective-permute-start.15 = (bf16[1,2,16,4096]{3,2,1,0:T(8,128)(2,1)S(1)}, bf16[1,2,16,4096]{3,2,1,0:T(8,128)(2,1)S(1)}, u32[]{:S(2)}, u32[]{:S(2)}) collective-permute-start(bf16[1,2,16,4096]{3,2,1,0:T(8,128)(2,1)S(1)} %shard_map.95.refs_2_), channel_id=1, source_target_pairs={{0,1},{2,3},{1,0},{3,2},{4,5},{6,7},{5,4},{7,6},{8,9},{10,11},{9,8... | collective-permute-start | bytes 786440 | tf_op jit(solution)/shard_map/ppermute | solution.py:328
  55.7 10.4 %collective-permute-start.17 = (bf16[1,2,16,4096]{3,2,1,0:T(8,128)(2,1)S(1)}, bf16[1,2,16,4096]{3,2,1,0:T(8,128)(2,1)S(1)}, u32[]{:S(2)}, u32[]{:S(2)}) collective-permute-start(bf16[1,2,16,4096]{3,2,1,0:T(8,128)(2,1)S(1)} %shard_map.96.refs_2_), channel_id=1, source_target_pairs={{1,2},{2,1},{5,6},{6,5},{9,10},{10,9},{13,14},{14,13},{17,18},{18,... | collective-permute-start | bytes 786440 | tf_op jit(solution)/shard_map/ppermute | solution.py:328
  59.3 13.1 %collective-permute-start.20 = (bf16[1,2,16,4096]{3,2,1,0:T(8,128)(2,1)S(1)}, bf16[1,2,16,4096]{3,2,1,0:T(8,128)(2,1)S(1)}, u32[]{:S(2)}, u32[]{:S(2)}) collective-permute-start(bf16[1,2,16,4096]{3,2,1,0:T(8,128)(2,1)S(1)} %shard_map.97.refs_2_), channel_id=1, source_target_pairs={{1,2},{2,1},{5,6},{6,5},{9,10},{10,9},{13,14},{14,13},{17,18},{18,... | collective-permute-start | bytes 786440 | tf_op jit(solution)/shard_map/ppermute | solution.py:328
  60.1 12.2 %collective-permute-start.18 = (bf16[1,2,16,4096]{3,2,1,0:T(8,128)(2,1)S(1)}, bf16[1,2,16,4096]{3,2,1,0:T(8,128)(2,1)S(1)}, u32[]{:S(2)}, u32[]{:S(2)}) collective-permute-start(bf16[1,2,16,4096]{3,2,1,0:T(8,128)(2,1)S(1)} %shard_map.98.refs_2_), channel_id=1, source_target_pairs={{0,1},{2,3},{1,0},{3,2},{4,5},{6,7},{5,4},{7,6},{8,9},{10,11},{9,8... | collective-permute-start | bytes 786440 | tf_op jit(solution)/shard_map/ppermute | solution.py:328
  65.2 3.1 %collective-permute-start.16 = (bf16[1,2,16,4096]{3,2,1,0:T(8,128)(2,1)S(1)}, bf16[1,2,16,4096]{3,2,1,0:T(8,128)(2,1)S(1)}, u32[]{:S(2)}, u32[]{:S(2)}) collective-permute-start(bf16[1,2,16,4096]{3,2,1,0:T(8,128)(2,1)S(1)} %shard_map.99.refs_2_), channel_id=1, source_target_pairs={{1,2},{2,1},{5,6},{6,5},{9,10},{10,9},{13,14},{14,13},{17,18},{18,... | collective-permute-start | bytes 786440 | tf_op jit(solution)/shard_map/ppermute | solution.py:328
  66.2 9.9 %collective-permute-start.19 = (bf16[1,2,16,4096]{3,2,1,0:T(8,128)(2,1)S(1)}, bf16[1,2,16,4096]{3,2,1,0:T(8,128)(2,1)S(1)}, u32[]{:S(2)}, u32[]{:S(2)}) collective-permute-start(bf16[1,2,16,4096]{3,2,1,0:T(8,128)(2,1)S(1)} %shard_map.102.refs_2_), channel_id=1, source_target_pairs={{0,1},{2,3},{1,0},{3,2},{4,5},{6,7},{5,4},{7,6},{8,9},{10,11},{9,8... | collective-permute-start | bytes 786440 | tf_op jit(solution)/shard_map/ppermute | solution.py:328

commit v7 on v6

--- a/solution.py
+++ b/solution.py
@@ -363,21 +363,34 @@
         given = [part] + [array for array, _ in came]
         places = [place for _, place in came]
 
+        earlier = [array.reshape(sources, BLOCK, cols) for array in earlier]
+
         def kernel(*refs):
-            earlier, (part, *rest), out = refs[: len(parts) - 1], refs[len(parts) - 1 : -1], refs[-1]
+            earlier, (part, *rest), (out, total, sems) = refs[: len(parts) - 1], refs[len(parts) - 1 : -3], refs[-3:]
             turned = lax.rem(lax.axis_index("dp"), 2) if paired else 0
-            for n in range(len(parts)):
-                total = earlier[n][...] if n < len(earlier) else sum_kernel(part, zip(rest, places))
-                total = total.reshape(sources, BLOCK, cols)
-                for source in range(sources):
-                    out[source ^ turned, pl.ds(n * BLOCK, BLOCK)] = total[source]
+            copies = [
+                pltpu.make_async_copy(array.at[source], out.at[source ^ turned, pl.ds(n * BLOCK, BLOCK)], sems.at[n, source])
+                for n, array in enumerate((*earlier, total))
+                for source in range(sources)
+            ]
+            for copy in copies[:-sources]:
+                copy.start()
+            total[...] = sum_kernel(part, zip(rest, places)).reshape(sources, BLOCK, cols)
+            for copy in copies[-sources:]:
+                copy.start()
+            for copy in copies:
+                copy.wait()
 
         vmem = pl.BlockSpec(memory_space=pltpu.VMEM)
         out = pl.pallas_call(
             kernel,
             out_shape=jax.ShapeDtypeStruct((sources, len(parts) * BLOCK, cols), jnp.float32),
             in_specs=[vmem] * (len(earlier) + len(given)),
-            out_specs=vmem,
+            out_specs=pl.BlockSpec(memory_space=pl.ANY),
+            scratch_shapes=[
+                pltpu.VMEM((sources, BLOCK, cols), jnp.float32),
+                pltpu.SemaphoreType.DMA((len(parts), sources)),
+            ],
             compiler_params=pltpu.CompilerParams(vmem_limit_bytes=16 << 20),
             cost_estimate=SHORT,
         )(*earlier, *given)

time: 77.7 us -> 77.7 us (level)
  no operation moved by 1% of the time
where the time goes in v7:
time: 77.7 us; the launch traced here: 77.4 us
  starting transfers between devices  38.8 us (50%)
  Pallas kernels  21.9 us (28%)
  waiting for transfers between devices  16.1 us (21%)
    ppermute x12, starting transfers between devices, send(): moved = lax.ppermute(value, 'tensor', links(entries[0][1], parity))  30.5 us
    pallas_call x3, Pallas kernels, attend(): pl.pallas_call(kernel, out_shape=shapes, in_specs=[anywhere] * (len(given...  12.4 us
    ppermute x12, waiting for transfers between devices, send(): moved = lax.ppermute(value, 'tensor', links(entries[0][1], parity))  11.2 us
    ppermute x9, starting transfers between devices, swap(): return lax.ppermute(array, 'dp', [(i, i ^ bits) for i in range(dp)])  8.27 us
    pallas_call x4, Pallas kernels, head(): pl.pallas_call(kernel, out_shape=jax.ShapeDtypeStruct((rows, cols), jnp.b...  7.14 us
    ppermute x9, waiting for transfers between devices, swap(): return lax.ppermute(array, 'dp', [(i, i ^ bits) for i in range(dp)])  4.88 us
  transfers between devices with their start and end apart: 21, of which 8 were waited for; matrix products, arithmetic and copies ran while one was open for 0% of the time, Pallas kernels for 22%

profile of v7, /device:TPU:0, one launch (start us, length us, event | category | flops | bytes accessed | tf_op | source)
XLA Modules:
  0.0 77.4 jit_solution(14776479423953990011)
XLA Ops:
  0.0 3.7 %shard_map.82 = (bf16[16,2048]{1,0:T(8,128)(2,1)S(1)}, bf16[2048,1024]{1,0:T(8,128)(2,1)S(1)}) custom-call(s32[48]{0:T(128)} %refs_0_.5, s32[48]{0:T(128)} %refs_1_.5, bf16[5,48,2048]{2,1,0:T(8,128)(2,1)} %bitcast.30, bf16[5,48,256]{2,1,0:T(8,128)(2,1)} %bitcast.33, bf16[5,48,256]{2,1,0:T(8,128)(2,1)} %bitcast.36, bf16[48,256,256]{2,1,0:T(8,128)(2,1)} %refs_5_.5, ...), custom_call_target="tpu_custom_call" | custom-call | flops 1 | bytes 1 | tf_op jit(solution)/shard_map/pallas_call | solution.py:159
  3.7 3.0 %collective-permute-start = (bf16[16,2048]{1,0:T(8,128)(2,1)S(1)}, bf16[16,2048]{1,0:T(8,128)(2,1)S(1)}, u32[]{:S(2)}, u32[]{:S(2)}) collective-permute-start(bf16[16,2048]{1,0:T(8,128)(2,1)S(1)} %get-tuple-element.18.refs_8_), channel_id=1, source_target_pairs={{0,8},{4,12},{8,0},{12,4},{16,24},{20,28},{24,16},{28,20},{1,9},{5... | collective-permute-start | bytes 196616 | tf_op jit(solution)/shard_map/ppermute | solution.py:235
  6.7 4.5 %shard_map.83 = (bf16[16,2048]{1,0:T(8,128)(2,1)S(1)}, bf16[2048,1536]{1,0:T(8,128)(2,1)S(1)}) custom-call(s32[48]{0:T(128)} %refs_0_.5, s32[48]{0:T(128)} %refs_1_.5, bf16[5,48,2048]{2,1,0:T(8,128)(2,1)} %bitcast.31, bf16[5,48,256]{2,1,0:T(8,128)(2,1)} %bitcast.34, bf16[5,48,256]{2,1,0:T(8,128)(2,1)} %bitcast.37, bf16[48,256,256]{2,1,0:T(8,128)(2,1)} %refs_5_.5, ...), custom_call_target="tpu_custom_call" | custom-call | flops 1 | bytes 1 | tf_op jit(solution)/shard_map/pallas_call | solution.py:159
  11.2 0.1 collective-permute-start.4
  11.3 0.0 collective-permute-done
  11.3 2.1 %collective-permute-start.1 = (bf16[32,2048]{1,0:T(8,128)(2,1)S(1)}, bf16[32,2048]{1,0:T(8,128)(2,1)S(1)}, u32[]{:S(2)}, u32[]{:S(2)}) collective-permute-start(bf16[32,2048]{1,0:T(8,128)(2,1)S(1)} %get-tuple-element.31.refs_8_), channel_id=1, source_target_pairs={{0,16},{4,20},{8,24},{12,28},{16,0},{20,4},{24,8},{28,12},{1,17},{... | collective-permute-start | bytes 393224 | tf_op jit(solution)/shard_map/ppermute | solution.py:235
  13.4 4.3 %shard_map.84 = (bf16[16,2048]{1,0:T(8,128)(2,1)S(1)}, bf16[2048,1536]{1,0:T(8,128)(2,1)S(1)}) custom-call(s32[48]{0:T(128)} %refs_0_.5, s32[48]{0:T(128)} %refs_1_.5, bf16[5,48,2048]{2,1,0:T(8,128)(2,1)} %bitcast.32, bf16[5,48,256]{2,1,0:T(8,128)(2,1)} %bitcast.35, bf16[5,48,256]{2,1,0:T(8,128)(2,1)} %bitcast.38, bf16[48,256,256]{2,1,0:T(8,128)(2,1)} %refs_5_.5, ...), custom_call_target="tpu_custom_call" | custom-call | flops 1 | bytes 1 | tf_op jit(solution)/shard_map/pallas_call | solution.py:159
  17.7 0.0 collective-permute-done.4
  17.7 0.0 collective-permute-done.1
  17.8 0.1 collective-permute-start.2
  17.9 0.7 collective-permute-start.5
  18.6 0.8 %collective-permute-done.2.refs_1_ = bf16[64,2048]{1,0:T(8,128)(2,1)S(1)} collective-permute-done((bf16[64,2048]{1,0:T(8,128)(2,1)S(1)}, bf16[64,2048]{1,0:T(8,128)(2,1)S(1)}, u32[]{:S(2)}, u32[]{:S(2)}) %collective-permute-start.2) | collective-permute-done | bytes 262176 | tf_op jit(solution)/shard_map/ppermute | solution.py:235
  19.4 2.3 %shard_map.85.refs_5_ = bf16[128,4096]{1,0:T(8,128)(2,1)S(1)} custom-call(bf16[64,2048]{1,0:T(8,128)(2,1)S(1)} %constant_dynamic-update-slice_fusion.2.refs_0_, bf16[64,2048]{1,0:T(8,128)(2,1)S(1)} %collective-permute-done.2.refs_1_, bf16[2048,1024]{1,0:T(8,128)(2,1)S(1)} %get-tuple-element.23.refs_2_, bf16[2048,1536]{1,0:T(8,128)(2,1)S(1)} %get-tuple-element.24.refs_3_, ...), custom_call_target="tpu_custom_call" | custom-call | flops 1 | bytes 1 | tf_op jit(solution)/shard_map/pallas_call | solution.py:223
  21.7 0.1 shard_map.86.refs_6_
  21.8 1.3 %collective-permute-start.3 = (bf16[2,2,16,4096]{3,2,1,0:T(8,128)(2,1)S(1)}, bf16[2,2,16,4096]{3,2,1,0:T(8,128)(2,1)S(1)}, u32[]{:S(2)}, u32[]{:S(2)}) collective-permute-start(bf16[2,2,16,4096]{3,2,1,0:T(8,128)(2,1)S(1)} %shard_map.86.refs_6_), channel_id=1, source_target_pairs={{0,1},{3,2},{4,5},{7,6},{8,9},{11,10},{12,13},{15,14},{16,17},{19,... | collective-permute-start | bytes 1572872 | tf_op jit(solution)/shard_map/ppermute | solution.py:328
  23.1 0.1 shard_map.87
  23.2 0.6 collective-permute-done.5
  23.8 1.5 %collective-permute-start.9 = (bf16[16,2048]{1,0:T(8,128)(2,1)S(1)}, bf16[16,2048]{1,0:T(8,128)(2,1)S(1)}, u32[]{:S(2)}, u32[]{:S(2)}) collective-permute-start(bf16[16,2048]{1,0:T(8,128)(2,1)S(1)} %get-tuple-element.28.refs_5_), channel_id=1, source_target_pairs={{0,8},{4,12},{8,0},{12,4},{16,24},{20,28},{24,16},{28,20},{1,9},{5... | collective-permute-start | bytes 196616 | tf_op jit(solution)/shard_map/ppermute | solution.py:235
  25.3 0.1 collective-permute-start.6
  25.3 2.7 %collective-permute-done.9 = bf16[16,2048]{1,0:T(8,128)(2,1)S(1)} collective-permute-done((bf16[16,2048]{1,0:T(8,128)(2,1)S(1)}, bf16[16,2048]{1,0:T(8,128)(2,1)S(1)}, u32[]{:S(2)}, u32[]{:S(2)}) %collective-permute-start.9) | collective-permute-done | bytes 65568 | tf_op jit(solution)/shard_map/ppermute | solution.py:235
  28.0 0.7 collective-permute-start.10
  28.7 0.0 collective-permute-done.6.refs_1_
  28.7 2.4 %shard_map.88 = bf16[128,4096]{1,0:T(8,128)(2,1)S(1)} custom-call(bf16[64,2048]{1,0:T(8,128)(2,1)S(1)} %constant_dynamic-update-slice_fusion.5.refs_0_, bf16[64,2048]{1,0:T(8,128)(2,1)S(1)} %collective-permute-done.6.refs_1_, bf16[2048,1024]{1,0:T(8,128)(2,1)S(1)} %get-tuple-element.23.refs_2_, bf16[2048,1536]{1,0:T(8,128)(2,1)S(1)} %get-tuple-element.24.refs_3_, ...), custom_call_target="tpu_custom_call" | custom-call | flops 1 | bytes 1 | tf_op jit(solution)/shard_map/pallas_call | solution.py:223
  31.1 0.1 shard_map.89.refs_4_
  31.2 3.5 %collective-permute-start.8 = (bf16[2,2,16,4096]{3,2,1,0:T(8,128)(2,1)S(1)}, bf16[2,2,16,4096]{3,2,1,0:T(8,128)(2,1)S(1)}, u32[]{:S(2)}, u32[]{:S(2)}) collective-permute-start(bf16[2,2,16,4096]{3,2,1,0:T(8,128)(2,1)S(1)} %shard_map.89.refs_4_), channel_id=1, source_target_pairs={{0,1},{3,2},{4,5},{7,6},{8,9},{11,10},{12,13},{15,14},{16,17},{19,... | collective-permute-start | bytes 1572872 | tf_op jit(solution)/shard_map/ppermute | solution.py:328
  34.7 0.6 collective-permute-done.3.refs_1_.refs_3_
  35.3 0.1 shard_map.90.refs_5_
  35.5 0.0 collective-permute-done.10
  35.5 0.1 collective-permute-start.11
  35.6 0.7 collective-permute-start.7
  36.3 0.8 %collective-permute-done.11.refs_1_ = bf16[64,2048]{1,0:T(8,128)(2,1)S(1)} collective-permute-done((bf16[64,2048]{1,0:T(8,128)(2,1)S(1)}, bf16[64,2048]{1,0:T(8,128)(2,1)S(1)}, u32[]{:S(2)}, u32[]{:S(2)}) %collective-permute-start.11) | collective-permute-done | bytes 262176 | tf_op jit(solution)/shard_map/ppermute | solution.py:235
  37.1 2.4 %shard_map.91 = bf16[128,4096]{1,0:T(8,128)(2,1)S(1)} custom-call(bf16[64,2048]{1,0:T(8,128)(2,1)S(1)} %constant_dynamic-update-slice_fusion.8.refs_0_, bf16[64,2048]{1,0:T(8,128)(2,1)S(1)} %collective-permute-done.11.refs_1_, bf16[2048,1024]{1,0:T(8,128)(2,1)S(1)} %get-tuple-element.23.refs_2_, bf16[2048,1536]{1,0:T(8,128)(2,1)S(1)} %get-tuple-element.24.refs_3_, ...), custom_call_target="tpu_custom_call" | custom-call | flops 1 | bytes 1 | tf_op jit(solution)/shard_map/pallas_call | solution.py:223
  39.5 7.5 %collective-permute-start.14 = (bf16[1,2,16,4096]{3,2,1,0:T(8,128)(2,1)S(1)}, bf16[1,2,16,4096]{3,2,1,0:T(8,128)(2,1)S(1)}, u32[]{:S(2)}, u32[]{:S(2)}) collective-permute-start(bf16[1,2,16,4096]{3,2,1,0:T(8,128)(2,1)S(1)} %shard_map.92.refs_1_), channel_id=1, source_target_pairs={{0,1},{3,2},{4,5},{7,6},{8,9},{11,10},{12,13},{15,14},{16,17},{19,... | collective-permute-start | bytes 786440 | tf_op jit(solution)/shard_map/ppermute | solution.py:328
  47.1 1.3 %collective-permute-start.13 = (bf16[1,2,16,4096]{3,2,1,0:T(8,128)(2,1)S(1)}, bf16[1,2,16,4096]{3,2,1,0:T(8,128)(2,1)S(1)}, u32[]{:S(2)}, u32[]{:S(2)}) collective-permute-start(bf16[1,2,16,4096]{3,2,1,0:T(8,128)(2,1)S(1)} %shard_map.93.refs_2_), channel_id=1, source_target_pairs={{0,1},{3,2},{4,5},{7,6},{8,9},{11,10},{12,13},{15,14},{16,17},{19,... | collective-permute-start | bytes 786440 | tf_op jit(solution)/shard_map/ppermute | solution.py:328
  48.4 0.0 collective-permute-done.8.refs_1_
  48.4 0.1 shard_map.94.refs_2_
  48.5 0.7 collective-permute-start.12
  49.2 0.0 collective-permute-done.7.refs_1_
  49.2 0.1 shard_map.95.refs_2_
  49.3 6.3 %collective-permute-start.15 = (bf16[1,2,16,4096]{3,2,1,0:T(8,128)(2,1)S(1)}, bf16[1,2,16,4096]{3,2,1,0:T(8,128)(2,1)S(1)}, u32[]{:S(2)}, u32[]{:S(2)}) collective-permute-start(bf16[1,2,16,4096]{3,2,1,0:T(8,128)(2,1)S(1)} %shard_map.95.refs_2_), channel_id=1, source_target_pairs={{0,1},{2,3},{1,0},{3,2},{4,5},{6,7},{5,4},{7,6},{8,9},{10,11},{9,8... | collective-permute-start | bytes 786440 | tf_op jit(solution)/shard_map/ppermute | solution.py:328
  55.6 0.0 collective-permute-done.14.refs_1_
  55.6 0.1 shard_map.96.refs_2_
  55.7 0.7 collective-permute-start.17
  56.4 2.9 %collective-permute-done.13.refs_1_ = bf16[1,2,16,4096]{3,2,1,0:T(8,128)(2,1)S(1)} collective-permute-done((bf16[1,2,16,4096]{3,2,1,0:T(8,128)(2,1)S(1)}, bf16[1,2,16,4096]{3,2,1,0:T(8,128)(2,1)S(1)}, u32[]{:S(2)}, u32[]{:S(2)}) %collective-permute-start.13) | collective-permute-done | bytes 262176 | tf_op jit(solution)/shard_map/ppermute | solution.py:328
  59.3 0.1 shard_map.97.refs_2_
  59.3 0.7 collective-permute-start.20
  60.0 0.0 collective-permute-done.12.refs_1_
  60.0 0.1 shard_map.98.refs_2_
  60.1 5.0 %collective-permute-start.18 = (bf16[1,2,16,4096]{3,2,1,0:T(8,128)(2,1)S(1)}, bf16[1,2,16,4096]{3,2,1,0:T(8,128)(2,1)S(1)}, u32[]{:S(2)}, u32[]{:S(2)}) collective-permute-start(bf16[1,2,16,4096]{3,2,1,0:T(8,128)(2,1)S(1)} %shard_map.98.refs_2_), channel_id=1, source_target_pairs={{0,1},{2,3},{1,0},{3,2},{4,5},{6,7},{5,4},{7,6},{8,9},{10,11},{9,8... | collective-permute-start | bytes 786440 | tf_op jit(solution)/shard_map/ppermute | solution.py:328
  65.1 0.1 shard_map.99.refs_2_
  65.2 0.7 collective-permute-start.16
  65.9 0.1 shard_map.100.refs_0_.refs_2_
  66.0 0.0 collective-permute-done.15.refs_1_
  66.1 0.0 collective-permute-done.17.refs_1_
  66.1 0.1 shard_map.102.refs_2_
  66.2 2.1 %collective-permute-start.19 = (bf16[1,2,16,4096]{3,2,1,0:T(8,128)(2,1)S(1)}, bf16[1,2,16,4096]{3,2,1,0:T(8,128)(2,1)S(1)}, u32[]{:S(2)}, u32[]{:S(2)}) collective-permute-start(bf16[1,2,16,4096]{3,2,1,0:T(8,128)(2,1)S(1)} %shard_map.102.refs_2_), channel_id=1, source_target_pairs={{0,1},{2,3},{1,0},{3,2},{4,5},{6,7},{5,4},{7,6},{8,9},{10,11},{9,8... | collective-permute-start | bytes 786440 | tf_op jit(solution)/shard_map/ppermute | solution.py:328
  68.3 0.0 collective-permute-done.16.refs_1_
  68.3 0.1 shard_map.103.refs_0_.refs_2_
  68.3 4.0 %collective-permute-done.18.refs_1_ = bf16[1,2,16,4096]{3,2,1,0:T(8,128)(2,1)S(1)} collective-permute-done((bf16[1,2,16,4096]{3,2,1,0:T(8,128)(2,1)S(1)}, bf16[1,2,16,4096]{3,2,1,0:T(8,128)(2,1)S(1)}, u32[]{:S(2)}, u32[]{:S(2)}) %collective-permute-start.18) | collective-permute-done | bytes 262176 | tf_op jit(solution)/shard_map/ppermute | solution.py:328
  72.4 0.0 collective-permute-done.20.refs_4_
  72.4 3.7 %collective-permute-done.19.refs_3_ = bf16[1,2,16,4096]{3,2,1,0:T(8,128)(2,1)S(1)} collective-permute-done((bf16[1,2,16,4096]{3,2,1,0:T(8,128)(2,1)S(1)}, bf16[1,2,16,4096]{3,2,1,0:T(8,128)(2,1)S(1)}, u32[]{:S(2)}, u32[]{:S(2)}) %collective-permute-start.19) | collective-permute-done | bytes 262176 | tf_op jit(solution)/shard_map/ppermute | solution.py:328
  76.1 1.2 %shard_map.105 = f32[2,48,4096]{2,1,0:T(8,128)} custom-call(f32[2,16,4096]{2,1,0:T(8,128)S(1)} %shard_map.101.refs_2_.refs_0_, f32[2,16,4096]{2,1,0:T(8,128)S(1)} %shard_map.104.refs_1_, bf16[2,4,16,4096]{3,2,1,0:T(8,128)(2,1)S(1)} %bitcast.21, bf16[1,2,16,4096]{3,2,1,0:T(8,128)(2,1)S(1)} %collective-permute-done.19.refs_3_, ...), custom_call_target="tpu_custom_call" | custom-call | flops 1 | bytes 1 | tf_op jit(solution)/shard_map/pallas_call | solution.py:385
  (15 shorter events, 0.3 us)
Async XLA Ops:
  3.7 7.6 %collective-permute-start = (bf16[16,2048]{1,0:T(8,128)(2,1)S(1)}, bf16[16,2048]{1,0:T(8,128)(2,1)S(1)}, u32[]{:S(2)}, u32[]{:S(2)}) collective-permute-start(bf16[16,2048]{1,0:T(8,128)(2,1)S(1)} %get-tuple-element.18.refs_8_), channel_id=1, source_target_pairs={{0,8},{4,12},{8,0},{12,4},{16,24},{20,28},{24,16},{28,20},{1,9},{5... | collective-permute-start | bytes 196616 | tf_op jit(solution)/shard_map/ppermute | solution.py:235
  11.2 6.5 %collective-permute-start.4 = (bf16[16,2048]{1,0:T(8,128)(2,1)S(1)}, bf16[16,2048]{1,0:T(8,128)(2,1)S(1)}, u32[]{:S(2)}, u32[]{:S(2)}) collective-permute-start(bf16[16,2048]{1,0:T(8,128)(2,1)S(1)} %get-tuple-element.19), channel_id=1, source_target_pairs={{0,8},{4,12},{8,0},{12,4},{16,24},{20,28},{24,16},{28,20},{1,9},{5... | collective-permute-start | bytes 196616 | tf_op jit(solution)/shard_map/ppermute | solution.py:235
  11.3 6.4 %collective-permute-start.1 = (bf16[32,2048]{1,0:T(8,128)(2,1)S(1)}, bf16[32,2048]{1,0:T(8,128)(2,1)S(1)}, u32[]{:S(2)}, u32[]{:S(2)}) collective-permute-start(bf16[32,2048]{1,0:T(8,128)(2,1)S(1)} %get-tuple-element.31.refs_8_), channel_id=1, source_target_pairs={{0,16},{4,20},{8,24},{12,28},{16,0},{20,4},{24,8},{28,12},{1,17},{... | collective-permute-start | bytes 393224 | tf_op jit(solution)/shard_map/ppermute | solution.py:235
  17.8 1.6 %collective-permute-start.2 = (bf16[64,2048]{1,0:T(8,128)(2,1)S(1)}, bf16[64,2048]{1,0:T(8,128)(2,1)S(1)}, u32[]{:S(2)}, u32[]{:S(2)}) collective-permute-start(bf16[64,2048]{1,0:T(8,128)(2,1)S(1)} %constant_dynamic-update-slice_fusion.2.refs_0_), channel_id=1, source_target_pairs={{0,4},{4,0},{8,12},{12,8},{16,20},{20,16},{24,28},{28,24},{1,5},{5... | collective-permute-start | bytes 786440 | tf_op jit(solution)/shard_map/ppermute | solution.py:235
  17.9 5.9 %collective-permute-start.5 = (bf16[32,2048]{1,0:T(8,128)(2,1)S(1)}, bf16[32,2048]{1,0:T(8,128)(2,1)S(1)}, u32[]{:S(2)}, u32[]{:S(2)}) collective-permute-start(bf16[32,2048]{1,0:T(8,128)(2,1)S(1)} %pad_maximum_fusion), channel_id=1, source_target_pairs={{0,16},{4,20},{8,24},{12,28},{16,0},{20,4},{24,8},{28,12},{1,17},{... | collective-permute-start | bytes 393224 | tf_op jit(solution)/shard_map/ppermute | solution.py:235
  21.8 13.5 %collective-permute-start.3 = (bf16[2,2,16,4096]{3,2,1,0:T(8,128)(2,1)S(1)}, bf16[2,2,16,4096]{3,2,1,0:T(8,128)(2,1)S(1)}, u32[]{:S(2)}, u32[]{:S(2)}) collective-permute-start(bf16[2,2,16,4096]{3,2,1,0:T(8,128)(2,1)S(1)} %shard_map.86.refs_6_), channel_id=1, source_target_pairs={{0,1},{3,2},{4,5},{7,6},{8,9},{11,10},{12,13},{15,14},{16,17},{19,... | collective-permute-start | bytes 1572872 | tf_op jit(solution)/shard_map/ppermute | solution.py:328
  23.8 4.3 %collective-permute-start.9 = (bf16[16,2048]{1,0:T(8,128)(2,1)S(1)}, bf16[16,2048]{1,0:T(8,128)(2,1)S(1)}, u32[]{:S(2)}, u32[]{:S(2)}) collective-permute-start(bf16[16,2048]{1,0:T(8,128)(2,1)S(1)} %get-tuple-element.28.refs_5_), channel_id=1, source_target_pairs={{0,8},{4,12},{8,0},{12,4},{16,24},{20,28},{24,16},{28,20},{1,9},{5... | collective-permute-start | bytes 196616 | tf_op jit(solution)/shard_map/ppermute | solution.py:235
  25.3 3.5 %collective-permute-start.6 = (bf16[64,2048]{1,0:T(8,128)(2,1)S(1)}, bf16[64,2048]{1,0:T(8,128)(2,1)S(1)}, u32[]{:S(2)}, u32[]{:S(2)}) collective-permute-start(bf16[64,2048]{1,0:T(8,128)(2,1)S(1)} %constant_dynamic-update-slice_fusion.5.refs_0_), channel_id=1, source_target_pairs={{0,4},{4,0},{8,12},{12,8},{16,20},{20,16},{24,28},{28,24},{1,5},{5... | collective-permute-start | bytes 786440 | tf_op jit(solution)/shard_map/ppermute | solution.py:235
  28.0 7.4 %collective-permute-start.10 = (bf16[32,2048]{1,0:T(8,128)(2,1)S(1)}, bf16[32,2048]{1,0:T(8,128)(2,1)S(1)}, u32[]{:S(2)}, u32[]{:S(2)}) collective-permute-start(bf16[32,2048]{1,0:T(8,128)(2,1)S(1)} %pad_maximum_fusion.1), channel_id=1, source_target_pairs={{0,16},{4,20},{8,24},{12,28},{16,0},{20,4},{24,8},{28,12},{1,17},{... | collective-permute-start | bytes 393224 | tf_op jit(solution)/shard_map/ppermute | solution.py:235
  31.2 17.2 %collective-permute-start.8 = (bf16[2,2,16,4096]{3,2,1,0:T(8,128)(2,1)S(1)}, bf16[2,2,16,4096]{3,2,1,0:T(8,128)(2,1)S(1)}, u32[]{:S(2)}, u32[]{:S(2)}) collective-permute-start(bf16[2,2,16,4096]{3,2,1,0:T(8,128)(2,1)S(1)} %shard_map.89.refs_4_), channel_id=1, source_target_pairs={{0,1},{3,2},{4,5},{7,6},{8,9},{11,10},{12,13},{15,14},{16,17},{19,... | collective-permute-start | bytes 1572872 | tf_op jit(solution)/shard_map/ppermute | solution.py:328
  35.5 1.6 %collective-permute-start.11 = (bf16[64,2048]{1,0:T(8,128)(2,1)S(1)}, bf16[64,2048]{1,0:T(8,128)(2,1)S(1)}, u32[]{:S(2)}, u32[]{:S(2)}) collective-permute-start(bf16[64,2048]{1,0:T(8,128)(2,1)S(1)} %constant_dynamic-update-slice_fusion.8.refs_0_), channel_id=1, source_target_pairs={{0,4},{4,0},{8,12},{12,8},{16,20},{20,16},{24,28},{28,24},{1,5},{5... | collective-permute-start | bytes 786440 | tf_op jit(solution)/shard_map/ppermute | solution.py:235
  35.6 13.6 %collective-permute-start.7 = (bf16[2,2,16,4096]{3,2,1,0:T(8,128)(2,1)S(1)}, bf16[2,2,16,4096]{3,2,1,0:T(8,128)(2,1)S(1)}, u32[]{:S(2)}, u32[]{:S(2)}) collective-permute-start(bf16[2,2,16,4096]{3,2,1,0:T(8,128)(2,1)S(1)} %shard_map.90.refs_5_), channel_id=1, source_target_pairs={{1,2},{2,1},{5,6},{6,5},{9,10},{10,9},{13,14},{14,13},{17,18},{18,... | collective-permute-start | bytes 1572872 | tf_op jit(solution)/shard_map/ppermute | solution.py:328
  39.5 16.1 %collective-permute-start.14 = (bf16[1,2,16,4096]{3,2,1,0:T(8,128)(2,1)S(1)}, bf16[1,2,16,4096]{3,2,1,0:T(8,128)(2,1)S(1)}, u32[]{:S(2)}, u32[]{:S(2)}) collective-permute-start(bf16[1,2,16,4096]{3,2,1,0:T(8,128)(2,1)S(1)} %shard_map.92.refs_1_), channel_id=1, source_target_pairs={{0,1},{3,2},{4,5},{7,6},{8,9},{11,10},{12,13},{15,14},{16,17},{19,... | collective-permute-start | bytes 786440 | tf_op jit(solution)/shard_map/ppermute | solution.py:328
  47.1 12.2 %collective-permute-start.13 = (bf16[1,2,16,4096]{3,2,1,0:T(8,128)(2,1)S(1)}, bf16[1,2,16,4096]{3,2,1,0:T(8,128)(2,1)S(1)}, u32[]{:S(2)}, u32[]{:S(2)}) collective-permute-start(bf16[1,2,16,4096]{3,2,1,0:T(8,128)(2,1)S(1)} %shard_map.93.refs_2_), channel_id=1, source_target_pairs={{0,1},{3,2},{4,5},{7,6},{8,9},{11,10},{12,13},{15,14},{16,17},{19,... | collective-permute-start | bytes 786440 | tf_op jit(solution)/shard_map/ppermute | solution.py:328
  48.5 11.6 %collective-permute-start.12 = (bf16[1,2,16,4096]{3,2,1,0:T(8,128)(2,1)S(1)}, bf16[1,2,16,4096]{3,2,1,0:T(8,128)(2,1)S(1)}, u32[]{:S(2)}, u32[]{:S(2)}) collective-permute-start(bf16[1,2,16,4096]{3,2,1,0:T(8,128)(2,1)S(1)} %shard_map.94.refs_2_), channel_id=1, source_target_pairs={{1,2},{2,1},{5,6},{6,5},{9,10},{10,9},{13,14},{14,13},{17,18},{18,... | collective-permute-start | bytes 786440 | tf_op jit(solution)/shard_map/ppermute | solution.py:328
  49.3 16.7 %collective-permute-start.15 = (bf16[1,2,16,4096]{3,2,1,0:T(8,128)(2,1)S(1)}, bf16[1,2,16,4096]{3,2,1,0:T(8,128)(2,1)S(1)}, u32[]{:S(2)}, u32[]{:S(2)}) collective-permute-start(bf16[1,2,16,4096]{3,2,1,0:T(8,128)(2,1)S(1)} %shard_map.95.refs_2_), channel_id=1, source_target_pairs={{0,1},{2,3},{1,0},{3,2},{4,5},{6,7},{5,4},{7,6},{8,9},{10,11},{9,8... | collective-permute-start | bytes 786440 | tf_op jit(solution)/shard_map/ppermute | solution.py:328
  55.7 10.4 %collective-permute-start.17 = (bf16[1,2,16,4096]{3,2,1,0:T(8,128)(2,1)S(1)}, bf16[1,2,16,4096]{3,2,1,0:T(8,128)(2,1)S(1)}, u32[]{:S(2)}, u32[]{:S(2)}) collective-permute-start(bf16[1,2,16,4096]{3,2,1,0:T(8,128)(2,1)S(1)} %shard_map.96.refs_2_), channel_id=1, source_target_pairs={{1,2},{2,1},{5,6},{6,5},{9,10},{10,9},{13,14},{14,13},{17,18},{18,... | collective-permute-start | bytes 786440 | tf_op jit(solution)/shard_map/ppermute | solution.py:328
  59.3 13.1 %collective-permute-start.20 = (bf16[1,2,16,4096]{3,2,1,0:T(8,128)(2,1)S(1)}, bf16[1,2,16,4096]{3,2,1,0:T(8,128)(2,1)S(1)}, u32[]{:S(2)}, u32[]{:S(2)}) collective-permute-start(bf16[1,2,16,4096]{3,2,1,0:T(8,128)(2,1)S(1)} %shard_map.97.refs_2_), channel_id=1, source_target_pairs={{1,2},{2,1},{5,6},{6,5},{9,10},{10,9},{13,14},{14,13},{17,18},{18,... | collective-permute-start | bytes 786440 | tf_op jit(solution)/shard_map/ppermute | solution.py:328
  60.1 12.2 %collective-permute-start.18 = (bf16[1,2,16,4096]{3,2,1,0:T(8,128)(2,1)S(1)}, bf16[1,2,16,4096]{3,2,1,0:T(8,128)(2,1)S(1)}, u32[]{:S(2)}, u32[]{:S(2)}) collective-permute-start(bf16[1,2,16,4096]{3,2,1,0:T(8,128)(2,1)S(1)} %shard_map.98.refs_2_), channel_id=1, source_target_pairs={{0,1},{2,3},{1,0},{3,2},{4,5},{6,7},{5,4},{7,6},{8,9},{10,11},{9,8... | collective-permute-start | bytes 786440 | tf_op jit(solution)/shard_map/ppermute | solution.py:328
  65.2 3.1 %collective-permute-start.16 = (bf16[1,2,16,4096]{3,2,1,0:T(8,128)(2,1)S(1)}, bf16[1,2,16,4096]{3,2,1,0:T(8,128)(2,1)S(1)}, u32[]{:S(2)}, u32[]{:S(2)}) collective-permute-start(bf16[1,2,16,4096]{3,2,1,0:T(8,128)(2,1)S(1)} %shard_map.99.refs_2_), channel_id=1, source_target_pairs={{1,2},{2,1},{5,6},{6,5},{9,10},{10,9},{13,14},{14,13},{17,18},{18,... | collective-permute-start | bytes 786440 | tf_op jit(solution)/shard_map/ppermute | solution.py:328
  66.2 9.9 %collective-permute-start.19 = (bf16[1,2,16,4096]{3,2,1,0:T(8,128)(2,1)S(1)}, bf16[1,2,16,4096]{3,2,1,0:T(8,128)(2,1)S(1)}, u32[]{:S(2)}, u32[]{:S(2)}) collective-permute-start(bf16[1,2,16,4096]{3,2,1,0:T(8,128)(2,1)S(1)} %shard_map.102.refs_2_), channel_id=1, source_target_pairs={{0,1},{2,3},{1,0},{3,2},{4,5},{6,7},{5,4},{7,6},{8,9},{10,11},{9,8... | collective-permute-start | bytes 786440 | tf_op jit(solution)/shard_map/ppermute | solution.py:328
